TPU v7x, 256 devices: a whole 4x4x8 slice. The times are simulated.
256 devices in a mesh: seq: 16 (over x_lo, y, core), ctx: 16 (over x_hi, z).
Axes of the slice: x: 4 (x_hi: 2, x_lo: 2; x = x_hi * 2 + x_lo), y: 4, z: 8, core: 2. Of those that a mesh axis runs over, the one named last changes fastest.
Arguments:
- order: int32 [16, 32], P('seq'), may hold values from 0 to 31, each once within a row
- queries: bfloat16 [16, 4096, 5, 128], P('seq', 'ctx'), may hold values from -11 to 11
- keys: bfloat16 [16, 4096, 128], P('seq', 'ctx'), may hold values from -6 to 6
- w_query_gate: float32 [5, 128, 128], replicated, may hold values from -12.5 to 12.5
- w_key_gate: float32 [384, 128], replicated, may hold values from -0.3125 to 0.3125
Outputs:
- target: float32 [16, 16, 5, 4, 64], P('seq', 'ctx')
- grad_query_gate: float32 [5, 128, 128], replicated
- grad_key_gate: float32 [384, 128], replicated
- loss: float32 [16], P('seq')
Inputs may be any that keep to these rules, and one draw needn't show every extreme that they name: Each row names every half-block of 128 tokens of its sequence once; device c of ctx holds the half-blocks named at entries 2 c and 2 c + 1, in that order.
All inputs are finite; a program needn't handle non-finite values.
Results may differ from a plain program's by a relative error of at most 0.0003.
Values may be sent and summed in bfloat16 or wider, within the bound.
No kernel may reach another device: no remote copies, remote signals or barrier semaphores. Data moves between devices by JAX's collectives and lax.ppermute only.
A program may use at most 192 MiB of HBM per device.

v0:
```python
import jax
import jax.numpy as jnp
from jax import lax
from jax.sharding import PartitionSpec as P

POOL = 64


masked_low = -1e30


def on_device(order, queries, keys, w_query_gate, w_key_gate):
    highest = lax.Precision.HIGHEST
    tok_rows = queries.shape[1]
    head_count = queries.shape[2]
    head_width = queries.shape[3]
    half_len = tok_rows // 2
    per_half = half_len // POOL
    local_blocks = tok_rows // POOL
    ctx_count = lax.axis_size("ctx")
    block_total = tok_rows * ctx_count // POOL
    order_row = order[0]
    ctx_place = lax.axis_index("ctx")
    local_rows = jnp.arange(tok_rows, dtype=jnp.int32) + ctx_place * tok_rows
    query_pos = jnp.take(order_row, local_rows // half_len) * half_len + local_rows % half_len
    row_pos = jnp.repeat(query_pos, head_count)
    q_flat = queries[0].reshape(tok_rows * head_count, head_width)
    key_rows = keys[0]
    score_scale = head_width ** (-0.5)

    def piece_scores(piece):
        count = piece.shape[0]
        rows = jnp.arange(count, dtype=jnp.int32)
        key_pos = jnp.take(order_row, rows // half_len) * half_len + rows % half_len
        scores = (
            lax.dot_general(
                q_flat, piece, (((1,), (1,)), ((), ())), preferred_element_type=jnp.float32
            )
            * score_scale
        )
        allowed = key_pos[None, :] <= row_pos[:, None]
        return (scores, allowed)

    start_top = jnp.full((tok_rows * head_count,), masked_low, jnp.float32)
    scores, allowed = piece_scores(lax.all_gather(key_rows, "ctx", axis=0, tiled=True))
    new_top = jnp.maximum(start_top, jnp.max(jnp.where(allowed, scores, masked_low), axis=1))
    row_total = jnp.sum(jnp.where(allowed, jnp.exp(scores - new_top[:, None]), 0.0), axis=1)
    row_top, row_total = (new_top, row_total)
    lse = row_top + jnp.log(row_total)
    piece = lax.all_gather(key_rows, "ctx", axis=0, tiled=True)
    scores, allowed = piece_scores(piece)
    count = piece.shape[0]
    probs = jnp.where(allowed, jnp.exp(scores - lse[:, None]), 0.0)
    block_part = probs.reshape(local_blocks, POOL, head_count, count // POOL, POOL).max(axis=(1, 4))
    maps = block_part
    maps = jnp.transpose(maps, (1, 0, 2))
    target = maps / jnp.sum(maps, axis=-1, keepdims=True)
    all_blocks = jnp.arange(block_total, dtype=jnp.int32)
    block_pos = jnp.take(order_row, all_blocks // per_half) * per_half + all_blocks % per_half
    own_blocks = jnp.arange(local_blocks, dtype=jnp.int32) + ctx_place * local_blocks
    query_block_pos = jnp.take(order_row, own_blocks // per_half) * per_half + own_blocks % per_half
    pooled_q = (
        queries[0]
        .astype(jnp.float32)
        .reshape(local_blocks, POOL, head_count, head_width)
        .mean(axis=1)
    )
    key_blocks = key_rows.reshape(local_blocks, POOL, head_width)
    pooled_k = jnp.concatenate(
        [
            key_blocks.max(axis=1).astype(jnp.float32),
            key_blocks.min(axis=1).astype(jnp.float32),
            key_blocks.astype(jnp.float32).mean(axis=1),
        ],
        axis=1,
    )
    pooled_all = lax.all_gather(pooled_k, "ctx", axis=0, tiled=True)
    gate_k = jnp.dot(pooled_all, w_key_gate, precision=highest)
    gate_q = jnp.einsum("qhd,hdg->hqg", pooled_q, w_query_gate, precision=highest)
    gate_width = w_key_gate.shape[1]
    logits = jnp.einsum("hqg,kg->hqk", gate_q, gate_k, precision=highest) * gate_width ** (-0.5)
    visible = (block_pos[None, :] <= query_block_pos[:, None])[None]
    peak = jnp.max(jnp.where(visible, logits, masked_low), axis=-1, keepdims=True)
    weights = jnp.where(visible, jnp.exp(logits - peak), 0.0)
    norm_sum = jnp.sum(weights, axis=-1, keepdims=True)
    log_gate = logits - peak - jnp.log(norm_sum)
    gate = weights / norm_sum
    count = head_count * block_total
    loss_part = -jnp.sum(jnp.where(visible, target * log_gate, 0.0)) / count
    d_logits = jnp.where(visible, gate - target, 0.0) / count * gate_width ** (-0.5)
    d_gate_q = jnp.einsum("hqk,kg->hqg", d_logits, gate_k, precision=highest)
    d_gate_k = jnp.einsum("hqk,hqg->kg", d_logits, gate_q, precision=highest)
    grad_q = jnp.einsum("qhd,hqg->hdg", pooled_q, d_gate_q, precision=highest)
    grad_k = lax.dot_general(pooled_all, d_gate_k, (((0,), (0,)), ((), ())), precision=highest)
    loss_value = lax.psum(loss_part, "ctx")
    grad_q, grad_k = lax.psum((grad_q, grad_k), ("seq", "ctx"))
    loss_out = jnp.reshape(loss_value, (1,))
    return (target[None, None], grad_q, grad_k, loss_out)


def solution(mesh):
    placed = (P("seq", None), P("seq", "ctx", None, None), P("seq", "ctx", None), P(), P())
    return jax.shard_map(
        on_device,
        mesh=mesh,
        in_specs=placed,
        out_specs=(P("seq", "ctx", None, None, None), P(), P(), P("seq")),
        check_vma=False,
    )
```

profile of v0, /device:TPU:1, one launch (start us, length us, event | category | flops | bytes accessed | tf_op | source)
XLA Modules:
  0.0 439.9 jit_solution(14651127707139151364)
XLA Ops:
  7.2 0.0 copy-start
  7.2 0.0 all-gather.4.cloned.1.call-start
  7.2 0.7 all-gather.4.cloned.1.call-update
  7.9 0.0 all-reduce.3.cloned.1.call-start
  8.4 2.1 fusion.87
  10.5 1.8 fusion.88
  12.3 0.9 fusion.86
  13.2 0.9 convert_reduce_fusion.1
  14.1 4.5 %compare_select_fusion.5 = s32[256,1]{0,1:T(1,128)S(1)} fusion(s32[]{:T(128)} %bitcast.58, s32[]{:T(128)} %bitcast.59, s32[]{:T(128)} %bitcast.60, s32[]{:T(128)} %bitcast.61, s32[]{:T(128)} %bitcast.62, s32[]{:T(128)} %bitcast.64, s32[]{:T(128)} %bitcast.63, s32[]{:T(128)S(6)} %mul.45), kind=kLoop, calls=%fused_computation.123 | loop fusion | flops 7936 | bytes 1056 | tf_op jit(solution)/shard_map/jit(_take)/gather | solution.py:25
  18.6 15.6 %fusion.72 = s32[256]{0:T(256)S(1)} fusion(pred[256]{0:T(512)(128)(4,1)S(1)} %get-tuple-element.91, pred[256]{0:T(512)(128)(4,1)S(1)} %get-tuple-element.92, pred[256]{0:T(512)(128)(4,1)S(1)} %get-tuple-element.93, pred[256]{0:T(512)(128)(4,1)S(1)} %get-tuple-element.94, pred[256]{0:T(512)(128)(4,1)S(1)} %get-tuple-element.95, ...), kind=kLoop, calls=%fused_computation.159 | loop fusion | flops 13824 | bytes 8552 | tf_op jit(solution)/shard_map/add | solution.py:25
  34.3 38.1 %all-gather.1 = f32[16,4,384]{2,1,0:T(4,128)S(1)} all-gather(f32[1,4,384]{2,1,0:T(4,128)S(1)} %maximum_bitcast_fusion), channel_id=1, replica_groups=mesh['seq'=16,'ctx'=16] {'ctx'}, dimensions={0}, use_global_device_ids=true | all-gather | bytes 104448 | tf_op jit(solution)/shard_map/all_gather | solution.py:77
  72.4 0.1 broadcast_in_dim.74
  72.5 0.2 le.86
  72.7 1.2 copy.14
  73.9 0.1 reshape_squeeze.6
  74.1 1.3 gather_fusion.1
  75.4 1.4 gather_fusion
  76.9 1.2 convolution_bitcast_fusion.1
  78.0 1.0 convert_reduce_fusion
  79.1 0.1 broadcast_compare_fusion
  79.2 0.0 copy-done
  79.2 0.4 fusion.63
  79.6 0.2 convolution_multiply_fusion.1
  79.8 0.7 fusion.58
  80.5 1.9 fusion.90
  82.3 2.1 fusion.89
  84.4 20.1 %fusion.21 = s32[4096]{0:T(1024)S(1)} fusion(s32[]{:T(128)} %bitcast.32, s32[]{:T(128)} %bitcast.31, s32[]{:T(128)} %bitcast.30, s32[]{:T(128)} %bitcast.29, s32[]{:T(128)} %bitcast.28, s32[]{:T(128)} %bitcast.27, s32[]{:T(128)} %bitcast.26, s32[]{:T(128)} %bitcast.25, s32[]{:T(128)} %bitcast.24, s32[]{:T(128)} %bitcast.23, s32[]{:T(128)} %bitcast.22, ...), kind=kLoop, calls=%fused_computation.38 | loop fusion | flops 339968 | bytes 16512 | tf_op jit(solution)/shard_map/add | solution.py:34
  104.5 0.0 all-gather.4.cloned.1.call-done
  104.5 5.0 %fusion.3 = (f32[1280]{0:T(1024)S(1)}, f32[1280,4096]{1,0:T(8,128)S(1)}) fusion(s32[4096]{0:T(1024)S(1)} %fusion.21, s32[1280]{0:T(1024)S(1)} %le.86, bf16[1280,128]{1,0:T(8,128)(2,1)S(1)} %reshape_squeeze.6, bf16[1,4096,128]{2,1,0:T(8,128)(2,1)} %all-gather.4.cloned.1.call-done), kind=kOutput, calls=%fused_computation.8 | convolution fusion | flops 1363147520 | bytes 22374400 | tf_op jit(solution)/shard_map/dot_general | solution.py:36
  109.6 5.5 %fusion.4 = f32[1280]{0:T(1024)S(1)} fusion(f32[1280,4096]{1,0:T(8,128)S(1)} %get-tuple-element.86, f32[1280]{0:T(1024)S(1)} %broadcast_maximum_fusion, s32[4096]{0:T(1024)S(1)} %fusion.21, s32[1280]{0:T(1024)S(1)} %le.86), kind=kLoop, calls=%fused_computation.9 | loop fusion | flops 20970240 | bytes 21003264 | tf_op jit(solution)/shard_map/reduce_sum | solution.py:47
  115.0 8.6 %compare_select_fusion = f32[1280,4096]{1,0:T(8,128)} fusion(f32[1280,4096]{1,0:T(8,128)S(1)} %get-tuple-element.86, f32[1280]{0:T(1024)S(1)} %log_add_fusion, s32[4096]{0:T(1024)S(1)} %fusion.21, s32[1280]{0:T(1024)S(1)} %le.86), kind=kLoop, calls=%fused_computation.5 | loop fusion | flops 15728640 | bytes 41969664 | tf_op jit(solution)/shard_map/jit(_where)/select_n | solution.py:53
  123.6 0.0 copy-start.1
  123.6 33.5 %reshape.300 = f32[4,64,5,64,64]{4,3,2,1,0:T(8,128)} reshape(f32[1280,4096]{1,0:T(8,128)} %compare_select_fusion) | data formatting | bytes 41943040 | tf_op jit(solution)/shard_map/reshape | solution.py:54
  157.1 15.3 %reduce_max.37 = f32[4,5,64]{2,1,0:T(8,128)S(1)} reduce(f32[4,64,5,64,64]{4,3,2,1,0:T(8,128)} %reshape.300, f32[]{:T(128)} %constant.176.clone.1), dimensions={1,4}, to_apply=%region_2.4 | reduce | flops 5241600 | bytes 20976644 | tf_op jit(solution)/shard_map/reduce_max | solution.py:54
  172.4 1.0 select_reduce_fusion.1
  173.4 0.2 fusion.9
  173.5 0.2 convolution_bitcast_fusion
  173.8 0.2 fusion.59
  174.0 1.2 fusion.91
  175.1 1.4 fusion.61
  176.6 0.0 all-reduce.3.cloned.1.call-update
  177.2 30.8 %psum.23 = f32[1]{0:T(128)} all-reduce(f32[1]{0:T(128)} %bitcast.76), channel_id=1, replica_groups=mesh['seq'=16,'ctx'=16] {'ctx'}, use_global_device_ids=true, to_apply=%region_13.15 | all-reduce | flops 1 | bytes 8 | tf_op jit(solution)/shard_map/psum | solution.py:95
  208.1 0.6 copy.18
  208.7 221.1 %all-reduce.3.cloned.1.call-done = (f32[5,128,128]{2,1,0:T(8,128)}, f32[384,128]{1,0:T(8,128)}) async-done(((f32[5,128,128]{2,1,0:T(8,128)}, f32[384,128]{1,0:T(8,128)}), (f32[5,128,128]{2,1,0:T(8,128)}, f32[384,128]{1,0:T(8,128)})) %all-reduce.3.cloned.1.call-update) | async-done | bytes 524304 | tf_op jit(solution)/shard_map/psum | solution.py:96
  429.8 1.7 copy.27
  431.5 1.6 copy.28
  433.1 0.0 copy-done.1
  (27 shorter events, 0.6 us)
Async XLA Ops:
  7.2 72.0 %copy-start = (f32[5,128,128]{2,1,0:T(8,128)S(1)}, f32[5,128,128]{2,1,0:T(8,128)}, u32[]{:S(2)}) copy-start(f32[5,128,128]{2,1,0:T(8,128)} %param.10) | copy-start | bytes 983044
  7.2 97.3 %all-gather.4.cloned.1.call-start = ((), (), s32[]{:S(2)}) async-start(), calls=%async_computation | async-start | bytes 1114112 | tf_op jit(solution)/shard_map/all_gather | solution.py:50
  7.9 421.8 %all-reduce.3.cloned.1.call-start = ((), (), s32[]{:S(2)}) async-start(), calls=%async_computation.1 | async-start | bytes 1048576 | tf_op jit(solution)/shard_map/psum | solution.py:96
  123.6 309.5 %copy-start.1 = (f32[5,128,128]{2,1,0:T(8,128)S(1)}, f32[5,128,128]{2,1,0:T(8,128)}, u32[]{:S(2)}) copy-start(f32[5,128,128]{2,1,0:T(8,128)} %param.10) | copy-start | bytes 983044
Sparse Core Ops, SparseCore 0:
  10.6 78.8 all-gather.3
  176.7 252.9 all-reduce.2
where the time goes:
time: 443 us; the launch traced here: 440 us
  waiting for transfers between devices  222 us (50%)
  other arithmetic  74.7 us (17%)
  blocking collectives  69 us (16%)
  local copies, waits for them, and re-layouts  49.6 us (11%)
  between operations  14.9 us (3%)
  matrix products  9.81 us (2%)
    psum x1, waiting for transfers between devices, on_device(): grad_q, grad_k = lax.psum((grad_q, grad_k), ('seq', 'ctx'))  221 us
    all_gather x1, blocking collectives, on_device(): pooled_all = lax.all_gather(pooled_k, 'ctx', axis=0, tiled=True)  38.1 us
    reshape x1, local copies, waits for them, and re-layouts, on_device(): probs.reshape(local_blocks, POOL, head_count, count // POOL, POOL)  33.5 us
    psum x1, blocking collectives, on_device(): loss_value = lax.psum(loss_part, 'ctx')  30.8 us
    add x1, other arithmetic, piece_scores(): key_pos = jnp.take(order_row, rows // half_len) * half_len + rows % half_len  20.1 us
    add x1, other arithmetic, on_device(): jnp.take(order_row, local_rows // half_len) * half_len  15.6 us
    reduce_max x1, other arithmetic, on_device(): probs.reshape(local_blocks, POOL, head_count, count // POOL, POOL)  15.3 us
  transfers between devices with their start and end apart: 2, of which 1 were waited for; matrix products, arithmetic and copies ran while one was open for 13% of the time, Pallas kernels for 0%

commit v1 on v0

v1 whole, which is shorter than its diff:
```python
import functools
import math

import jax
import jax.numpy as jnp
from jax import lax
from jax.experimental import pallas as pl
from jax.experimental.pallas import tpu as pltpu
from jax.sharding import PartitionSpec as P

POOL = 64
LOW = -1e30
HIGHEST = lax.Precision.HIGHEST
VMEM = pl.BlockSpec(memory_space=pltpu.VMEM)
SMEM = pl.BlockSpec(memory_space=pltpu.SMEM)
PARAMS = pltpu.CompilerParams(vmem_limit_bytes=40 * 1024 * 1024)
CHUNK = 512
SUB = 8


def dot_nt(a, b, precision=None):
    return lax.dot_general(
        a, b, (((1,), (1,)), ((), ())), precision=precision, preferred_element_type=jnp.float32
    )


def dot_tn(a, b, precision=None):
    return lax.dot_general(
        a, b, (((0,), (0,)), ((), ())), precision=precision, preferred_element_type=jnp.float32
    )


def dot_nn(a, b, precision=None):
    return lax.dot_general(
        a, b, (((1,), (0,)), ((), ())), precision=precision, preferred_element_type=jnp.float32
    )


def local_kernel(scale, q_ref, k_ref, wq_ref, diag_ref, top_ref, tot_ref, pooled_ref, gate_q_ref):
    heads, rows, width = q_ref.shape
    half = rows // 2
    blocks = rows // POOL
    diag_ref[...] = jnp.full(diag_ref.shape, LOW, jnp.float32)
    key_row = lax.broadcasted_iota(jnp.int32, (half, half), 0)
    query_lane = lax.broadcasted_iota(jnp.int32, (half, half), 1)
    causal = key_row <= query_lane
    blank = jnp.zeros((SUB - blocks, width), jnp.float32)
    for h in range(heads):
        q = q_ref[h]
        pooled = jnp.sum(q.astype(jnp.float32).reshape(blocks, POOL, width), axis=1) * (1.0 / POOL)
        pooled_ref[h * SUB : (h + 1) * SUB, :] = jnp.concatenate([blank, pooled], axis=0)
        gate_q_ref[h * SUB : (h + 1) * SUB, :] = dot_nn(
            jnp.concatenate([pooled, blank], axis=0), wq_ref[h], HIGHEST
        )
        for part in range(2):
            s = dot_nt(k_ref[part * half : (part + 1) * half, :], q[part * half : (part + 1) * half, :])
            s = jnp.where(causal, s * scale, LOW)
            per = half // POOL
            block_top = jnp.max(s.reshape(per, POOL, half), axis=1)
            top = jnp.max(block_top, axis=0, keepdims=True)
            p = jnp.exp2(s - top)
            lanes = slice(h * rows + part * half, h * rows + (part + 1) * half)
            diag_ref[part * per : (part + 1) * per, lanes] = block_top
            top_ref[:, lanes] = top
            tot_ref[:, lanes] = jnp.sum(p.reshape(half // SUB, SUB, half), axis=0)


def attend(scale, base, order_ref, own_ref, q_ref, k_ref, top_ref, tot_ref, map_ref, map_row, pool_ref, pool_row):
    heads, rows, width = q_ref.shape
    half = rows // 2
    kb_chunk = CHUNK // POOL
    halves_chunk = CHUNK // half
    kb_row = lax.broadcasted_iota(jnp.int32, (kb_chunk, rows), 0)
    lane = lax.broadcasted_iota(jnp.int32, (kb_chunk, rows), 1)
    query_half = jnp.where(lane < half, own_ref[1], own_ref[2])

    def step(i, carry):
        start = pl.multiple_of(i * CHUNK, CHUNK)
        keys = k_ref[pl.ds(start, CHUNK), :]
        key_half = jnp.full((kb_chunk, rows), order_ref[0, base + i * halves_chunk], jnp.int32)
        for j in range(1, halves_chunk):
            key_half = jnp.where(
                kb_row >= j * (half // POOL), order_ref[0, base + i * halves_chunk + j], key_half
            )
        seen = jnp.where(key_half < query_half, 1.0, 0.0)
        seen_rows = jnp.broadcast_to(seen[:, None, :], (kb_chunk, SUB, rows)) > 0.5
        seen = seen > 0.5
        blocks = keys.astype(jnp.float32).reshape(kb_chunk, POOL, width)
        pool_at = pl.ds(pl.multiple_of(pool_row + i * kb_chunk, kb_chunk), kb_chunk)
        pool_ref[pool_at, 0:width] = jnp.max(blocks, axis=1)
        pool_ref[pool_at, width : 2 * width] = jnp.min(blocks, axis=1)
        pool_ref[pool_at, 2 * width : 3 * width] = jnp.sum(blocks, axis=1) * (1.0 / POOL)
        map_at = pl.ds(pl.multiple_of(map_row + i * kb_chunk, kb_chunk), kb_chunk)
        for h in range(heads):
            lanes = slice(h * rows, (h + 1) * rows)
            s = dot_nt(keys, q_ref[h]) * scale
            s = s.reshape(kb_chunk, POOL // SUB, SUB, rows)
            block_top = jnp.max(jnp.max(s, axis=1), axis=1)
            block_top = jnp.where(seen, block_top, LOW)
            map_ref[map_at, lanes] = block_top
            top = top_ref[:, lanes]
            new_top = jnp.maximum(top, jnp.max(block_top, axis=0, keepdims=True))
            part = jnp.sum(jnp.exp2(s - new_top.reshape(1, 1, 1, rows)), axis=1)
            part = jnp.sum(jnp.where(seen_rows, part, 0.0), axis=0)
            tot_ref[:, lanes] = tot_ref[:, lanes] * jnp.exp2(top - new_top) + part
            top_ref[:, lanes] = new_top
        return carry

    lax.fori_loop(0, k_ref.shape[0] // CHUNK, step, 0)


def near_kernel(
    scale, order_ref, own_ref, q_ref, k_ref, top_in, tot_in, map_ref, top_ref, tot_ref, pool_ref
):
    top_ref[...] = top_in[...]
    tot_ref[...] = tot_in[...]
    attend(
        scale, own_ref[3], order_ref, own_ref, q_ref, k_ref, top_ref, tot_ref, map_ref, 0, pool_ref, 0
    )


def far_kernel(
    scale,
    order_ref,
    own_ref,
    q_ref,
    k_ref,
    top_in,
    tot_in,
    near_map,
    near_pool,
    diag_ref,
    pooled_ref,
    gate_q_ref,
    wk_ref,
    kb_pos_ref,
    target_ref,
    send_ref,
    pool_ref,
    gate_k_ref,
    map_ref,
    top_ref,
    tot_ref,
    block_ref,
):
    heads, rows, width = q_ref.shape
    half = rows // 2
    blocks = rows // POOL
    near_rows = near_map.shape[0]
    total = 2 * near_rows
    per = half // POOL
    top_ref[...] = top_in[...]
    tot_ref[...] = tot_in[...]
    near_at = pl.multiple_of(own_ref[3] * per, near_rows)
    far_at = pl.multiple_of(own_ref[4] * per, near_rows)
    map_ref[pl.ds(near_at, near_rows), :] = near_map[...]
    pool_ref[pl.ds(near_at, near_rows), :] = near_pool[...]
    attend(
        scale, own_ref[4], order_ref, own_ref, q_ref, k_ref, top_ref, tot_ref, map_ref, far_at, pool_ref, far_at
    )
    block_ref[...] = jnp.ones(block_ref.shape, jnp.float32)
    kb_index = lax.broadcasted_iota(jnp.int32, (total, half), 0)
    own_block = own_ref[0] * blocks
    for h in range(heads):
        for part in range(2):
            lanes = slice(h * rows + part * half, h * rows + (part + 1) * half)
            m = map_ref[:, lanes]
            for j in range(part * per, (part + 1) * per):
                m = jnp.where(kb_index == own_block + j, diag_ref[j : j + 1, lanes], m)
            lse = top_ref[:, lanes] + jnp.log2(jnp.sum(tot_ref[:, lanes], axis=0, keepdims=True))
            b = jnp.exp2(m - lse).T.reshape(per, POOL, total)
            block_ref[h * SUB + part * per : h * SUB + (part + 1) * per, :] = jnp.max(b, axis=1)
    block_map = block_ref[...]
    target = block_map / jnp.sum(block_map, axis=1, keepdims=True)
    for h in range(heads):
        target_ref[h] = target[h * SUB : h * SUB + blocks, :]
    gate_k = dot_nn(pool_ref[...], wk_ref[...], HIGHEST)
    gate_k_ref[...] = gate_k
    gate_width = gate_k.shape[1]
    row = lax.broadcasted_iota(jnp.int32, (heads * SUB, total), 0) % SUB
    query_pos = jnp.where(row < per, own_ref[1], own_ref[2]) * per + row % per
    visible = (kb_pos_ref[...] <= query_pos) & (row < blocks)
    logits = dot_nt(gate_q_ref[...], gate_k, HIGHEST) * gate_width ** (-0.5)
    peak = jnp.max(jnp.where(visible, logits, LOW), axis=1, keepdims=True)
    weights = jnp.where(visible, jnp.exp(logits - peak), 0.0)
    norm_sum = jnp.where(row[:, :1] < blocks, jnp.sum(weights, axis=1, keepdims=True), 1.0)
    log_gate = logits - peak - jnp.log(norm_sum)
    count = heads * total
    loss = -jnp.sum(jnp.where(visible, target * log_gate, 0.0)) / count
    d_logits = jnp.where(visible, weights / norm_sum - target, 0.0) / count * gate_width ** (-0.5)
    msg = jnp.concatenate([d_logits, jnp.zeros((heads * SUB, width - total), jnp.float32)], axis=1)
    msg_row = lax.broadcasted_iota(jnp.int32, msg.shape, 0)
    msg_lane = lax.broadcasted_iota(jnp.int32, msg.shape, 1)
    msg = jnp.where((msg_row == 0) & (msg_lane == total), loss, msg + pooled_ref[...])
    send_ref[...] = jnp.broadcast_to(msg[None], send_ref.shape)


def grad_kernel(got_ref, pool_ref, gate_k_ref, wq_ref, grad_ref, loss_ref):
    peers, msg_rows, width = got_ref.shape
    heads = wq_ref.shape[0]
    total = gate_k_ref.shape[0]
    gate_k = gate_k_ref[...]
    gate_k_grad = jnp.zeros(gate_k.shape, jnp.float32)
    row = lax.broadcasted_iota(jnp.int32, (peers * SUB, width), 0) % SUB
    for h in range(heads):
        both = got_ref[:, h * SUB : (h + 1) * SUB, :].reshape(peers * SUB, width)
        d_logits = jnp.where(row < SUB // 2, both, 0.0)[:, :total]
        pooled = pltpu.roll(both, peers * SUB - SUB // 2, 0)
        mixed = dot_tn(d_logits, pooled, HIGHEST)
        grad_ref[h * width : (h + 1) * width, :] = dot_tn(mixed, gate_k, HIGHEST)
        gate_k_grad = gate_k_grad + dot_nn(mixed, wq_ref[h], HIGHEST)
    grad_ref[heads * width :, :] = dot_tn(pool_ref[...], gate_k_grad, HIGHEST)
    first = got_ref[:, 0, :]
    lane = lax.broadcasted_iota(jnp.int32, first.shape, 1)
    loss_ref[...] = jnp.sum(
        jnp.sum(jnp.where(lane == total, first, 0.0), axis=0, keepdims=True), axis=1, keepdims=True
    )


def on_device(order, queries, keys, w_query_gate, w_key_gate):
    tok_rows = queries.shape[1]
    heads = queries.shape[2]
    width = queries.shape[3]
    per_half = tok_rows // 2 // POOL
    blocks = tok_rows // POOL
    ctx_count = lax.axis_size("ctx")
    seq_count = lax.axis_size("seq")
    near = ctx_count // 2
    total = ctx_count * blocks
    scale = width ** (-0.5) * math.log2(math.e)
    f32 = jnp.float32
    columns = heads * tok_rows

    place = lax.axis_index("ctx")
    group = place // near
    own_halves = lax.dynamic_slice(order, (0, place * 2), (1, 2))[0]
    own = jnp.concatenate(
        [place[None], own_halves, (group * near * 2)[None], ((1 - group) * near * 2)[None]]
    ).astype(jnp.int32)
    kb_pos = (order.reshape(-1, 1) * per_half + jnp.arange(per_half, dtype=jnp.int32)[None]).reshape(1, total)

    groups = [list(range(near)), list(range(near, 2 * near))]
    spread = jnp.broadcast_to(keys, (near,) + keys.shape[1:])
    near_keys = lax.all_to_all(spread, "ctx", 0, 0, axis_index_groups=groups, tiled=True)
    far_keys = lax.ppermute(near_keys, "ctx", [(j, (j + near) % ctx_count) for j in range(ctx_count)])
    near_keys = near_keys.reshape(near * tok_rows, width)
    far_keys = far_keys.reshape(near * tok_rows, width)

    q = jnp.transpose(queries[0], (1, 0, 2))
    diag, top, tot, pooled, gate_q = pl.pallas_call(
        functools.partial(local_kernel, scale),
        out_shape=(
            jax.ShapeDtypeStruct((SUB, columns), f32),
            jax.ShapeDtypeStruct((1, columns), f32),
            jax.ShapeDtypeStruct((SUB, columns), f32),
            jax.ShapeDtypeStruct((heads * SUB, width), f32),
            jax.ShapeDtypeStruct((heads * SUB, width), f32),
        ),
        in_specs=[VMEM] * 3,
        out_specs=(VMEM,) * 5,
        compiler_params=PARAMS,
        name="local",
    )(q, keys[0], w_query_gate)

    flops = 2 * near * tok_rows * columns * width
    near_map, top, tot, near_pool = pl.pallas_call(
        functools.partial(near_kernel, scale),
        out_shape=(
            jax.ShapeDtypeStruct((total // 2, columns), f32),
            jax.ShapeDtypeStruct((1, columns), f32),
            jax.ShapeDtypeStruct((SUB, columns), f32),
            jax.ShapeDtypeStruct((total // 2, 3 * width), f32),
        ),
        in_specs=[SMEM, SMEM] + [VMEM] * 4,
        out_specs=(VMEM,) * 4,
        compiler_params=PARAMS,
        cost_estimate=pl.CostEstimate(
            flops=4 * flops, bytes_accessed=2 * 1024 * 1024, transcendentals=near * tok_rows * columns
        ),
        name="near",
    )(order, own, q, near_keys, top, tot)

    target, send, pool, gate_k = pl.pallas_call(
        functools.partial(far_kernel, scale),
        out_shape=(
            jax.ShapeDtypeStruct((heads, blocks, total), f32),
            jax.ShapeDtypeStruct((ctx_count, heads * SUB, width), f32),
            jax.ShapeDtypeStruct((total, 3 * width), f32),
            jax.ShapeDtypeStruct((total, w_key_gate.shape[1]), f32),
        ),
        in_specs=[SMEM, SMEM] + [VMEM] * 11,
        out_specs=(VMEM,) * 4,
        scratch_shapes=[
            pltpu.VMEM((total, columns), f32),
            pltpu.VMEM((1, columns), f32),
            pltpu.VMEM((SUB, columns), f32),
            pltpu.VMEM((heads * SUB, total), f32),
        ],
        compiler_params=PARAMS,
        name="far",
    )(order, own, q, far_keys, top, tot, near_map, near_pool, diag, pooled, gate_q, w_key_gate, kb_pos)

    got = lax.all_to_all(send, "ctx", 0, 0, tiled=True)
    grads, loss = pl.pallas_call(
        grad_kernel,
        out_shape=(
            jax.ShapeDtypeStruct((heads * width + 3 * width, w_key_gate.shape[1]), f32),
            jax.ShapeDtypeStruct((1, 1), f32),
        ),
        in_specs=[VMEM] * 4,
        out_specs=(VMEM, VMEM),
        compiler_params=PARAMS,
        name="grad",
    )(got, pool, gate_k, w_query_gate)

    tiles = grads.reshape(seq_count, -1, grads.shape[1])
    own_tile = jnp.sum(lax.all_to_all(tiles, "seq", 0, 0, tiled=True), axis=0)
    spread = jnp.broadcast_to(own_tile[None], tiles.shape)
    grads = lax.all_to_all(spread, "seq", 0, 0, tiled=True).reshape(grads.shape)
    grad_q = grads[: heads * width].reshape(heads, width, -1)
    grad_k = grads[heads * width :]
    return (target[None, None], grad_q, grad_k, loss.reshape(1))


def solution(mesh):
    placed = (P("seq", None), P("seq", "ctx", None, None), P("seq", "ctx", None), P(), P())
    return jax.shard_map(
        on_device,
        mesh=mesh,
        in_specs=placed,
        out_specs=(P("seq", "ctx", None, None, None), P(), P(), P("seq")),
        check_vma=False,
    )
```

time: 443 us -> 99.2 us (0.22)
  waiting for transfers between devices: 222 us -> 24.5 us
  other arithmetic: 74.7 us -> 0.19 us
  local copies, waits for them, and re-layouts: 49.6 us -> 3.39 us
  blocking collectives: 69 us -> 45.2 us
  between operations: 14.9 us -> 0.7 us
  Pallas kernels: 0 us -> 13.1 us
  starting transfers between devices: 0.08 us -> 11.9 us
  matrix products: 9.81 us -> 0 us
    psum x1 -> x0, waiting for transfers between devices: 221 us -> none  [on_device(): grad_q, grad_k = lax.psum((grad_q, grad_k), ('seq', 'ctx'))]
    all_to_all x0 -> x3, blocking collectives: none -> 45.2 us  [the longest x1 17.3 us: on_device(): own_tile = jnp.sum(lax.all_to_all(tiles, 'seq', 0, 0, tiled=True), axis=0)]
    all_gather x1 -> x0, blocking collectives: 38.1 us -> none  [on_device(): pooled_all = lax.all_gather(pooled_k, 'ctx', axis=0, tiled=True)]
    add x5 -> x1, other arithmetic: 35.8 us -> 0.07 us  [on_device(): order.reshape(-1, 1) * per_half]
    reshape x1 -> x0, local copies, waits for them, and re-layouts: 33.5 us -> none  [on_device(): probs.reshape(local_blocks, POOL, head_count, count // POOL, POOL)]
    psum x1 -> x0, blocking collectives: 30.8 us -> none  [on_device(): loss_value = lax.psum(loss_part, 'ctx')]
    all_to_all x0 -> x1, waiting for transfers between devices: none -> 17.9 us  [on_device(): lax.all_to_all(spread, 'ctx', 0, 0, axis_index_groups=groups, tiled=True)]
    reduce_max x2 -> x0, other arithmetic: 16.2 us -> none  [the longest x1 15.3 us: on_device(): probs.reshape(local_blocks, POOL, head_count, count // POOL, POOL)]
  transfers between devices with their start and end apart: 2 -> 2, of which waited for: 1 -> 2; matrix products, arithmetic and copies ran while one was open for 13% -> 0% of each run, Pallas kernels for 0% -> 5%
where the time goes in v1:
time: 99.2 us; the launch traced here: 98.9 us
  blocking collectives  45.2 us (46%)
  waiting for transfers between devices  24.5 us (25%)
  Pallas kernels  13.1 us (13%)
  starting transfers between devices  11.9 us (12%)
  local copies, waits for them, and re-layouts  3.39 us (3%)
    all_to_all x1, waiting for transfers between devices, on_device(): lax.all_to_all(spread, 'ctx', 0, 0, axis_index_groups=groups, tiled=True)  17.9 us
    all_to_all x1, blocking collectives, on_device(): own_tile = jnp.sum(lax.all_to_all(tiles, 'seq', 0, 0, tiled=True), axis=0)  17.3 us
    all_to_all x1, blocking collectives, on_device(): got = lax.all_to_all(send, 'ctx', 0, 0, tiled=True)  14.4 us
    all_to_all x1, blocking collectives, on_device(): grads = lax.all_to_all(spread, 'seq', 0, 0, tiled=True).reshape(grads.shape)  13.5 us
    all_to_all x1, starting transfers between devices, on_device(): lax.all_to_all(spread, 'ctx', 0, 0, axis_index_groups=groups, tiled=True)  9.15 us
    ppermute x1, waiting for transfers between devices, on_device(): lax.ppermute(near_keys, 'ctx', [(j, (j + near) % ctx_count) for j in rang...  6.56 us
    pallas_call x1, Pallas kernels, on_device(): pl.pallas_call(functools.partial(far_kernel, scale), out_shape=(jax.Shape...  5.54 us
    pallas_call x1, Pallas kernels, on_device(): pl.pallas_call(functools.partial(near_kernel, scale), out_shape=(jax.Shap...  4.18 us
  transfers between devices with their start and end apart: 2, of which 2 were waited for; matrix products, arithmetic and copies ran while one was open for 0% of the time, Pallas kernels for 5%

profile of v1, /device:TPU:1, one launch (start us, length us, event | category | flops | bytes accessed | tf_op | source)
XLA Modules:
  0.0 98.9 jit_solution(17283496091144865689)
XLA Ops:
  0.6 1.7 %broadcast_in_dim.30 = bf16[8,256,128]{2,1,0:T(8,128)(2,1)} broadcast(bf16[256,128]{1,0:T(8,128)(2,1)} %bitcast.24), dimensions={1,2} | broadcast | bytes 589824 | tf_op jit(solution)/shard_map/broadcast_in_dim | solution.py:243
  2.3 0.0 copy-start.4
  2.3 0.0 copy-start
  2.3 0.0 copy-start.1
  2.3 9.1 %all-to-all-start = ((bf16[8,256,128]{2,1,0:T(8,128)(2,1)}), bf16[8,256,128]{2,1,0:T(8,128)(2,1)S(1)}, u32[]{:S(2)}, u32[]{:S(2)}) async-start(bf16[8,256,128]{2,1,0:T(8,128)(2,1)} %broadcast_in_dim.30), calls=%async_computation | async-start | bytes 1048576 | tf_op jit(solution)/shard_map/all_to_all | solution.py:244
  11.5 0.0 copy-done.4
  11.5 0.0 copy-start.2
  11.5 17.9 %all-to-all-done = bf16[8,256,128]{2,1,0:T(8,128)(2,1)S(1)} async-done(((bf16[8,256,128]{2,1,0:T(8,128)(2,1)}), bf16[8,256,128]{2,1,0:T(8,128)(2,1)S(1)}, u32[]{:S(2)}, u32[]{:S(2)}) %all-to-all-start) | async-done | bytes 524320 | tf_op jit(solution)/shard_map/all_to_all | solution.py:244
  29.4 2.7 %collective-permute-start = (bf16[8,256,128]{2,1,0:T(8,128)(2,1)S(1)}, bf16[8,256,128]{2,1,0:T(8,128)(2,1)S(1)}, u32[]{:S(2)}, u32[]{:S(2)}) collective-permute-start(bf16[8,256,128]{2,1,0:T(8,128)(2,1)S(1)} %all-to-all-done), channel_id=1, source_target_pairs={{0,8},{1,9},{2,10},{3,11},{4,12},{5,13},{6,14},{7,15},{8,0},{9,1},... | collective-permute-start | bytes 1572872 | tf_op jit(solution)/shard_map/ppermute | solution.py:245
  32.2 0.1 iota_add_fusion
  32.3 0.1 add.31.kb_pos_ref
  32.4 0.0 copy-done
  32.4 0.0 copy-done.1
  32.4 0.0 copy-done.2
  32.4 0.6 local.1
  33.0 0.1 dynamic-slice_bitcast_fusion
  33.1 0.1 pad_add_fusion.own_ref
  33.2 0.0 copy-start.3
  33.2 4.2 %near.1 = (f32[32,1280]{1,0:T(8,128)S(1)}, f32[1,1280]{1,0:T(1,128)S(1)}, f32[8,1280]{1,0:T(8,128)S(1)}, f32[32,384]{1,0:T(8,128)S(1)}) custom-call(s32[1,32]{1,0:T(1,128)S(1)} %copy-done.4, s32[5]{0:T(128)S(1)} %pad_add_fusion.own_ref, bf16[5,256,128]{2,1,0:T(8,128)(2,1)S(1)} %bitcast.19, bf16[2048,128]{1,0:T(8,128)(2,1)S(1)} %bitcast.21, ...), custom_call_target="tpu_custom_call" | custom-call | flops 2684354560 | bytes 2097152 | tf_op jit(solution)/shard_map/near/pallas_call | solution.py:266
  37.4 6.6 %collective-permute-done = bf16[8,256,128]{2,1,0:T(8,128)(2,1)S(1)} collective-permute-done((bf16[8,256,128]{2,1,0:T(8,128)(2,1)S(1)}, bf16[8,256,128]{2,1,0:T(8,128)(2,1)S(1)}, u32[]{:S(2)}, u32[]{:S(2)}) %collective-permute-start) | collective-permute-done | bytes 524320 | tf_op jit(solution)/shard_map/ppermute | solution.py:245
  44.0 0.0 copy-done.3
  44.0 5.5 %far.1 = (f32[5,4,64]{2,1,0:T(4,128)}, f32[16,40,128]{2,1,0:T(8,128)S(1)}, f32[64,384]{1,0:T(8,128)S(1)}, f32[64,128]{1,0:T(8,128)S(1)}) custom-call(s32[1,32]{1,0:T(1,128)S(1)} %copy-done.4, s32[5]{0:T(128)S(1)} %pad_add_fusion.own_ref, bf16[5,256,128]{2,1,0:T(8,128)(2,1)S(1)} %bitcast.20, bf16[2048,128]{1,0:T(8,128)(2,1)S(1)} %bitcast.22, ...), custom_call_target="tpu_custom_call" | custom-call | tf_op jit(solution)/shard_map/far/pallas_call | solution.py:283
  49.5 14.4 %all_to_all.20.got_ref = f32[16,40,128]{2,1,0:T(8,128)S(1)} all-to-all(f32[16,40,128]{2,1,0:T(8,128)S(1)} %get-tuple-element.29), channel_id=1, replica_groups=mesh['seq'=16,'ctx'=16] {'ctx'}, dimensions={0} | all-to-all | bytes 655360 | tf_op jit(solution)/shard_map/all_to_all | solution.py:303
  63.9 2.7 %grad.1 = (f32[1024,128]{1,0:T(8,128)S(1)}, f32[1,1]{1,0:T(1,128)}) custom-call(f32[16,40,128]{2,1,0:T(8,128)S(1)} %all_to_all.20.got_ref, f32[64,384]{1,0:T(8,128)S(1)} %get-tuple-element.30.pool_ref, f32[64,128]{1,0:T(8,128)S(1)} %get-tuple-element.31.gate_k_ref, f32[5,128,128]{2,1,0:T(8,128)S(1)} %copy-done.1), custom_call_target="tpu_custom_call" | custom-call | tf_op jit(solution)/shard_map/grad/pallas_call | solution.py:304
  66.6 17.3 %all_to_all.21 = f32[16,64,128]{2,1,0:T(8,128)S(1)} all-to-all(f32[16,64,128]{2,1,0:T(8,128)S(1)} %bitcast.23), channel_id=1, replica_groups=mesh['seq'=16,'ctx'=16] {'seq'}, dimensions={0} | all-to-all | bytes 1048576 | tf_op jit(solution)/shard_map/all_to_all | solution.py:317
  84.0 13.5 %all_to_all.22 = f32[16,64,128]{2,1,0:T(8,128)S(1)} all-to-all(f32[16,64,128]{2,1,0:T(8,128)S(1)} %broadcast_in_dim.32), channel_id=1, replica_groups=mesh['seq'=16,'ctx'=16] {'seq'}, dimensions={0} | all-to-all | bytes 1048576 | tf_op jit(solution)/shard_map/all_to_all | solution.py:319
  97.5 0.7 slice.13
  98.2 0.7 slice.14
  (3 shorter events, 0.1 us)
Async XLA Ops:
  2.3 9.2 %copy-start.4 = (s32[1,32]{1,0:T(1,128)S(1)}, s32[1,32]{1,0:T(1,128)}, u32[]{:S(2)}) copy-start(s32[1,32]{1,0:T(1,128)} %order_ref.3) | copy-start | bytes 388
  2.3 30.0 %copy-start = (bf16[1,256,5,128]{3,1,2,0:T(8,128)(2,1)S(1)}, bf16[1,256,5,128]{3,1,2,0:T(8,128)(2,1)}, u32[]{:S(2)}) copy-start(bf16[1,256,5,128]{3,1,2,0:T(8,128)(2,1)} %param.6) | copy-start | bytes 983044
  2.3 30.0 %copy-start.1 = (f32[5,128,128]{2,1,0:T(8,128)S(1)}, f32[5,128,128]{2,1,0:T(8,128)}, u32[]{:S(2)}) copy-start(f32[5,128,128]{2,1,0:T(8,128)} %wq_ref.3) | copy-start | bytes 983044
  2.3 27.1 %all-to-all-start = ((bf16[8,256,128]{2,1,0:T(8,128)(2,1)}), bf16[8,256,128]{2,1,0:T(8,128)(2,1)S(1)}, u32[]{:S(2)}, u32[]{:S(2)}) async-start(bf16[8,256,128]{2,1,0:T(8,128)(2,1)} %broadcast_in_dim.30), calls=%async_computation | async-start | bytes 1048576 | tf_op jit(solution)/shard_map/all_to_all | solution.py:244
  11.5 20.9 %copy-start.2 = (bf16[1,256,128]{2,1,0:T(8,128)(2,1)S(1)}, bf16[1,256,128]{2,1,0:T(8,128)(2,1)}, u32[]{:S(2)}) copy-start(bf16[1,256,128]{2,1,0:T(8,128)(2,1)} %param.7) | copy-start | bytes 196612
  29.4 14.5 %collective-permute-start = (bf16[8,256,128]{2,1,0:T(8,128)(2,1)S(1)}, bf16[8,256,128]{2,1,0:T(8,128)(2,1)S(1)}, u32[]{:S(2)}, u32[]{:S(2)}) collective-permute-start(bf16[8,256,128]{2,1,0:T(8,128)(2,1)S(1)} %all-to-all-done), channel_id=1, source_target_pairs={{0,8},{1,9},{2,10},{3,11},{4,12},{5,13},{6,14},{7,15},{8,0},{9,1},... | collective-permute-start | bytes 1572872 | tf_op jit(solution)/shard_map/ppermute | solution.py:245
  33.2 10.8 %copy-start.3 = (f32[384,128]{1,0:T(8,128)S(1)}, f32[384,128]{1,0:T(8,128)}, u32[]{:S(2)}) copy-start(f32[384,128]{1,0:T(8,128)} %wk_ref.1) | copy-start | bytes 589828

commit v2 on v1

v2 whole, which is shorter than its diff:
```python
import functools
import math

import jax
import jax.numpy as jnp
from jax import lax
from jax.experimental import pallas as pl
from jax.experimental.pallas import tpu as pltpu
from jax.sharding import PartitionSpec as P

POOL = 64
LOW = -1e30
HIGHEST = lax.Precision.HIGHEST
VMEM = pl.BlockSpec(memory_space=pltpu.VMEM)
SMEM = pl.BlockSpec(memory_space=pltpu.SMEM)
PARAMS = pltpu.CompilerParams(vmem_limit_bytes=40 * 1024 * 1024)
SUB = 8
CHUNK = 512


def dot_nt(a, b, precision=None):
    return lax.dot_general(
        a, b, (((1,), (1,)), ((), ())), precision=precision, preferred_element_type=jnp.float32
    )


def dot_tn(a, b, precision=None):
    return lax.dot_general(
        a, b, (((0,), (0,)), ((), ())), precision=precision, preferred_element_type=jnp.float32
    )


def dot_nn(a, b, precision=None):
    return lax.dot_general(
        a, b, (((1,), (0,)), ((), ())), precision=precision, preferred_element_type=jnp.float32
    )


def local_kernel(scale, q_ref, k_ref, wq_ref, diag_ref, top_ref, tot_ref, pooled_ref, gate_q_ref):
    heads, rows, width = q_ref.shape
    half = rows // 2
    blocks = rows // POOL
    diag_ref[...] = jnp.full(diag_ref.shape, LOW, jnp.float32)
    key_row = lax.broadcasted_iota(jnp.int32, (half, half), 0)
    query_lane = lax.broadcasted_iota(jnp.int32, (half, half), 1)
    causal = key_row <= query_lane
    blank = jnp.zeros((SUB - blocks, width), jnp.float32)
    for h in range(heads):
        q = q_ref[h]
        pooled = jnp.sum(q.astype(jnp.float32).reshape(blocks, POOL, width), axis=1) * (1.0 / POOL)
        pooled = jnp.concatenate([pooled, blank], axis=0)
        pooled_ref[h * SUB : (h + 1) * SUB, :] = pooled
        gate_q_ref[h * SUB : (h + 1) * SUB, :] = dot_nn(pooled, wq_ref[h], HIGHEST)
        for part in range(2):
            s = dot_nt(k_ref[part * half : (part + 1) * half, :], q[part * half : (part + 1) * half, :])
            s = jnp.where(causal, s * scale, LOW)
            per = half // POOL
            block_top = jnp.max(s.reshape(per, POOL, half), axis=1)
            top = jnp.max(block_top, axis=0, keepdims=True)
            p = jnp.exp2(s - top)
            lanes = slice(h * rows + part * half, h * rows + (part + 1) * half)
            diag_ref[part * per : (part + 1) * per, lanes] = block_top
            top_ref[:, lanes] = top
            tot_ref[:, lanes] = jnp.sum(p.reshape(half // SUB, SUB, half), axis=0)


def spread_kernel(k_ref, out_ref):
    k = k_ref[...]
    for j in range(out_ref.shape[0]):
        out_ref[j] = k


def attend(scale, order_ref, first_half, query_owner, q_ref, k_ref, top_ref, tot_ref, map_ref, pool_ref=None):
    heads, rows, width = q_ref.shape
    half = rows // 2
    per = half // POOL
    kb_count = CHUNK // POOL
    halves = CHUNK // half
    kb_row = lax.broadcasted_iota(jnp.int32, (kb_count, rows), 0)
    lane = lax.broadcasted_iota(jnp.int32, (kb_count, rows), 1)
    query_half = jnp.where(lane < half, order_ref[0, 2 * query_owner], order_ref[0, 2 * query_owner + 1])

    def step(i, carry):
        start = pl.multiple_of(i * CHUNK, CHUNK)
        keys = k_ref[pl.ds(start, CHUNK), :]
        key_half = jnp.full((kb_count, rows), order_ref[0, first_half + i * halves], jnp.int32)
        for j in range(1, halves):
            key_half = jnp.where(kb_row >= j * per, order_ref[0, first_half + i * halves + j], key_half)
        seen = jnp.where(key_half < query_half, 1.0, 0.0)
        seen_rows = jnp.broadcast_to(seen[:, None, :], (kb_count, SUB, rows)) > 0.5
        seen = seen > 0.5
        here = pl.ds(pl.multiple_of(i * kb_count, kb_count), kb_count)
        if pool_ref is not None:
            x = keys.astype(jnp.float32).reshape(kb_count, POOL, width)
            pool_ref[here, 0:width] = jnp.max(x, axis=1)
            pool_ref[here, width : 2 * width] = jnp.min(x, axis=1)
            pool_ref[here, 2 * width : 3 * width] = jnp.sum(x, axis=1) * (1.0 / POOL)
        for h in range(heads):
            lanes = slice(h * rows, (h + 1) * rows)
            s = dot_nt(keys, q_ref[h]) * scale
            s = s.reshape(kb_count, POOL // SUB, SUB, rows)
            block_top = jnp.max(jnp.max(s, axis=1), axis=1)
            block_top = jnp.where(seen, block_top, LOW)
            map_ref[here, lanes] = block_top
            top = top_ref[:, lanes]
            new_top = jnp.maximum(top, jnp.max(block_top, axis=0, keepdims=True))
            part = jnp.sum(jnp.exp2(s - new_top.reshape(1, 1, 1, rows)), axis=1)
            part = jnp.sum(jnp.where(seen_rows, part, 0.0), axis=0)
            tot_ref[:, lanes] = tot_ref[:, lanes] * jnp.exp2(top - new_top) + part
            top_ref[:, lanes] = new_top
        return carry

    lax.fori_loop(0, k_ref.shape[0] // CHUNK, step, 0)


def partner_kernel(scale, order_ref, own_ref, q_ref, k_ref, send_ref, top_ref, tot_ref):
    heads, rows, width = q_ref.shape
    columns = heads * rows
    near = k_ref.shape[0] // POOL
    top_ref[...] = jnp.full(top_ref.shape, LOW, jnp.float32)
    tot_ref[...] = jnp.zeros(tot_ref.shape, jnp.float32)
    attend(
        scale,
        order_ref,
        own_ref[1],
        own_ref[2],
        q_ref,
        k_ref,
        top_ref,
        tot_ref,
        send_ref,
        send_ref.at[:, pl.ds(columns, 3 * width)],
    )
    send_ref[near:, :] = jnp.zeros((send_ref.shape[0] - near, send_ref.shape[1]), jnp.float32)
    send_ref[near : near + 1, 0:columns] = top_ref[...]
    send_ref[near + 1 : near + 2, 0:columns] = jnp.sum(tot_ref[...], axis=0, keepdims=True)


def own_kernel(
    scale, order_ref, own_ref, q_ref, k_ref, top_in, tot_in, sent_ref, wk_ref, map_ref, top_ref, tot_ref, gate_k_ref
):
    columns = map_ref.shape[1]
    near = map_ref.shape[0]
    top_ref[...] = top_in[...]
    tot_ref[...] = tot_in[...]
    gate_k_ref[...] = dot_nn(sent_ref[0:near, columns:], wk_ref[...], HIGHEST)
    attend(scale, order_ref, own_ref[1], own_ref[0], q_ref, k_ref, top_ref, tot_ref, map_ref)


def finish_kernel(
    order_ref,
    own_ref,
    near_map,
    near_top,
    near_tot,
    near_gate_k,
    sent_ref,
    got_ref,
    diag_ref,
    pooled_ref,
    gate_q_ref,
    wk_ref,
    kb_pos_ref,
    target_ref,
    keep_ref,
    give_ref,
    gate_k_ref,
    pool_ref,
    map_ref,
    block_ref,
    grad_ref,
):
    width = pooled_ref.shape[1]
    columns = near_top.shape[1]
    near = near_map.shape[0]
    total = 2 * near
    heads, blocks, _ = target_ref.shape
    rows = columns // heads
    half = rows // 2
    per = half // POOL
    place = own_ref[0]
    near_at = pl.multiple_of(own_ref[1] * per, near)
    far_at = pl.multiple_of(near - own_ref[1] * per, near)
    map_ref[pl.ds(near_at, near), :] = near_map[...]
    map_ref[pl.ds(far_at, near), :] = got_ref[0:near, 0:columns]
    pool_ref[pl.ds(near_at, near), :] = sent_ref[0:near, columns:]
    pool_ref[pl.ds(far_at, near), :] = got_ref[0:near, columns:]
    gate_k_ref[pl.ds(near_at, near), :] = near_gate_k[...]
    gate_k_ref[pl.ds(far_at, near), :] = dot_nn(got_ref[0:near, columns:], wk_ref[...], HIGHEST)
    block_ref[...] = jnp.ones(block_ref.shape, jnp.float32)
    kb_index = lax.broadcasted_iota(jnp.int32, (total, half), 0)
    own_block = place * blocks
    for h in range(heads):
        for part in range(2):
            lanes = slice(h * rows + part * half, h * rows + (part + 1) * half)
            m = map_ref[:, lanes]
            for j in range(part * per, (part + 1) * per):
                m = jnp.where(kb_index == own_block + j, diag_ref[j : j + 1, lanes], m)
            far_top = got_ref[near : near + 1, lanes]
            top = jnp.maximum(near_top[:, lanes], far_top)
            tot = jnp.sum(near_tot[:, lanes], axis=0, keepdims=True) * jnp.exp2(near_top[:, lanes] - top)
            tot = tot + got_ref[near + 1 : near + 2, lanes] * jnp.exp2(far_top - top)
            b = jnp.exp2(m - (top + jnp.log2(tot))).T.reshape(per, POOL, total)
            block_ref[h * SUB + part * per : h * SUB + (part + 1) * per, :] = jnp.max(b, axis=1)
    block_map = block_ref[...]
    target = block_map / jnp.sum(block_map, axis=1, keepdims=True)
    for h in range(heads):
        target_ref[h] = target[h * SUB : h * SUB + blocks, :]
    gate_k = gate_k_ref[...]
    gate_width = gate_k.shape[1]
    row = lax.broadcasted_iota(jnp.int32, (heads * SUB, total), 0) % SUB
    query_half = jnp.where(row < per, order_ref[0, 2 * place], order_ref[0, 2 * place + 1])
    visible = (kb_pos_ref[...] <= query_half * per + row % per) & (row < blocks)
    logits = dot_nt(gate_q_ref[...], gate_k, HIGHEST) * gate_width ** (-0.5)
    peak = jnp.max(jnp.where(visible, logits, LOW), axis=1, keepdims=True)
    weights = jnp.where(visible, jnp.exp(logits - peak), 0.0)
    norm_sum = jnp.where(row[:, :1] < blocks, jnp.sum(weights, axis=1, keepdims=True), 1.0)
    log_gate = logits - peak - jnp.log(norm_sum)
    count = heads * total
    loss = -jnp.sum(jnp.where(visible, target * log_gate, 0.0)) / count
    d_logits = jnp.where(visible, weights / norm_sum - target, 0.0) / count * gate_width ** (-0.5)
    gate_q = gate_q_ref[...]
    gate_q_grad = dot_nn(d_logits, gate_k, HIGHEST)
    for h in range(heads):
        here = slice(h * SUB, (h + 1) * SUB)
        grad_ref[h * width : (h + 1) * width, :] = dot_tn(pooled_ref[here, :], gate_q_grad[here], HIGHEST)
    grad_ref[heads * width :, :] = dot_tn(pool_ref[...], dot_tn(d_logits, gate_q, HIGHEST), HIGHEST)
    part = keep_ref.shape[0]
    keep_ref[...] = grad_ref[pl.ds(pl.multiple_of(own_ref[3] * part, part), part), :]
    give_ref[0:part, :] = grad_ref[pl.ds(pl.multiple_of((1 - own_ref[3]) * part, part), part), :]
    lane = lax.broadcasted_iota(jnp.int32, (SUB, gate_width), 1)
    give_ref[part:, :] = jnp.where(lane == own_ref[4], loss, 0.0)


def fold_kernel(keep_ref, give_ref, got_ref, out_ref):
    tiles, tile_rows, width = out_ref.shape
    part = keep_ref.shape[0]
    rows = part // tiles
    out_ref[:, 0:rows, :] = (keep_ref[...] + got_ref[0:part, :]).reshape(tiles, rows, width)
    loss = give_ref[part:, :] + got_ref[part:, :]
    out_ref[:, rows:, :] = jnp.broadcast_to(loss[None], (tiles, tile_rows - rows, width))


def sum_kernel(parts_ref, out_ref):
    total = jnp.sum(parts_ref[...], axis=0)
    for j in range(out_ref.shape[0]):
        out_ref[j] = total


def join_kernel(own_ref, parts_ref, out_ref, loss_ref):
    total = jnp.sum(parts_ref[...], axis=0)
    rows = out_ref.shape[1]
    for j in range(out_ref.shape[0]):
        out_ref[j] = total[:rows]
    losses = total[rows : rows + 1]
    lane = lax.broadcasted_iota(jnp.int32, losses.shape, 1)
    loss_ref[...] = jnp.sum(jnp.where(lane == own_ref[4], losses, 0.0), axis=1, keepdims=True)


def last_kernel(own_ref, mine_ref, other_ref, grad_q_ref, grad_k_ref):
    heads, width, _ = grad_q_ref.shape
    part = mine_ref.shape[0]
    whole = part // width
    first = own_ref[3] == 0
    for h in range(2 * whole):
        here = slice(h % whole * width, (h % whole + 1) * width)
        mine = first if h < whole else jnp.logical_not(first)
        tile = jnp.where(mine, mine_ref[here, :], other_ref[here, :])
        if h < heads:
            grad_q_ref[h] = tile
        else:
            grad_k_ref[(h - heads) * width : (h - heads + 1) * width, :] = tile


def f32(*shape):
    return jax.ShapeDtypeStruct(shape, jnp.float32)


def call(kernel, out_shape, specs, name, scratch=(), cost=None):
    return pl.pallas_call(
        kernel,
        out_shape=out_shape,
        in_specs=specs,
        out_specs=tuple(VMEM for _ in out_shape),
        scratch_shapes=scratch,
        compiler_params=PARAMS,
        cost_estimate=cost,
        name=name,
    )


def on_device(order, queries, keys, w_query_gate, w_key_gate):
    tok_rows = queries.shape[1]
    heads = queries.shape[2]
    width = queries.shape[3]
    gate_width = w_key_gate.shape[1]
    per_half = tok_rows // 2 // POOL
    blocks = tok_rows // POOL
    ctx_count = lax.axis_size("ctx")
    seq_count = lax.axis_size("seq")
    near = ctx_count // 2
    total = ctx_count * blocks
    scale = width ** (-0.5) * math.log2(math.e)
    columns = heads * tok_rows

    place = lax.axis_index("ctx")
    own_seq = lax.axis_index("seq")
    own = jnp.stack(
        [place, jnp.where(place < near, 0, 2 * near), lax.rem(place + near, ctx_count), lax.rem(own_seq, 2), own_seq]
    ).astype(jnp.int32)
    kb_pos = (order.reshape(-1, 1) * per_half + jnp.arange(per_half, dtype=jnp.int32)[None]).reshape(1, total)

    across = [(j, (j + near) % ctx_count) for j in range(ctx_count)]
    q = jnp.transpose(queries[0], (1, 0, 2))
    partner_q = lax.ppermute(q, "ctx", across)
    (spread,) = call(
        spread_kernel, (jax.ShapeDtypeStruct((near, tok_rows, width), keys.dtype),), [VMEM], "spread"
    )(keys[0])
    groups = [list(range(near)), list(range(near, ctx_count))]
    near_keys = lax.all_to_all(spread, "ctx", 0, 0, axis_index_groups=groups, tiled=True)
    near_keys = near_keys.reshape(near * tok_rows, width)

    diag, top, tot, pooled, gate_q = call(
        functools.partial(local_kernel, scale),
        (f32(SUB, columns), f32(1, columns), f32(SUB, columns), f32(heads * SUB, width), f32(heads * SUB, gate_width)),
        [VMEM] * 3,
        "local",
        cost=pl.CostEstimate(flops=4 * 10**8, bytes_accessed=10**6, transcendentals=10**5),
    )(q, keys[0], w_query_gate)

    cost = pl.CostEstimate(
        flops=8 * near * tok_rows * columns * width,
        bytes_accessed=10**6,
        transcendentals=near * tok_rows * columns,
    )
    state = [pltpu.VMEM((1, columns), jnp.float32), pltpu.VMEM((SUB, columns), jnp.float32)]
    (sent,) = call(
        functools.partial(partner_kernel, scale),
        (f32(near * blocks + SUB, columns + 3 * width),),
        [SMEM, SMEM, VMEM, VMEM],
        "partner",
        scratch=state,
        cost=cost,
    )(order, own, partner_q, near_keys)
    far = lax.ppermute(sent, "ctx", across)

    near_map, top, tot, near_gate_k = call(
        functools.partial(own_kernel, scale),
        (f32(near * blocks, columns), f32(1, columns), f32(SUB, columns), f32(near * blocks, gate_width)),
        [SMEM, SMEM] + [VMEM] * 6,
        "own",
        cost=cost,
    )(order, own, q, near_keys, top, tot, sent, w_key_gate)

    grad_rows = heads * width + 3 * width
    part = grad_rows // 2
    target, keep, give = call(
        finish_kernel,
        (f32(heads, blocks, total), f32(part, gate_width), f32(part + SUB, gate_width)),
        [SMEM, SMEM] + [VMEM] * 11,
        "finish",
        scratch=[
            pltpu.VMEM((total, gate_width), jnp.float32),
            pltpu.VMEM((total, 3 * width), jnp.float32),
            pltpu.VMEM((total, columns), jnp.float32),
            pltpu.VMEM((heads * SUB, total), jnp.float32),
            pltpu.VMEM((grad_rows, gate_width), jnp.float32),
        ],
    )(order, own, near_map, top, tot, near_gate_k, sent, far, diag, pooled, gate_q, w_key_gate, kb_pos)

    every = ("seq", "ctx")
    half_seq = seq_count // 2

    def flat(x_lo, y, core, x_hi, z):
        return (x_lo * half_seq + y * 2 + core) * ctx_count + x_hi * near + z

    ys = range(half_seq // 2)
    zs = range(near)
    pair = (0, 1)
    cores = [
        (flat(a, y, b, c, z), flat(a, y, 1 - b, c, z)) for a in pair for y in ys for b in pair for c in pair for z in zs
    ]
    planes = [[flat(a, y, b, c, z) for a in pair for c in pair for y in ys] for b in pair for z in zs]
    tiles = len(planes[0])
    got = lax.ppermute(give, every, cores)
    (parts,) = call(
        fold_kernel, (f32(tiles, part // tiles + SUB, gate_width),), [VMEM] * 3, "fold"
    )(keep, give, got)
    parts = lax.all_to_all(parts, every, 0, 0, axis_index_groups=planes, tiled=True)
    (spread,) = call(sum_kernel, (f32(near, part // tiles + SUB, gate_width),), [VMEM], "sum")(parts)
    parts = lax.all_to_all(spread, "ctx", 0, 0, axis_index_groups=groups, tiled=True)
    spread, loss = call(
        join_kernel, (f32(tiles, part // tiles, gate_width), f32(1, 1)), [SMEM, VMEM], "join"
    )(own, parts)
    mine = lax.all_to_all(spread, every, 0, 0, axis_index_groups=planes, tiled=True).reshape(part, gate_width)
    other = lax.ppermute(mine, every, cores)
    grad_q, grad_k = call(
        last_kernel,
        (f32(heads, width, gate_width), f32(3 * width, gate_width)),
        [SMEM, VMEM, VMEM],
        "last",
    )(own, mine, other)
    return (target[None, None], grad_q, grad_k, loss.reshape(1))


def solution(mesh):
    placed = (P("seq", None), P("seq", "ctx", None, None), P("seq", "ctx", None), P(), P())
    return jax.shard_map(
        on_device,
        mesh=mesh,
        in_specs=placed,
        out_specs=(P("seq", "ctx", None, None, None), P(), P(), P("seq")),
        check_vma=False,
    )
```

time: 99.2 us -> 91.7 us (0.924)
  blocking collectives: 45.2 us -> 35.8 us
  starting transfers between devices: 11.9 us -> 20.5 us
  waiting for transfers between devices: 24.5 us -> 18.3 us
  local copies, waits for them, and re-layouts: 3.39 us -> 1.04 us
  Pallas kernels: 13.1 us -> 15 us
    all_to_all x1, waiting for transfers between devices: 17.9 us -> 8.09 us  [on_device(): lax.all_to_all(spread, 'ctx', 0, 0, axis_index_groups=groups, tiled=True)]
    all_to_all x3, blocking collectives: 45.2 us -> 35.8 us  [the longest x1 14.8 us: on_device(): lax.all_to_all(parts, every, 0, 0, axis_index_groups=planes, tiled=True)]
    ppermute x1 -> x4, starting transfers between devices: 2.74 us -> 11.4 us  [the longest x1 4.3 us: on_device(): other = lax.ppermute(mine, every, cores)]
    ppermute x1 -> x4, waiting for transfers between devices: 6.56 us -> 10.2 us  [the longest x1 6.86 us: on_device(): partner_q = lax.ppermute(q, 'ctx', across)]
    pallas_call x4 -> x9, Pallas kernels: 13.1 us -> 15 us  [the longest x1 4.46 us: on_device(): call(functools.partial(own_kernel, scale), (f32(near * blocks, columns),...]
    broadcast_in_dim x2 -> x0, local copies, waits for them, and re-layouts: 1.75 us -> none  [the longest x1 1.71 us: on_device(): spread = jnp.broadcast_to(keys, (near,) + keys.shape[1:])]
    slice x2 -> x0, local copies, waits for them, and re-layouts: 1.44 us -> none  [the longest x1 0.75 us: on_device(): grad_q = grads[:heads * width].reshape(heads, width, -1)]
  transfers between devices with their start and end apart: 2 -> 5, of which waited for: 2 -> 5; matrix products, arithmetic and copies ran while one was open for 0% -> 0% of each run, Pallas kernels for 5% -> 6%
where the time goes in v2:
time: 91.7 us; the launch traced here: 91.4 us
  blocking collectives  35.8 us (39%)
  starting transfers between devices  20.5 us (22%)
  waiting for transfers between devices  18.3 us (20%)
  Pallas kernels  15 us (16%)
  local copies, waits for them, and re-layouts  1.04 us (1%)
    all_to_all x1, blocking collectives, on_device(): lax.all_to_all(parts, every, 0, 0, axis_index_groups=planes, tiled=True)  14.8 us
    all_to_all x1, blocking collectives, on_device(): lax.all_to_all(spread, 'ctx', 0, 0, axis_index_groups=groups, tiled=True)  10.7 us
    all_to_all x1, blocking collectives, on_device(): lax.all_to_all(spread, every, 0, 0, axis_index_groups=planes, tiled=True)  10.3 us
    all_to_all x1, starting transfers between devices, on_device(): lax.all_to_all(spread, 'ctx', 0, 0, axis_index_groups=groups, tiled=True)  9.15 us
    all_to_all x1, waiting for transfers between devices, on_device(): lax.all_to_all(spread, 'ctx', 0, 0, axis_index_groups=groups, tiled=True)  8.09 us
    ppermute x1, waiting for transfers between devices, on_device(): partner_q = lax.ppermute(q, 'ctx', across)  6.86 us
    pallas_call x1, Pallas kernels, on_device(): call(functools.partial(own_kernel, scale), (f32(near * blocks, columns),...  4.46 us
    ppermute x1, starting transfers between devices, on_device(): other = lax.ppermute(mine, every, cores)  4.3 us
  transfers between devices with their start and end apart: 5, of which 5 were waited for; matrix products, arithmetic and copies ran while one was open for 0% of the time, Pallas kernels for 6%

profile of v2, /device:TPU:1, one launch (start us, length us, event | category | flops | bytes accessed | tf_op | source)
XLA Modules:
  0.0 91.4 jit_solution(16401554982180811312)
XLA Ops:
  0.6 0.0 copy-start.1
  0.6 0.8 copy-done.1
  1.5 0.9 spread.1
  2.3 0.0 copy-start.5
  2.3 9.1 %all-to-all-start = ((bf16[8,256,128]{2,1,0:T(8,128)(2,1)}), bf16[8,256,128]{2,1,0:T(8,128)(2,1)S(1)}, u32[]{:S(2)}, u32[]{:S(2)}) async-start(bf16[8,256,128]{2,1,0:T(8,128)(2,1)} %spread.1), calls=%async_computation | async-start | bytes 1048576 | tf_op jit(solution)/shard_map/all_to_all | solution.py:320
  11.5 0.0 copy-start.3
  11.5 0.0 copy-done.5
  11.5 2.8 %collective-permute-start = (bf16[5,256,128]{2,1,0:T(8,128)(2,1)S(1)}, bf16[5,256,128]{2,1,0:T(8,128)(2,1)S(1)}, u32[]{:S(2)}, u32[]{:S(2)}) collective-permute-start(bf16[5,256,128]{2,1,0:T(8,128)(2,1)S(1)} %bitcast.21), channel_id=1, source_target_pairs={{0,8},{1,9},{2,10},{3,11},{4,12},{5,13},{6,14},{7,15},{8,0},{9,1},... | collective-permute-start | bytes 983048 | tf_op jit(solution)/shard_map/ppermute | solution.py:315
  14.3 0.0 copy-done.3
  14.3 0.1 stack.23.own_ref
  14.4 0.1 iota_add_fusion
  14.5 6.9 %collective-permute-done.q_ref = bf16[5,256,128]{2,1,0:T(8,128)(2,1)S(1)} collective-permute-done((bf16[5,256,128]{2,1,0:T(8,128)(2,1)S(1)}, bf16[5,256,128]{2,1,0:T(8,128)(2,1)S(1)}, u32[]{:S(2)}, u32[]{:S(2)}) %collective-permute-start) | collective-permute-done | bytes 327712 | tf_op jit(solution)/shard_map/ppermute | solution.py:315
  21.4 8.1 %all-to-all-done = bf16[8,256,128]{2,1,0:T(8,128)(2,1)S(1)} async-done(((bf16[8,256,128]{2,1,0:T(8,128)(2,1)}), bf16[8,256,128]{2,1,0:T(8,128)(2,1)S(1)}, u32[]{:S(2)}, u32[]{:S(2)}) %all-to-all-start) | async-done | bytes 524320 | tf_op jit(solution)/shard_map/all_to_all | solution.py:320
  29.4 0.0 copy-start.2
  29.4 0.0 copy-start.4
  29.4 4.2 %partner.1.sent_ref = f32[40,1664]{1,0:T(8,128)S(1)} custom-call(s32[1,32]{1,0:T(1,128)S(1)} %copy-done.3, s32[5]{0:T(128)S(1)} %stack.23.own_ref, bf16[5,256,128]{2,1,0:T(8,128)(2,1)S(1)} %collective-permute-done.q_ref, bf16[2048,128]{1,0:T(8,128)(2,1)S(1)} %bitcast.17), custom_call_target="tpu_custom_call" | custom-call | flops 2684354560 | bytes 1000000 | tf_op jit(solution)/shard_map/partner/pallas_call | solution.py:337
  33.7 0.0 copy-start
  33.7 2.8 %collective-permute-start.1 = (f32[40,1664]{1,0:T(8,128)S(1)}, f32[40,1664]{1,0:T(8,128)S(1)}, u32[]{:S(2)}, u32[]{:S(2)}) collective-permute-start(f32[40,1664]{1,0:T(8,128)S(1)} %partner.1.sent_ref), channel_id=1, source_target_pairs={{0,8},{1,9},{2,10},{3,11},{4,12},{5,13},{6,14},{7,15},{8,0},{9,1},... | collective-permute-start | bytes 798728 | tf_op jit(solution)/shard_map/ppermute | solution.py:345
  36.5 0.0 copy-done.2
  36.5 0.0 copy-done.4
  36.5 0.6 local.1
  37.2 0.1 add.30.kb_pos_ref
  37.3 0.0 copy-done
  37.3 4.5 %own.1 = (f32[32,1280]{1,0:T(8,128)S(1)}, f32[1,1280]{1,0:T(1,128)S(1)}, f32[8,1280]{1,0:T(8,128)S(1)}, f32[32,128]{1,0:T(8,128)S(1)}) custom-call(s32[1,32]{1,0:T(1,128)S(1)} %copy-done.3, s32[5]{0:T(128)S(1)} %stack.23.own_ref, bf16[5,256,128]{2,1,0:T(8,128)(2,1)S(1)} %bitcast.23, bf16[2048,128]{1,0:T(8,128)(2,1)S(1)} %bitcast.18, ...), custom_call_target="tpu_custom_call" | custom-call | flops 2684354560 | bytes 1000000 | tf_op jit(solution)/shard_map/own/pallas_call | solution.py:347
  41.8 1.0 %collective-permute-done.1.got_ref = f32[40,1664]{1,0:T(8,128)S(1)} collective-permute-done((f32[40,1664]{1,0:T(8,128)S(1)}, f32[40,1664]{1,0:T(8,128)S(1)}, u32[]{:S(2)}, u32[]{:S(2)}) %collective-permute-start.1) | collective-permute-done | bytes 266272 | tf_op jit(solution)/shard_map/ppermute | solution.py:345
  42.7 2.2 %finish.1 = (f32[5,4,64]{2,1,0:T(4,128)}, f32[512,128]{1,0:T(8,128)S(1)}, f32[520,128]{1,0:T(8,128)S(1)}) custom-call(s32[1,32]{1,0:T(1,128)S(1)} %copy-done.3, s32[5]{0:T(128)S(1)} %stack.23.own_ref, f32[32,1280]{1,0:T(8,128)S(1)} %get-tuple-element.22.near_map, f32[1,1280]{1,0:T(1,128)S(1)} %get-tuple-element.23.near_top, ...), custom_call_target="tpu_custom_call" | custom-call | tf_op jit(solution)/shard_map/finish/pallas_call | solution.py:357
  45.0 1.4 %collective-permute-start.2 = (f32[520,128]{1,0:T(8,128)S(1)}, f32[520,128]{1,0:T(8,128)S(1)}, u32[]{:S(2)}, u32[]{:S(2)}) collective-permute-start(f32[520,128]{1,0:T(8,128)S(1)} %get-tuple-element.31.give_ref), channel_id=1, source_target_pairs={{0,16},{1,17},{2,18},{3,19},{4,20},{5,21},{6,22},{7,23},{8,24},{9,... | collective-permute-start | bytes 798728 | tf_op jit(solution)/shard_map/ppermute | solution.py:385
  46.4 1.2 %collective-permute-done.2.got_ref = f32[520,128]{1,0:T(8,128)S(1)} collective-permute-done((f32[520,128]{1,0:T(8,128)S(1)}, f32[520,128]{1,0:T(8,128)S(1)}, u32[]{:S(2)}, u32[]{:S(2)}) %collective-permute-start.2) | collective-permute-done | bytes 266272 | tf_op jit(solution)/shard_map/ppermute | solution.py:385
  47.6 14.8 %all_to_all.20.parts_ref = f32[16,40,128]{2,1,0:T(8,128)S(1)} all-to-all(f32[16,40,128]{2,1,0:T(8,128)S(1)} %fold.1), channel_id=1, replica_groups={{0,32,64,96,8,40,72,104,128,160,192,224,136,168,200,232},{1,33,65,97,9,..., dimensions={0} | all-to-all | bytes 655360 | tf_op jit(solution)/shard_map/all_to_all | solution.py:389
  62.4 10.7 %all_to_all.21.parts_ref = f32[8,40,128]{2,1,0:T(8,128)S(1)} all-to-all(f32[8,40,128]{2,1,0:T(8,128)S(1)} %sum.1), channel_id=1, replica_groups={{0,1,2,3,4,5,6,7},{8,9,10,11,12,13,14,15},{16,17,18,19,20,21,22,23},{24..., dimensions={0} | all-to-all | bytes 327680 | tf_op jit(solution)/shard_map/all_to_all | solution.py:391
  73.1 1.1 %join.1 = (f32[16,32,128]{2,1,0:T(8,128)S(1)}, f32[1,1]{1,0:T(1,128)}) custom-call(s32[5]{0:T(128)S(1)} %stack.23.own_ref, f32[8,40,128]{2,1,0:T(8,128)S(1)} %all_to_all.21.parts_ref), custom_call_target="tpu_custom_call" | custom-call | tf_op jit(solution)/shard_map/join/pallas_call | solution.py:392
  74.3 10.3 %all_to_all.22 = f32[16,32,128]{2,1,0:T(8,128)S(1)} all-to-all(f32[16,32,128]{2,1,0:T(8,128)S(1)} %get-tuple-element.32), channel_id=1, replica_groups={{0,32,64,96,8,40,72,104,128,160,192,224,136,168,200,232},{1,33,65,97,9,..., dimensions={0} | all-to-all | bytes 524288 | tf_op jit(solution)/shard_map/all_to_all | solution.py:395
  84.6 4.3 %collective-permute-start.3 = (f32[512,128]{1,0:T(8,128)S(1)}, f32[512,128]{1,0:T(8,128)S(1)}, u32[]{:S(2)}, u32[]{:S(2)}) collective-permute-start(f32[512,128]{1,0:T(8,128)S(1)} %bitcast.15), channel_id=1, source_target_pairs={{0,16},{1,17},{2,18},{3,19},{4,20},{5,21},{6,22},{7,23},{8,24},{9,... | collective-permute-start | bytes 786440 | tf_op jit(solution)/shard_map/ppermute | solution.py:396
  88.9 1.2 %collective-permute-done.3.other_ref = f32[512,128]{1,0:T(8,128)S(1)} collective-permute-done((f32[512,128]{1,0:T(8,128)S(1)}, f32[512,128]{1,0:T(8,128)S(1)}, u32[]{:S(2)}, u32[]{:S(2)}) %collective-permute-start.3) | collective-permute-done | bytes 262176 | tf_op jit(solution)/shard_map/ppermute | solution.py:396
  90.0 1.4 %last.1 = (f32[5,128,128]{2,1,0:T(8,128)}, f32[384,128]{1,0:T(8,128)}) custom-call(s32[5]{0:T(128)S(1)} %stack.23.own_ref, f32[512,128]{1,0:T(8,128)S(1)} %bitcast.16, f32[512,128]{1,0:T(8,128)S(1)} %collective-permute-done.3.other_ref), custom_call_target="tpu_custom_call" | custom-call | tf_op jit(solution)/shard_map/last/pallas_call | solution.py:397
  (3 shorter events, 0.1 us)
Async XLA Ops:
  0.6 0.8 copy-start.1
  2.3 9.2 %copy-start.5 = (bf16[1,256,5,128]{3,1,2,0:T(8,128)(2,1)S(1)}, bf16[1,256,5,128]{3,1,2,0:T(8,128)(2,1)}, u32[]{:S(2)}) copy-start(bf16[1,256,5,128]{3,1,2,0:T(8,128)(2,1)} %param.6) | copy-start | bytes 983044
  2.3 27.1 %all-to-all-start = ((bf16[8,256,128]{2,1,0:T(8,128)(2,1)}), bf16[8,256,128]{2,1,0:T(8,128)(2,1)S(1)}, u32[]{:S(2)}, u32[]{:S(2)}) async-start(bf16[8,256,128]{2,1,0:T(8,128)(2,1)} %spread.1), calls=%async_computation | async-start | bytes 1048576 | tf_op jit(solution)/shard_map/all_to_all | solution.py:320
  11.5 2.8 %copy-start.3 = (s32[1,32]{1,0:T(1,128)S(1)}, s32[1,32]{1,0:T(1,128)}, u32[]{:S(2)}) copy-start(s32[1,32]{1,0:T(1,128)} %order_ref.5) | copy-start | bytes 388
  11.5 9.9 %collective-permute-start = (bf16[5,256,128]{2,1,0:T(8,128)(2,1)S(1)}, bf16[5,256,128]{2,1,0:T(8,128)(2,1)S(1)}, u32[]{:S(2)}, u32[]{:S(2)}) collective-permute-start(bf16[5,256,128]{2,1,0:T(8,128)(2,1)S(1)} %bitcast.21), channel_id=1, source_target_pairs={{0,8},{1,9},{2,10},{3,11},{4,12},{5,13},{6,14},{7,15},{8,0},{9,1},... | collective-permute-start | bytes 983048 | tf_op jit(solution)/shard_map/ppermute | solution.py:315
  29.4 7.1 %copy-start.2 = (bf16[1,256,128]{2,1,0:T(8,128)(2,1)S(1)}, bf16[1,256,128]{2,1,0:T(8,128)(2,1)}, u32[]{:S(2)}) copy-start(bf16[1,256,128]{2,1,0:T(8,128)(2,1)} %param.7) | copy-start | bytes 196612
  29.4 7.1 %copy-start.4 = (f32[5,128,128]{2,1,0:T(8,128)S(1)}, f32[5,128,128]{2,1,0:T(8,128)}, u32[]{:S(2)}) copy-start(f32[5,128,128]{2,1,0:T(8,128)} %wq_ref.1) | copy-start | bytes 983044
  33.7 3.6 %copy-start = (f32[384,128]{1,0:T(8,128)S(1)}, f32[384,128]{1,0:T(8,128)}, u32[]{:S(2)}) copy-start(f32[384,128]{1,0:T(8,128)} %wk_ref.3) | copy-start | bytes 589828
  33.7 9.1 %collective-permute-start.1 = (f32[40,1664]{1,0:T(8,128)S(1)}, f32[40,1664]{1,0:T(8,128)S(1)}, u32[]{:S(2)}, u32[]{:S(2)}) collective-permute-start(f32[40,1664]{1,0:T(8,128)S(1)} %partner.1.sent_ref), channel_id=1, source_target_pairs={{0,8},{1,9},{2,10},{3,11},{4,12},{5,13},{6,14},{7,15},{8,0},{9,1},... | collective-permute-start | bytes 798728 | tf_op jit(solution)/shard_map/ppermute | solution.py:345
  45.0 2.6 %collective-permute-start.2 = (f32[520,128]{1,0:T(8,128)S(1)}, f32[520,128]{1,0:T(8,128)S(1)}, u32[]{:S(2)}, u32[]{:S(2)}) collective-permute-start(f32[520,128]{1,0:T(8,128)S(1)} %get-tuple-element.31.give_ref), channel_id=1, source_target_pairs={{0,16},{1,17},{2,18},{3,19},{4,20},{5,21},{6,22},{7,23},{8,24},{9,... | collective-permute-start | bytes 798728 | tf_op jit(solution)/shard_map/ppermute | solution.py:385
  84.6 5.5 %collective-permute-start.3 = (f32[512,128]{1,0:T(8,128)S(1)}, f32[512,128]{1,0:T(8,128)S(1)}, u32[]{:S(2)}, u32[]{:S(2)}) collective-permute-start(f32[512,128]{1,0:T(8,128)S(1)} %bitcast.15), channel_id=1, source_target_pairs={{0,16},{1,17},{2,18},{3,19},{4,20},{5,21},{6,22},{7,23},{8,24},{9,... | collective-permute-start | bytes 786440 | tf_op jit(solution)/shard_map/ppermute | solution.py:396

commit v3 on v2

v3 whole, which is shorter than its diff:
```python
import functools
import math

import jax
import jax.numpy as jnp
from jax import lax
from jax.experimental import pallas as pl
from jax.experimental.pallas import tpu as pltpu
from jax.sharding import PartitionSpec as P

POOL = 64
LOW = -1e30
HIGHEST = lax.Precision.HIGHEST
VMEM = pl.BlockSpec(memory_space=pltpu.VMEM)
SMEM = pl.BlockSpec(memory_space=pltpu.SMEM)
ANY = pl.BlockSpec(memory_space=pl.ANY)
PARAMS = pltpu.CompilerParams(vmem_limit_bytes=40 * 1024 * 1024)
SUB = 8
NT = (((1,), (1,)), ((), ()))
TN = (((0,), (0,)), ((), ()))
NN = (((1,), (0,)), ((), ()))


def dot(a, b, dims, precision=None):
    return lax.dot_general(a, b, dims, precision=precision, preferred_element_type=jnp.float32)


def split(x):
    high = x.astype(jnp.bfloat16)
    return high, (x - high.astype(jnp.float32)).astype(jnp.bfloat16)


def dot_split(a, b, dims):
    a_high, a_low = split(a)
    b_high, b_low = split(b)
    return dot(a_high, b_high, dims) + (dot(a_high, b_low, dims) + dot(a_low, b_high, dims))


def local_kernel(scale, q_ref, k_ref, wq_ref, *refs):
    diag_ref, top_ref, tot_ref, pooled_ref, gate_q_ref, q2_ref = refs[-6:]
    heads, rows, width = q_ref.shape
    half = rows // 2
    blocks = rows // POOL
    per = half // POOL
    diag_ref[...] = jnp.full(diag_ref.shape, LOW, jnp.float32)
    key_row = lax.broadcasted_iota(jnp.int32, (half, half), 0)
    query_lane = lax.broadcasted_iota(jnp.int32, (half, half), 1)
    causal = key_row <= query_lane
    blank = jnp.zeros((SUB - blocks, width), jnp.float32)
    for h in range(heads):
        q = q_ref[h].astype(jnp.float32)
        pooled = jnp.sum(q.reshape(blocks, POOL, width), axis=1) * (1.0 / POOL)
        pooled = jnp.concatenate([pooled, blank], axis=0)
        pooled_ref[h * SUB : (h + 1) * SUB, :] = pooled
        gate_q_ref[h * SUB : (h + 1) * SUB, :] = dot(pooled, wq_ref[h], NN, HIGHEST)
        high, low = split(q * scale)
        q2_ref[h, :, 0:width] = high
        q2_ref[h, :, width:] = low
        for part in range(2):
            keys = k_ref[part * half : (part + 1) * half, :]
            s = dot(jnp.concatenate([keys, keys], axis=1), q2_ref[h, part * half : (part + 1) * half, :], NT)
            s = jnp.where(causal, s, LOW)
            block_top = jnp.max(s.reshape(per, POOL, half), axis=1)
            top = jnp.max(block_top, axis=0, keepdims=True)
            p = jnp.exp2(s - top)
            lanes = slice(h * rows + part * half, h * rows + (part + 1) * half)
            diag_ref[part * per : (part + 1) * per, lanes] = block_top
            top_ref[:, lanes] = top
            tot_ref[:, lanes] = jnp.sum(p.reshape(half // SUB, SUB, half), axis=0)


def attend(order_ref, own_ref, q2_ref, chunks, top_in, tot_in, top_ref, tot_ref, map_ref, pool_ref):
    heads, rows, _ = q2_ref.shape
    half = rows // 2
    per = half // POOL
    blocks = rows // POOL
    place, along, near = own_ref[0], own_ref[1], own_ref[3]
    tops = [top_in[:, h * rows : (h + 1) * rows] for h in range(heads)]
    tots = [tot_in[:, h * rows : (h + 1) * rows] for h in range(heads)]
    row = 0
    for first in range(0, len(chunks), 2):
        group = chunks[first : first + 2]
        keys = jnp.concatenate([read() for read, _, _ in group], axis=0)
        count = len(group) * blocks
        x = keys.astype(jnp.float32).reshape(count, POOL, keys.shape[1])
        pool_ref[row : row + count, :] = jnp.concatenate(
            [jnp.max(x, axis=1), jnp.min(x, axis=1), jnp.sum(x, axis=1) * (1.0 / POOL)], axis=1
        )
        kb_row = lax.broadcasted_iota(jnp.int32, (count, rows), 0)
        lane = lax.broadcasted_iota(jnp.int32, (count, rows), 1)
        query_half = jnp.where(lane < half, order_ref[0, 2 * place], order_ref[0, 2 * place + 1])
        key_half = jnp.zeros((count, rows), jnp.int32)
        for j, (_, base, offset) in enumerate(group):
            owner = base + lax.rem(along + offset, near)
            for part in range(2):
                key_half = jnp.where(kb_row >= j * blocks + part * per, order_ref[0, 2 * owner + part], key_half)
        seen = jnp.where(key_half < query_half, 1.0, 0.0)
        seen_rows = jnp.broadcast_to(seen[:, None, :], (count, SUB, rows)) > 0.5
        seen = seen > 0.5
        keys = jnp.concatenate([keys, keys], axis=1)
        for h in range(heads):
            s = dot(keys, q2_ref[h], NT).reshape(count, POOL // SUB, SUB, rows)
            block_top = jnp.max(jnp.max(s, axis=1), axis=1)
            block_top = jnp.where(seen, block_top, LOW)
            map_ref[row : row + count, h * rows : (h + 1) * rows] = block_top
            top = jnp.maximum(tops[h], jnp.max(block_top, axis=0, keepdims=True))
            part = jnp.sum(jnp.exp2(s - top.reshape(1, 1, 1, rows)), axis=1)
            part = jnp.sum(jnp.where(seen_rows, part, 0.0), axis=0)
            tots[h] = tots[h] * jnp.exp2(tops[h] - top) + part
            tops[h] = top
        row += count
    for h in range(heads):
        top_ref[:, h * rows : (h + 1) * rows] = tops[h]
        tot_ref[:, h * rows : (h + 1) * rows] = tots[h]


def chunks_of(refs, layout, own_ref, rows):
    chunks = []
    for ref, (other, offsets) in zip(refs, layout):
        for j, offset in enumerate(offsets):
            read = functools.partial(lambda r, j: r[j * rows : (j + 1) * rows, :], ref, j)
            chunks.append((read, own_ref[2 + 2 * other], offset))
    return chunks


def attend_kernel(layout, *refs):
    order_ref, own_ref, q2_ref, top_in, tot_in = refs[:5]
    top_ref, tot_ref, map_ref, pool_ref = refs[-4:]
    chunks = chunks_of(refs[5:-4], layout, own_ref, q2_ref.shape[1])
    attend(order_ref, own_ref, q2_ref, chunks, top_in, tot_in, top_ref, tot_ref, map_ref, pool_ref)


def finish_kernel(layout, places, *refs):
    order_ref, own_ref, q2_ref, top_in, tot_in, diag_ref, pooled_ref, gate_q_ref, wk_ref, kb_pos_ref = refs[:10]
    key_refs = refs[10 : 10 + len(layout)]
    earlier = refs[10 + len(layout) : -12]
    target_ref, keep_ref, give_ref = refs[-12:-9]
    top_ref, tot_ref, last_map, last_pool, map_ref, rel_pool, pool_ref, block_ref, grad_ref = refs[-9:]
    heads, rows, _ = q2_ref.shape
    half = rows // 2
    per = half // POOL
    blocks = rows // POOL
    total = map_ref.shape[0]
    near = total // 2
    width = pooled_ref.shape[1]
    place = own_ref[0]
    chunks = chunks_of(key_refs, layout, own_ref, rows)
    attend(order_ref, own_ref, q2_ref, chunks, top_in, tot_in, top_ref, tot_ref, last_map, last_pool)
    maps = list(earlier[0::2]) + [last_map]
    pools = list(earlier[1::2]) + [last_pool]
    for map_in, pool_in, where in zip(maps, pools, places):
        for j, (other, offset) in enumerate(where):
            here = slice(other * near + offset * blocks, other * near + (offset + 1) * blocks)
            map_ref[here, :] = map_in[j * blocks : (j + 1) * blocks, :]
            rel_pool[here, :] = pool_in[j * blocks : (j + 1) * blocks, :]
    shift = own_ref[1] * blocks
    for other in range(2):
        at = pl.multiple_of(own_ref[2 + 2 * other] * blocks, near)
        pool_ref[pl.ds(at, near), :] = pltpu.roll(rel_pool[other * near : (other + 1) * near, :], shift, 0)
    block_ref[...] = jnp.ones(block_ref.shape, jnp.float32)
    for h in range(heads):
        for part in range(2):
            lanes = slice(h * rows + part * half, h * rows + (part + 1) * half)
            own_rows = slice(part * per, (part + 1) * per)
            map_ref[own_rows, lanes] = diag_ref[own_rows, lanes]
            tot = jnp.sum(tot_ref[:, lanes], axis=0, keepdims=True)
            b = jnp.exp2(map_ref[:, lanes] - (top_ref[:, lanes] + jnp.log2(tot)))
            b = jnp.max(b.T.reshape(per, POOL, total), axis=1)
            block_ref[h * SUB + part * per : h * SUB + (part + 1) * per, :] = b
    block_map = block_ref[...]
    copies = 128 // near
    group = [
        pltpu.roll(jnp.concatenate([block_map[:, j * near : (j + 1) * near]] * copies, axis=1), shift, 1)[:, :total]
        for j in range(2)
    ]
    lane = lax.broadcasted_iota(jnp.int32, (heads * SUB, total), 1)
    in_near = (lane >= own_ref[2] * blocks) & (lane < (own_ref[2] + own_ref[3]) * blocks)
    block_map = jnp.where(in_near, group[0], group[1])
    target = block_map / jnp.sum(block_map, axis=1, keepdims=True)
    for h in range(heads):
        target_ref[h] = target[h * SUB : h * SUB + blocks, :]
    gate_q = gate_q_ref[...]
    gate_k = dot(pool_ref[...], wk_ref[...], NN, HIGHEST)
    gate_width = gate_k.shape[1]
    row = lax.broadcasted_iota(jnp.int32, (heads * SUB, total), 0) % SUB
    query_half = jnp.where(row < per, order_ref[0, 2 * place], order_ref[0, 2 * place + 1])
    visible = (kb_pos_ref[...] <= query_half * per + row % per) & (row < blocks)
    logits = dot(gate_q, gate_k, NT, HIGHEST) * gate_width ** (-0.5)
    peak = jnp.max(jnp.where(visible, logits, LOW), axis=1, keepdims=True)
    weights = jnp.where(visible, jnp.exp(logits - peak), 0.0)
    norm_sum = jnp.where(row[:, :1] < blocks, jnp.sum(weights, axis=1, keepdims=True), 1.0)
    log_gate = logits - peak - jnp.log(norm_sum)
    count = heads * total
    loss = -jnp.sum(jnp.where(visible, target * log_gate, 0.0)) / count
    d_logits = jnp.where(visible, weights / norm_sum - target, 0.0) / count * gate_width ** (-0.5)
    gate_q_grad = dot_split(d_logits, gate_k, NN)
    for h in range(heads):
        here = slice(h * SUB, (h + 1) * SUB)
        grad_ref[h * width : (h + 1) * width, :] = dot_split(pooled_ref[here, :], gate_q_grad[here], TN)
    grad_ref[heads * width :, :] = dot_split(pool_ref[...], dot_split(d_logits, gate_q, TN), TN)
    part = keep_ref.shape[0]
    keep_ref[...] = grad_ref[pl.ds(pl.multiple_of(own_ref[5] * part, part), part), :]
    give_ref[0:part, :] = grad_ref[pl.ds(pl.multiple_of((1 - own_ref[5]) * part, part), part), :]
    lane = lax.broadcasted_iota(jnp.int32, (SUB, gate_width), 1)
    give_ref[part:, :] = jnp.where(lane == own_ref[6], loss, 0.0)


def fold_kernel(keep_ref, give_ref, got_ref, out_ref):
    tiles, tile_rows, width = out_ref.shape
    part = keep_ref.shape[0]
    rows = part // tiles
    out_ref[:, 0:rows, :] = (keep_ref[...] + got_ref[0:part, :]).reshape(tiles, rows, width)
    loss = give_ref[part:, :] + got_ref[part:, :]
    out_ref[:, rows:, :] = jnp.broadcast_to(loss[None], (tiles, tile_rows - rows, width))


def sum_kernel(parts_ref, out_ref):
    total = jnp.sum(parts_ref[...], axis=0)
    for j in range(out_ref.shape[0]):
        out_ref[j] = total


def join_kernel(parts_ref, out_ref, loss_ref):
    total = jnp.sum(parts_ref[...], axis=0)
    rows = out_ref.shape[1]
    for j in range(out_ref.shape[0]):
        out_ref[j] = total[:rows]
    loss_ref[...] = total[rows:]


def last_kernel(own_ref, mine_ref, other_ref, losses_ref, grad_q_ref, grad_k_ref, loss_ref):
    heads, width, _ = grad_q_ref.shape
    part = mine_ref.shape[0]
    whole = part // width
    first = own_ref[5] == 0
    for h in range(2 * whole):
        here = slice(h % whole * width, (h % whole + 1) * width)
        mine = first if h < whole else jnp.logical_not(first)
        tile = jnp.where(mine, mine_ref[here, :], other_ref[here, :])
        if h < heads:
            grad_q_ref[h] = tile
        else:
            grad_k_ref[(h - heads) * width : (h - heads + 1) * width, :] = tile
    losses = losses_ref[0:1, :]
    lane = lax.broadcasted_iota(jnp.int32, losses.shape, 1)
    loss_ref[...] = jnp.sum(jnp.where(lane == own_ref[6], losses, 0.0), axis=1, keepdims=True)


def f32(*shape):
    return jax.ShapeDtypeStruct(shape, jnp.float32)


def call(kernel, out_shape, specs, name, scratch=(), cost=None):
    return pl.pallas_call(
        kernel,
        out_shape=out_shape,
        in_specs=specs,
        out_specs=tuple(VMEM for _ in out_shape),
        scratch_shapes=scratch,
        compiler_params=PARAMS,
        cost_estimate=cost,
        name=name,
    )


def on_device(order, queries, keys, w_query_gate, w_key_gate):
    tok_rows = queries.shape[1]
    heads = queries.shape[2]
    width = queries.shape[3]
    gate_width = w_key_gate.shape[1]
    per_half = tok_rows // 2 // POOL
    blocks = tok_rows // POOL
    ctx_count = lax.axis_size("ctx")
    seq_count = lax.axis_size("seq")
    near = ctx_count // 2
    total = ctx_count * blocks
    scale = width ** (-0.5) * math.log2(math.e)
    columns = heads * tok_rows

    place = lax.axis_index("ctx")
    own_seq = lax.axis_index("seq")
    along = lax.rem(place, near)
    base = place - along
    index = jnp.arange(8, dtype=jnp.int32)
    own = jnp.zeros((8,), jnp.int32)
    for j, value in enumerate((place, along, base, near, near - base, lax.rem(own_seq, 2), own_seq)):
        own = jnp.where(index == j, value, own)
    kb_pos = (order.reshape(-1, 1) * per_half + jnp.arange(per_half, dtype=jnp.int32)[None]).reshape(1, total)

    def get(x, offset):
        return lax.ppermute(x, "ctx", [(j, j // near * near + (j - offset) % near) for j in range(ctx_count)])

    def across(x):
        return lax.ppermute(x, "ctx", [(j, (j + near) % ctx_count) for j in range(ctx_count)])

    own_keys = keys[0]
    step = {offset: get(own_keys, offset % near) for offset in (1, -1, near // 2)}
    ahead = get(jnp.concatenate([own_keys, step[1]], axis=0), 2)
    behind = get(jnp.concatenate([own_keys, step[-1]], axis=0), near - 2)
    mid = jnp.concatenate([own_keys, step[1], step[-1], step[near // 2]], axis=0)
    mid_far = across(mid)
    mid_from = (0, 1, near - 1, near // 2)
    ahead_from = (2, 3)
    behind_from = (near - 2, near - 3)

    q = jnp.transpose(queries[0], (1, 0, 2))
    state = (f32(1, columns), f32(SUB, columns))
    diag, top, tot, pooled, gate_q, q2 = call(
        functools.partial(local_kernel, scale),
        (f32(SUB, columns),)
        + state
        + (
            f32(heads * SUB, width),
            f32(heads * SUB, gate_width),
            jax.ShapeDtypeStruct((heads, tok_rows, 2 * width), jnp.bfloat16),
        ),
        [VMEM] * 3 + [ANY] * 2,
        "local",
        cost=pl.CostEstimate(flops=4 * 10**8, bytes_accessed=10**6, transcendentals=10**5),
    )(q, own_keys, w_query_gate, step[1], step[-1])

    def attend_to(layout, top, tot, *keys):
        count = sum(len(offsets) for _, offsets in layout)
        return call(
            functools.partial(attend_kernel, layout),
            state + (f32(count * blocks, columns), f32(count * blocks, 3 * width)),
            [SMEM, SMEM] + [VMEM] * (3 + len(keys)),
            "attend",
            cost=pl.CostEstimate(flops=1200000000, bytes_accessed=10**6, transcendentals=1300000),
        )(order, own, q2, top, tot, *keys)

    layouts = (
        ((0, mid_from),),
        ((0, ahead_from), (0, behind_from)),
        ((1, mid_from),),
        ((1, ahead_from), (1, behind_from)),
    )
    places = [[(other, offset) for other, offsets in layout for offset in offsets] for layout in layouts]
    ahead_far = across(ahead)
    behind_far = across(behind)
    earlier = []
    for layout, key_parts in zip(layouts[:-1], ((mid,), (ahead, behind), (mid_far,))):
        top, tot, *found = attend_to(layout, top, tot, *key_parts)
        earlier += found

    grad_rows = heads * width + 3 * width
    part = grad_rows // 2
    last_blocks = len(places[-1]) * blocks
    target, keep, give = call(
        functools.partial(finish_kernel, layouts[-1], places),
        (f32(heads, blocks, total), f32(part, gate_width), f32(part + SUB, gate_width)),
        [SMEM, SMEM] + [VMEM] * (10 + len(earlier)),
        "finish",
        scratch=[
            pltpu.VMEM(shape, jnp.float32)
            for shape in (
                (1, columns),
                (SUB, columns),
                (last_blocks, columns),
                (last_blocks, 3 * width),
                (total, columns),
                (total, 3 * width),
                (total, 3 * width),
                (heads * SUB, total),
                (grad_rows, gate_width),
            )
        ],
    )(order, own, q2, top, tot, diag, pooled, gate_q, w_key_gate, kb_pos, ahead_far, behind_far, *earlier)

    every = ("seq", "ctx")
    half_seq = seq_count // 2

    def flat(x_lo, y, core, x_hi, z):
        return (x_lo * half_seq + y * 2 + core) * ctx_count + x_hi * near + z

    ys = range(half_seq // 2)
    zs = range(near)
    pair = (0, 1)
    cores = [
        (flat(a, y, b, c, z), flat(a, y, 1 - b, c, z)) for a in pair for y in ys for b in pair for c in pair for z in zs
    ]
    planes = [[flat(a, y, b, c, z) for a in pair for c in pair for y in ys] for b in pair for z in zs]
    tiles = len(planes[0])
    got = lax.ppermute(give, every, cores)
    (parts,) = call(
        fold_kernel, (f32(tiles, part // tiles + SUB, gate_width),), [VMEM] * 3, "fold"
    )(keep, give, got)
    parts = lax.all_to_all(parts, every, 0, 0, axis_index_groups=planes, tiled=True)
    (spread,) = call(sum_kernel, (f32(near, part // tiles + SUB, gate_width),), [VMEM], "sum")(parts)
    parts = lax.all_to_all(
        spread,
        "ctx",
        0,
        0,
        axis_index_groups=[list(range(near)), list(range(near, ctx_count))],
        tiled=True,
    )
    spread, losses = call(
        join_kernel, (f32(tiles, part // tiles, gate_width), f32(SUB, gate_width)), [VMEM], "join"
    )(parts)
    mine = lax.all_to_all(spread, every, 0, 0, axis_index_groups=planes, tiled=True).reshape(part, gate_width)
    other = lax.ppermute(mine, every, cores)
    grad_q, grad_k, loss = call(
        last_kernel,
        (f32(heads, width, gate_width), f32(3 * width, gate_width), f32(1, 1)),
        [SMEM, VMEM, VMEM, VMEM],
        "last",
    )(own, mine, other, losses)
    return (target[None, None], grad_q, grad_k, loss.reshape(1))


def solution(mesh):
    placed = (P("seq", None), P("seq", "ctx", None, None), P("seq", "ctx", None), P(), P())
    return jax.shard_map(
        on_device,
        mesh=mesh,
        in_specs=placed,
        out_specs=(P("seq", "ctx", None, None, None), P(), P(), P("seq")),
        check_vma=False,
    )
```

time: 91.7 us -> 81.6 us (0.89)
  waiting for transfers between devices: 18.3 us -> 4.42 us
  starting transfers between devices: 20.5 us -> 25.9 us
  Pallas kernels: 15 us -> 12 us
  blocking collectives: 35.8 us -> 36.8 us
    ppermute x2 -> x8, starting transfers between devices: 5.67 us -> 17.6 us  [the longest x5 11.7 us: get(): lax.ppermute(x, 'ctx', [(j, j // near * near + (j - offset) % near) for j...]
    all_to_all x1 -> x0, starting transfers between devices: 9.15 us -> none  [on_device(): lax.all_to_all(spread, 'ctx', 0, 0, axis_index_groups=groups, tiled=True)]
    all_to_all x1 -> x0, waiting for transfers between devices: 8.09 us -> none  [on_device(): lax.all_to_all(spread, 'ctx', 0, 0, axis_index_groups=groups, tiled=True)]
    ppermute x2 -> x8, waiting for transfers between devices: 7.85 us -> 2.09 us  [the longest x5 1.51 us: get(): lax.ppermute(x, 'ctx', [(j, j // near * near + (j - offset) % near) for j...]
    pallas_call x6, Pallas kernels: 13.5 us -> 10.6 us  [the longest x3 6.29 us: attend_to(): call(functools.partial(attend_kernel, layout), state + (f32(count * block...]
    ppermute x1, starting transfers between devices: 1.43 us -> 3.7 us  [on_device(): got = lax.ppermute(give, every, cores)]
    all_to_all x1, blocking collectives: 10.7 us -> 12.7 us  [on_device(): lax.all_to_all(spread, 'ctx', 0, 0, axis_index_groups=[list(range(near)),...]
  transfers between devices with their start and end apart: 5 -> 10, of which waited for: 5 -> 4; matrix products, arithmetic and copies ran while one was open for 0% -> 1% of each run, Pallas kernels for 6% -> 9%
where the time goes in v3:
time: 81.6 us; the launch traced here: 81.4 us
  blocking collectives  36.8 us (45%)
  starting transfers between devices  25.9 us (32%)
  Pallas kernels  12 us (15%)
  waiting for transfers between devices  4.42 us (5%)
    all_to_all x1, blocking collectives, on_device(): lax.all_to_all(parts, every, 0, 0, axis_index_groups=planes, tiled=True)  13.9 us
    all_to_all x1, blocking collectives, on_device(): lax.all_to_all(spread, 'ctx', 0, 0, axis_index_groups=[list(range(near)),...  12.7 us
    ppermute x5, starting transfers between devices, get(): lax.ppermute(x, 'ctx', [(j, j // near * near + (j - offset) % near) for j...  11.7 us
    all_to_all x1, blocking collectives, on_device(): lax.all_to_all(spread, every, 0, 0, axis_index_groups=planes, tiled=True)  10.3 us
    pallas_call x3, Pallas kernels, attend_to(): call(functools.partial(attend_kernel, layout), state + (f32(count * block...  6.29 us
    ppermute x3, starting transfers between devices, across(): lax.ppermute(x, 'ctx', [(j, (j + near) % ctx_count) for j in range(ctx_co...  5.89 us
    ppermute x1, starting transfers between devices, on_device(): other = lax.ppermute(mine, every, cores)  4.56 us
    ppermute x1, starting transfers between devices, on_device(): got = lax.ppermute(give, every, cores)  3.7 us
  transfers between devices with their start and end apart: 10, of which 4 were waited for; matrix products, arithmetic and copies ran while one was open for 1% of the time, Pallas kernels for 9%

profile of v3, /device:TPU:1, one launch (start us, length us, event | category | flops | bytes accessed | tf_op | source)
XLA Modules:
  0.0 81.4 jit_solution(1778638946711142041)
XLA Ops:
  0.6 0.0 copy-start
  0.6 6.5 %collective-permute-start = (bf16[256,128]{1,0:T(8,128)(2,1)}, bf16[256,128]{1,0:T(8,128)(2,1)S(1)}, u32[]{:S(2)}, u32[]{:S(2)}) collective-permute-start(bf16[256,128]{1,0:T(8,128)(2,1)} %bitcast.11), channel_id=1, source_target_pairs={{0,7},{1,0},{2,1},{3,2},{4,3},{5,4},{6,5},{7,6},{8,15},{9,8},{10,9... | collective-permute-start | bytes 196616 | tf_op jit(solution)/shard_map/ppermute | solution.py:291
  7.1 0.0 collective-permute-start.1
  7.1 2.8 %collective-permute-start.2 = (bf16[256,128]{1,0:T(8,128)(2,1)}, bf16[256,128]{1,0:T(8,128)(2,1)S(1)}, u32[]{:S(2)}, u32[]{:S(2)}) collective-permute-start(bf16[256,128]{1,0:T(8,128)(2,1)} %bitcast.13), channel_id=1, source_target_pairs={{0,4},{1,5},{2,6},{3,7},{4,0},{5,1},{6,2},{7,3},{8,12},{9,13},{10,... | collective-permute-start | bytes 196616 | tf_op jit(solution)/shard_map/ppermute | solution.py:291
  9.9 0.7 multiply_bitcast_fusion
  10.6 0.1 iota_add_fusion
  10.7 0.1 add.26.refs_9_
  10.8 0.0 collective-permute-done.refs_0_
  10.8 1.5 %collective-permute-done.1.refs_1_ = bf16[256,128]{1,0:T(8,128)(2,1)S(1)} collective-permute-done((bf16[256,128]{1,0:T(8,128)(2,1)}, bf16[256,128]{1,0:T(8,128)(2,1)S(1)}, u32[]{:S(2)}, u32[]{:S(2)}) %collective-permute-start.1) | collective-permute-done | bytes 65568 | tf_op jit(solution)/shard_map/ppermute | solution.py:291
  12.3 0.0 copy-done
  12.3 0.0 copy-start.4
  12.3 0.0 copy-start.3
  12.3 0.1 collective-permute-start.3
  12.4 2.4 %collective-permute-start.4 = (bf16[512,128]{1,0:T(8,128)(2,1)S(1)}, bf16[512,128]{1,0:T(8,128)(2,1)S(1)}, u32[]{:S(2)}, u32[]{:S(2)}) collective-permute-start(bf16[512,128]{1,0:T(8,128)(2,1)S(1)} %get-tuple-element.56), channel_id=1, source_target_pairs={{0,2},{1,3},{2,4},{3,5},{4,6},{5,7},{6,0},{7,1},{8,10},{9,11},{10,... | collective-permute-start | bytes 393224 | tf_op jit(solution)/shard_map/ppermute | solution.py:291
  14.8 0.0 collective-permute-done.2
  14.8 2.8 %collective-permute-start.5 = (bf16[1024,128]{1,0:T(8,128)(2,1)S(1)}, bf16[1024,128]{1,0:T(8,128)(2,1)S(1)}, u32[]{:S(2)}, u32[]{:S(2)}) collective-permute-start(bf16[1024,128]{1,0:T(8,128)(2,1)S(1)} %pad_maximum_fusion.refs_5_), channel_id=1, source_target_pairs={{0,8},{1,9},{2,10},{3,11},{4,12},{5,13},{6,14},{7,15},{8,0},{9,1},... | collective-permute-start | bytes 786440 | tf_op jit(solution)/shard_map/ppermute | solution.py:294
  17.6 0.0 copy-done.4
  17.6 0.0 copy-done.3
  17.6 0.7 local.1
  18.3 0.0 copy-start.2
  18.4 0.6 copy-done.2
  19.0 2.1 %attend.3 = (f32[1,1280]{1,0:T(1,128)S(1)}, f32[8,1280]{1,0:T(8,128)S(1)}, f32[16,1280]{1,0:T(8,128)S(1)}, f32[16,384]{1,0:T(8,128)S(1)}) custom-call(s32[1,32]{1,0:T(1,128)S(1)} %copy-done.2, s32[8]{0:T(128)S(1)} %compare_select_fusion.6.refs_1_.own_ref, bf16[5,256,256]{2,1,0:T(8,128)(2,1)S(1)} %get-tuple-element.30.refs_2_, ...), custom_call_target="tpu_custom_call" | custom-call | flops 1200000000 | bytes 1000000 | tf_op jit(solution)/shard_map/attend/pallas_call | solution.py:324
  21.1 0.0 collective-permute-done.3.refs_5_
  21.1 1.7 %collective-permute-start.6 = (bf16[512,128]{1,0:T(8,128)(2,1)S(1)}, bf16[512,128]{1,0:T(8,128)(2,1)S(1)}, u32[]{:S(2)}, u32[]{:S(2)}) collective-permute-start(bf16[512,128]{1,0:T(8,128)(2,1)S(1)} %collective-permute-done.3.refs_5_), channel_id=1, source_target_pairs={{0,8},{1,9},{2,10},{3,11},{4,12},{5,13},{6,14},{7,15},{8,0},{9,1},... | collective-permute-start | bytes 393224 | tf_op jit(solution)/shard_map/ppermute | solution.py:294
  22.8 0.0 collective-permute-done.4.refs_6_
  22.8 1.3 %collective-permute-start.7 = (bf16[512,128]{1,0:T(8,128)(2,1)S(1)}, bf16[512,128]{1,0:T(8,128)(2,1)S(1)}, u32[]{:S(2)}, u32[]{:S(2)}) collective-permute-start(bf16[512,128]{1,0:T(8,128)(2,1)S(1)} %collective-permute-done.4.refs_6_), channel_id=1, source_target_pairs={{0,8},{1,9},{2,10},{3,11},{4,12},{5,13},{6,14},{7,15},{8,0},{9,1},... | collective-permute-start | bytes 393224 | tf_op jit(solution)/shard_map/ppermute | solution.py:294
  24.2 2.1 %attend.4 = (f32[1,1280]{1,0:T(1,128)S(1)}, f32[8,1280]{1,0:T(8,128)S(1)}, f32[16,1280]{1,0:T(8,128)S(1)}, f32[16,384]{1,0:T(8,128)S(1)}) custom-call(s32[1,32]{1,0:T(1,128)S(1)} %copy-done.2, s32[8]{0:T(128)S(1)} %compare_select_fusion.6.refs_1_.own_ref, bf16[5,256,256]{2,1,0:T(8,128)(2,1)S(1)} %get-tuple-element.30.refs_2_, ...), custom_call_target="tpu_custom_call" | custom-call | flops 1200000000 | bytes 1000000 | tf_op jit(solution)/shard_map/attend/pallas_call | solution.py:324
  26.3 0.0 collective-permute-done.5.refs_5_
  26.3 0.0 copy-start.1
  26.3 2.1 %attend.5 = (f32[1,1280]{1,0:T(1,128)S(1)}, f32[8,1280]{1,0:T(8,128)S(1)}, f32[16,1280]{1,0:T(8,128)S(1)}, f32[16,384]{1,0:T(8,128)S(1)}) custom-call(s32[1,32]{1,0:T(1,128)S(1)} %copy-done.2, s32[8]{0:T(128)S(1)} %compare_select_fusion.6.refs_1_.own_ref, bf16[5,256,256]{2,1,0:T(8,128)(2,1)S(1)} %get-tuple-element.30.refs_2_, ...), custom_call_target="tpu_custom_call" | custom-call | flops 1200000000 | bytes 1000000 | tf_op jit(solution)/shard_map/attend/pallas_call | solution.py:324
  28.4 0.0 collective-permute-done.6.refs_10_
  28.4 0.6 collective-permute-done.7.refs_11_
  29.0 0.0 copy-done.1
  29.0 3.6 %finish.1 = (f32[5,4,64]{2,1,0:T(4,128)}, f32[512,128]{1,0:T(8,128)S(1)}, f32[520,128]{1,0:T(8,128)S(1)}) custom-call(s32[1,32]{1,0:T(1,128)S(1)} %copy-done.2, s32[8]{0:T(128)S(1)} %compare_select_fusion.6.refs_1_.own_ref, bf16[5,256,256]{2,1,0:T(8,128)(2,1)S(1)} %get-tuple-element.30.refs_2_, f32[1,1280]{1,0:T(1,128)S(1)} %get-tuple-element.37.refs_3_, ...), custom_call_target="tpu_custom_call" | custom-call | tf_op jit(solution)/shard_map/finish/pallas_call | solution.py:349
  32.6 3.7 %collective-permute-start.8 = (f32[520,128]{1,0:T(8,128)S(1)}, f32[520,128]{1,0:T(8,128)S(1)}, u32[]{:S(2)}, u32[]{:S(2)}) collective-permute-start(f32[520,128]{1,0:T(8,128)S(1)} %get-tuple-element.50.give_ref), channel_id=1, source_target_pairs={{0,16},{1,17},{2,18},{3,19},{4,20},{5,21},{6,22},{7,23},{8,24},{9,... | collective-permute-start | bytes 798728 | tf_op jit(solution)/shard_map/ppermute | solution.py:384
  36.3 1.2 %collective-permute-done.8.got_ref = f32[520,128]{1,0:T(8,128)S(1)} collective-permute-done((f32[520,128]{1,0:T(8,128)S(1)}, f32[520,128]{1,0:T(8,128)S(1)}, u32[]{:S(2)}, u32[]{:S(2)}) %collective-permute-start.8) | collective-permute-done | bytes 266272 | tf_op jit(solution)/shard_map/ppermute | solution.py:384
  37.5 13.9 %all_to_all.15.parts_ref = f32[16,40,128]{2,1,0:T(8,128)S(1)} all-to-all(f32[16,40,128]{2,1,0:T(8,128)S(1)} %fold.1), channel_id=1, replica_groups={{0,32,64,96,8,40,72,104,128,160,192,224,136,168,200,232},{1,33,65,97,9,..., dimensions={0} | all-to-all | bytes 655360 | tf_op jit(solution)/shard_map/all_to_all | solution.py:388
  51.4 12.7 %all_to_all.16.parts_ref = f32[8,40,128]{2,1,0:T(8,128)S(1)} all-to-all(f32[8,40,128]{2,1,0:T(8,128)S(1)} %sum.1), channel_id=1, replica_groups={{0,1,2,3,4,5,6,7},{8,9,10,11,12,13,14,15},{16,17,18,19,20,21,22,23},{24..., dimensions={0} | all-to-all | bytes 327680 | tf_op jit(solution)/shard_map/all_to_all | solution.py:390
  64.1 10.3 %all_to_all.17 = f32[16,32,128]{2,1,0:T(8,128)S(1)} all-to-all(f32[16,32,128]{2,1,0:T(8,128)S(1)} %get-tuple-element.51), channel_id=1, replica_groups={{0,32,64,96,8,40,72,104,128,160,192,224,136,168,200,232},{1,33,65,97,9,..., dimensions={0} | all-to-all | bytes 524288 | tf_op jit(solution)/shard_map/all_to_all | solution.py:401
  74.3 4.6 %collective-permute-start.9 = (f32[512,128]{1,0:T(8,128)S(1)}, f32[512,128]{1,0:T(8,128)S(1)}, u32[]{:S(2)}, u32[]{:S(2)}) collective-permute-start(f32[512,128]{1,0:T(8,128)S(1)} %bitcast.9), channel_id=1, source_target_pairs={{0,16},{1,17},{2,18},{3,19},{4,20},{5,21},{6,22},{7,23},{8,24},{9,... | collective-permute-start | bytes 786440 | tf_op jit(solution)/shard_map/ppermute | solution.py:402
  78.9 1.2 %collective-permute-done.9.other_ref = f32[512,128]{1,0:T(8,128)S(1)} collective-permute-done((f32[512,128]{1,0:T(8,128)S(1)}, f32[512,128]{1,0:T(8,128)S(1)}, u32[]{:S(2)}, u32[]{:S(2)}) %collective-permute-start.9) | collective-permute-done | bytes 262176 | tf_op jit(solution)/shard_map/ppermute | solution.py:402
  80.1 1.4 %last.1 = (f32[5,128,128]{2,1,0:T(8,128)}, f32[384,128]{1,0:T(8,128)}, f32[1,1]{1,0:T(1,128)}) custom-call(s32[8]{0:T(128)S(1)} %compare_select_fusion.6.refs_1_.own_ref, f32[512,128]{1,0:T(8,128)S(1)} %bitcast.10, f32[512,128]{1,0:T(8,128)S(1)} %collective-permute-done.9.other_ref, f32[8,128]{1,0:T(8,128)S(1)} %get-tuple-element.52.losses_ref), custom_call_target="tpu_custom_call" | custom-call | tf_op jit(solution)/shard_map/last/pallas_call | solution.py:403
  (6 shorter events, 0.1 us)
Async XLA Ops:
  0.6 11.7 %copy-start = (bf16[1,256,128]{2,1,0:T(8,128)(2,1)S(1)}, bf16[1,256,128]{2,1,0:T(8,128)(2,1)}, u32[]{:S(2)}) copy-start(bf16[1,256,128]{2,1,0:T(8,128)(2,1)} %param.7) | copy-start | bytes 196612
  0.6 10.1 %collective-permute-start = (bf16[256,128]{1,0:T(8,128)(2,1)}, bf16[256,128]{1,0:T(8,128)(2,1)S(1)}, u32[]{:S(2)}, u32[]{:S(2)}) collective-permute-start(bf16[256,128]{1,0:T(8,128)(2,1)} %bitcast.11), channel_id=1, source_target_pairs={{0,7},{1,0},{2,1},{3,2},{4,3},{5,4},{6,5},{7,6},{8,15},{9,8},{10,9... | collective-permute-start | bytes 196616 | tf_op jit(solution)/shard_map/ppermute | solution.py:291
  7.1 5.2 %collective-permute-start.1 = (bf16[256,128]{1,0:T(8,128)(2,1)}, bf16[256,128]{1,0:T(8,128)(2,1)S(1)}, u32[]{:S(2)}, u32[]{:S(2)}) collective-permute-start(bf16[256,128]{1,0:T(8,128)(2,1)} %bitcast.12), channel_id=1, source_target_pairs={{0,1},{1,2},{2,3},{3,4},{4,5},{5,6},{6,7},{7,0},{8,9},{9,10},{10,1... | collective-permute-start | bytes 196616 | tf_op jit(solution)/shard_map/ppermute | solution.py:291
  7.1 7.7 %collective-permute-start.2 = (bf16[256,128]{1,0:T(8,128)(2,1)}, bf16[256,128]{1,0:T(8,128)(2,1)S(1)}, u32[]{:S(2)}, u32[]{:S(2)}) collective-permute-start(bf16[256,128]{1,0:T(8,128)(2,1)} %bitcast.13), channel_id=1, source_target_pairs={{0,4},{1,5},{2,6},{3,7},{4,0},{5,1},{6,2},{7,3},{8,12},{9,13},{10,... | collective-permute-start | bytes 196616 | tf_op jit(solution)/shard_map/ppermute | solution.py:291
  12.3 5.3 %copy-start.4 = (f32[5,128,128]{2,1,0:T(8,128)S(1)}, f32[5,128,128]{2,1,0:T(8,128)}, u32[]{:S(2)}) copy-start(f32[5,128,128]{2,1,0:T(8,128)} %wq_ref.1) | copy-start | bytes 983044
  12.3 5.3 %copy-start.3 = (bf16[1,256,5,128]{3,1,2,0:T(8,128)(2,1)S(1)}, bf16[1,256,5,128]{3,1,2,0:T(8,128)(2,1)}, u32[]{:S(2)}) copy-start(bf16[1,256,5,128]{3,1,2,0:T(8,128)(2,1)} %param.6) | copy-start | bytes 983044
  12.3 8.8 %collective-permute-start.3 = (bf16[512,128]{1,0:T(8,128)(2,1)S(1)}, bf16[512,128]{1,0:T(8,128)(2,1)S(1)}, u32[]{:S(2)}, u32[]{:S(2)}) collective-permute-start(bf16[512,128]{1,0:T(8,128)(2,1)S(1)} %get-tuple-element.57), channel_id=1, source_target_pairs={{0,6},{1,7},{2,0},{3,1},{4,2},{5,3},{6,4},{7,5},{8,14},{9,15},{10,... | collective-permute-start | bytes 393224 | tf_op jit(solution)/shard_map/ppermute | solution.py:291
  12.4 10.4 %collective-permute-start.4 = (bf16[512,128]{1,0:T(8,128)(2,1)S(1)}, bf16[512,128]{1,0:T(8,128)(2,1)S(1)}, u32[]{:S(2)}, u32[]{:S(2)}) collective-permute-start(bf16[512,128]{1,0:T(8,128)(2,1)S(1)} %get-tuple-element.56), channel_id=1, source_target_pairs={{0,2},{1,3},{2,4},{3,5},{4,6},{5,7},{6,0},{7,1},{8,10},{9,11},{10,... | collective-permute-start | bytes 393224 | tf_op jit(solution)/shard_map/ppermute | solution.py:291
  14.8 11.5 %collective-permute-start.5 = (bf16[1024,128]{1,0:T(8,128)(2,1)S(1)}, bf16[1024,128]{1,0:T(8,128)(2,1)S(1)}, u32[]{:S(2)}, u32[]{:S(2)}) collective-permute-start(bf16[1024,128]{1,0:T(8,128)(2,1)S(1)} %pad_maximum_fusion.refs_5_), channel_id=1, source_target_pairs={{0,8},{1,9},{2,10},{3,11},{4,12},{5,13},{6,14},{7,15},{8,0},{9,1},... | collective-permute-start | bytes 786440 | tf_op jit(solution)/shard_map/ppermute | solution.py:294
  18.3 0.7 copy-start.2
  21.1 7.3 %collective-permute-start.6 = (bf16[512,128]{1,0:T(8,128)(2,1)S(1)}, bf16[512,128]{1,0:T(8,128)(2,1)S(1)}, u32[]{:S(2)}, u32[]{:S(2)}) collective-permute-start(bf16[512,128]{1,0:T(8,128)(2,1)S(1)} %collective-permute-done.3.refs_5_), channel_id=1, source_target_pairs={{0,8},{1,9},{2,10},{3,11},{4,12},{5,13},{6,14},{7,15},{8,0},{9,1},... | collective-permute-start | bytes 393224 | tf_op jit(solution)/shard_map/ppermute | solution.py:294
  22.8 6.2 %collective-permute-start.7 = (bf16[512,128]{1,0:T(8,128)(2,1)S(1)}, bf16[512,128]{1,0:T(8,128)(2,1)S(1)}, u32[]{:S(2)}, u32[]{:S(2)}) collective-permute-start(bf16[512,128]{1,0:T(8,128)(2,1)S(1)} %collective-permute-done.4.refs_6_), channel_id=1, source_target_pairs={{0,8},{1,9},{2,10},{3,11},{4,12},{5,13},{6,14},{7,15},{8,0},{9,1},... | collective-permute-start | bytes 393224 | tf_op jit(solution)/shard_map/ppermute | solution.py:294
  26.3 2.7 %copy-start.1 = (f32[384,128]{1,0:T(8,128)S(1)}, f32[384,128]{1,0:T(8,128)}, u32[]{:S(2)}) copy-start(f32[384,128]{1,0:T(8,128)} %refs_8_.1) | copy-start | bytes 589828
  32.6 4.9 %collective-permute-start.8 = (f32[520,128]{1,0:T(8,128)S(1)}, f32[520,128]{1,0:T(8,128)S(1)}, u32[]{:S(2)}, u32[]{:S(2)}) collective-permute-start(f32[520,128]{1,0:T(8,128)S(1)} %get-tuple-element.50.give_ref), channel_id=1, source_target_pairs={{0,16},{1,17},{2,18},{3,19},{4,20},{5,21},{6,22},{7,23},{8,24},{9,... | collective-permute-start | bytes 798728 | tf_op jit(solution)/shard_map/ppermute | solution.py:384
  74.3 5.7 %collective-permute-start.9 = (f32[512,128]{1,0:T(8,128)S(1)}, f32[512,128]{1,0:T(8,128)S(1)}, u32[]{:S(2)}, u32[]{:S(2)}) collective-permute-start(f32[512,128]{1,0:T(8,128)S(1)} %bitcast.9), channel_id=1, source_target_pairs={{0,16},{1,17},{2,18},{3,19},{4,20},{5,21},{6,22},{7,23},{8,24},{9,... | collective-permute-start | bytes 786440 | tf_op jit(solution)/shard_map/ppermute | solution.py:402

commit v4 on v3

--- a/solution.py
+++ b/solution.py
@@ -12,7 +12,6 @@
 LOW = -1e30
 HIGHEST = lax.Precision.HIGHEST
 VMEM = pl.BlockSpec(memory_space=pltpu.VMEM)
-SMEM = pl.BlockSpec(memory_space=pltpu.SMEM)
 ANY = pl.BlockSpec(memory_space=pl.ANY)
 PARAMS = pltpu.CompilerParams(vmem_limit_bytes=40 * 1024 * 1024)
 SUB = 8
@@ -36,8 +35,13 @@
     return dot(a_high, b_high, dims) + (dot(a_high, b_low, dims) + dot(a_low, b_high, dims))
 
 
-def local_kernel(scale, q_ref, k_ref, wq_ref, *refs):
-    diag_ref, top_ref, tot_ref, pooled_ref, gate_q_ref, q2_ref = refs[-6:]
+def pick(values, index):
+    lane = lax.broadcasted_iota(jnp.int32, (index.shape[0], values.shape[1]), 1)
+    return jnp.sum(jnp.where(lane == index, values, 0.0), axis=1, keepdims=True)
+
+
+def local_kernel(scale, near, q_ref, k_ref, wq_ref, order_ref, *refs):
+    diag_ref, top_ref, tot_ref, pooled_ref, gate_q_ref, q2_ref, seen_ref, visible_ref = refs[-8:]
     heads, rows, width = q_ref.shape
     half = rows // 2
     blocks = rows // POOL
@@ -67,34 +71,43 @@
             diag_ref[part * per : (part + 1) * per, lanes] = block_top
             top_ref[:, lanes] = top
             tot_ref[:, lanes] = jnp.sum(p.reshape(half // SUB, SUB, half), axis=0)
-
-
-def attend(order_ref, own_ref, q2_ref, chunks, top_in, tot_in, top_ref, tot_ref, map_ref, pool_ref):
+    place = lax.axis_index("ctx")
+    along = lax.rem(place, near)
+    base = place - along
+    group = near * blocks
+    order = order_ref[...].astype(jnp.float32)
+    kb = lax.broadcasted_iota(jnp.int32, (2 * group, 1), 0)
+    key_half = pick(order, kb // per)
+    lane = lax.broadcasted_iota(jnp.int32, (2 * group, rows), 1)
+    halves = [pick(order, jnp.full((1, 1), 2 * place + part, jnp.int32)) for part in range(2)]
+    seen = jnp.where(key_half < jnp.where(lane < half, halves[0], halves[1]), 1.0, 0.0)
+    shift = (near - along) * blocks
+    low, high = [pltpu.roll(seen[j * group : (j + 1) * group], shift, 0) for j in range(2)]
+    seen_ref[0:group, :] = jnp.where(base == 0, low, high)
+    seen_ref[group:, :] = jnp.where(base == 0, high, low)
+    key_pos = key_half * per + (kb % per).astype(jnp.float32)
+    diagonal = lax.broadcasted_iota(jnp.int32, (2 * group, 2 * group), 1) == kb
+    key_pos = jnp.sum(jnp.where(diagonal, key_pos, 0.0), axis=0, keepdims=True)
+    row = lax.broadcasted_iota(jnp.int32, (heads * SUB, 1), 0) % SUB
+    query_pos = jnp.where(row < per, halves[0], halves[1]) * per + (row % per).astype(jnp.float32)
+    visible_ref[...] = jnp.where((key_pos <= query_pos) & (row < blocks), 1.0, 0.0)
+
+
+def attend(q2_ref, seen_ref, chunks, top_in, tot_in, top_ref, tot_ref, map_ref, pool_ref):
     heads, rows, _ = q2_ref.shape
-    half = rows // 2
-    per = half // POOL
     blocks = rows // POOL
-    place, along, near = own_ref[0], own_ref[1], own_ref[3]
     tops = [top_in[:, h * rows : (h + 1) * rows] for h in range(heads)]
     tots = [tot_in[:, h * rows : (h + 1) * rows] for h in range(heads)]
     row = 0
     for first in range(0, len(chunks), 2):
         group = chunks[first : first + 2]
-        keys = jnp.concatenate([read() for read, _, _ in group], axis=0)
+        keys = jnp.concatenate([read() for read, _ in group], axis=0)
         count = len(group) * blocks
         x = keys.astype(jnp.float32).reshape(count, POOL, keys.shape[1])
         pool_ref[row : row + count, :] = jnp.concatenate(
             [jnp.max(x, axis=1), jnp.min(x, axis=1), jnp.sum(x, axis=1) * (1.0 / POOL)], axis=1
         )
-        kb_row = lax.broadcasted_iota(jnp.int32, (count, rows), 0)
-        lane = lax.broadcasted_iota(jnp.int32, (count, rows), 1)
-        query_half = jnp.where(lane < half, order_ref[0, 2 * place], order_ref[0, 2 * place + 1])
-        key_half = jnp.zeros((count, rows), jnp.int32)
-        for j, (_, base, offset) in enumerate(group):
-            owner = base + lax.rem(along + offset, near)
-            for part in range(2):
-                key_half = jnp.where(kb_row >= j * blocks + part * per, order_ref[0, 2 * owner + part], key_half)
-        seen = jnp.where(key_half < query_half, 1.0, 0.0)
+        seen = jnp.concatenate([seen_ref[at : at + blocks, :] for _, at in group], axis=0)
         seen_rows = jnp.broadcast_to(seen[:, None, :], (count, SUB, rows)) > 0.5
         seen = seen > 0.5
         keys = jnp.concatenate([keys, keys], axis=1)
@@ -114,26 +127,37 @@
         tot_ref[:, h * rows : (h + 1) * rows] = tots[h]
 
 
-def chunks_of(refs, layout, own_ref, rows):
+def chunks_of(refs, layout, rows, group):
     chunks = []
     for ref, (other, offsets) in zip(refs, layout):
         for j, offset in enumerate(offsets):
             read = functools.partial(lambda r, j: r[j * rows : (j + 1) * rows, :], ref, j)
-            chunks.append((read, own_ref[2 + 2 * other], offset))
+            chunks.append((read, other * group + offset * rows // POOL))
     return chunks
 
 
 def attend_kernel(layout, *refs):
-    order_ref, own_ref, q2_ref, top_in, tot_in = refs[:5]
+    q2_ref, seen_ref, top_in, tot_in = refs[:4]
     top_ref, tot_ref, map_ref, pool_ref = refs[-4:]
-    chunks = chunks_of(refs[5:-4], layout, own_ref, q2_ref.shape[1])
-    attend(order_ref, own_ref, q2_ref, chunks, top_in, tot_in, top_ref, tot_ref, map_ref, pool_ref)
+    chunks = chunks_of(refs[4:-4], layout, q2_ref.shape[1], seen_ref.shape[0] // 2)
+    attend(q2_ref, seen_ref, chunks, top_in, tot_in, top_ref, tot_ref, map_ref, pool_ref)
+
+
+def copy_kernel(in_ref, out_ref):
+    out_ref[...] = in_ref[...]
+
+
+def pair_kernel(own_ref, a_ref, b_ref, ahead_ref, behind_ref):
+    rows = own_ref.shape[0]
+    for out_ref, other_ref in ((ahead_ref, a_ref), (behind_ref, b_ref)):
+        out_ref[0:rows, :] = own_ref[...]
+        out_ref[rows:, :] = other_ref[...]
 
 
 def finish_kernel(layout, places, *refs):
-    order_ref, own_ref, q2_ref, top_in, tot_in, diag_ref, pooled_ref, gate_q_ref, wk_ref, kb_pos_ref = refs[:10]
-    key_refs = refs[10 : 10 + len(layout)]
-    earlier = refs[10 + len(layout) : -12]
+    q2_ref, seen_ref, top_in, tot_in, diag_ref, pooled_ref, gate_q_ref, wk_ref, visible_ref = refs[:9]
+    key_refs = refs[9 : 9 + len(layout)]
+    earlier = refs[9 + len(layout) : -12]
     target_ref, keep_ref, give_ref = refs[-12:-9]
     top_ref, tot_ref, last_map, last_pool, map_ref, rel_pool, pool_ref, block_ref, grad_ref = refs[-9:]
     heads, rows, _ = q2_ref.shape
@@ -143,9 +167,13 @@
     total = map_ref.shape[0]
     near = total // 2
     width = pooled_ref.shape[1]
-    place = own_ref[0]
-    chunks = chunks_of(key_refs, layout, own_ref, rows)
-    attend(order_ref, own_ref, q2_ref, chunks, top_in, tot_in, top_ref, tot_ref, last_map, last_pool)
+    devices = near // blocks
+    place = lax.axis_index("ctx")
+    along = lax.rem(place, devices)
+    bases = (place - along, devices - (place - along))
+    attend(
+        q2_ref, seen_ref, chunks_of(key_refs, layout, rows, near), top_in, tot_in, top_ref, tot_ref, last_map, last_pool
+    )
     maps = list(earlier[0::2]) + [last_map]
     pools = list(earlier[1::2]) + [last_pool]
     for map_in, pool_in, where in zip(maps, pools, places):
@@ -153,9 +181,9 @@
             here = slice(other * near + offset * blocks, other * near + (offset + 1) * blocks)
             map_ref[here, :] = map_in[j * blocks : (j + 1) * blocks, :]
             rel_pool[here, :] = pool_in[j * blocks : (j + 1) * blocks, :]
-    shift = own_ref[1] * blocks
+    shift = along * blocks
     for other in range(2):
-        at = pl.multiple_of(own_ref[2 + 2 * other] * blocks, near)
+        at = pl.multiple_of(bases[other] * blocks, near)
         pool_ref[pl.ds(at, near), :] = pltpu.roll(rel_pool[other * near : (other + 1) * near, :], shift, 0)
     block_ref[...] = jnp.ones(block_ref.shape, jnp.float32)
     for h in range(heads):
@@ -174,7 +202,7 @@
         for j in range(2)
     ]
     lane = lax.broadcasted_iota(jnp.int32, (heads * SUB, total), 1)
-    in_near = (lane >= own_ref[2] * blocks) & (lane < (own_ref[2] + own_ref[3]) * blocks)
+    in_near = (lane >= bases[0] * blocks) & (lane < (bases[0] + devices) * blocks)
     block_map = jnp.where(in_near, group[0], group[1])
     target = block_map / jnp.sum(block_map, axis=1, keepdims=True)
     for h in range(heads):
@@ -183,8 +211,7 @@
     gate_k = dot(pool_ref[...], wk_ref[...], NN, HIGHEST)
     gate_width = gate_k.shape[1]
     row = lax.broadcasted_iota(jnp.int32, (heads * SUB, total), 0) % SUB
-    query_half = jnp.where(row < per, order_ref[0, 2 * place], order_ref[0, 2 * place + 1])
-    visible = (kb_pos_ref[...] <= query_half * per + row % per) & (row < blocks)
+    visible = visible_ref[...] > 0.5
     logits = dot(gate_q, gate_k, NT, HIGHEST) * gate_width ** (-0.5)
     peak = jnp.max(jnp.where(visible, logits, LOW), axis=1, keepdims=True)
     weights = jnp.where(visible, jnp.exp(logits - peak), 0.0)
@@ -199,10 +226,12 @@
         grad_ref[h * width : (h + 1) * width, :] = dot_split(pooled_ref[here, :], gate_q_grad[here], TN)
     grad_ref[heads * width :, :] = dot_split(pool_ref[...], dot_split(d_logits, gate_q, TN), TN)
     part = keep_ref.shape[0]
-    keep_ref[...] = grad_ref[pl.ds(pl.multiple_of(own_ref[5] * part, part), part), :]
-    give_ref[0:part, :] = grad_ref[pl.ds(pl.multiple_of((1 - own_ref[5]) * part, part), part), :]
+    own_seq = lax.axis_index("seq")
+    core = lax.rem(own_seq, 2)
+    keep_ref[...] = grad_ref[pl.ds(pl.multiple_of(core * part, part), part), :]
+    give_ref[0:part, :] = grad_ref[pl.ds(pl.multiple_of((1 - core) * part, part), part), :]
     lane = lax.broadcasted_iota(jnp.int32, (SUB, gate_width), 1)
-    give_ref[part:, :] = jnp.where(lane == own_ref[6], loss, 0.0)
+    give_ref[part:, :] = jnp.where(lane == own_seq, loss, 0.0)
 
 
 def fold_kernel(keep_ref, give_ref, got_ref, out_ref):
@@ -228,34 +257,51 @@
     loss_ref[...] = total[rows:]
 
 
-def last_kernel(own_ref, mine_ref, other_ref, losses_ref, grad_q_ref, grad_k_ref, loss_ref):
-    heads, width, _ = grad_q_ref.shape
-    part = mine_ref.shape[0]
-    whole = part // width
-    first = own_ref[5] == 0
-    for h in range(2 * whole):
-        here = slice(h % whole * width, (h % whole + 1) * width)
-        mine = first if h < whole else jnp.logical_not(first)
-        tile = jnp.where(mine, mine_ref[here, :], other_ref[here, :])
-        if h < heads:
-            grad_q_ref[h] = tile
-        else:
-            grad_k_ref[(h - heads) * width : (h - heads + 1) * width, :] = tile
+def last_kernel(mine_ref, other_ref, losses_ref, grad_q_ref, grad_k_ref, loss_ref, sems):
+    tiles = mine_ref.shape[0]
+    left = grad_q_ref.shape[0] - tiles
+    own_seq = lax.axis_index("seq")
+    core = lax.rem(own_seq, 2)
+
+    def write(low_ref, high_ref):
+        copies = [
+            pltpu.make_async_copy(source, target, sems.at[j])
+            for j, (source, target) in enumerate(
+                (
+                    (low_ref, grad_q_ref.at[pl.ds(0, tiles)]),
+                    (high_ref.at[pl.ds(0, left)], grad_q_ref.at[pl.ds(tiles, left)]),
+                    (high_ref.at[pl.ds(left, tiles - left)], grad_k_ref),
+                )
+            )
+        ]
+        for copy in copies:
+            copy.start()
+        for copy in copies:
+            copy.wait()
+
+    @pl.when(core == 0)
+    def _():
+        write(mine_ref, other_ref)
+
+    @pl.when(core != 0)
+    def _():
+        write(other_ref, mine_ref)
+
     losses = losses_ref[0:1, :]
     lane = lax.broadcasted_iota(jnp.int32, losses.shape, 1)
-    loss_ref[...] = jnp.sum(jnp.where(lane == own_ref[6], losses, 0.0), axis=1, keepdims=True)
+    loss_ref[...] = jnp.sum(jnp.where(lane == own_seq, losses, 0.0), axis=1, keepdims=True)
 
 
 def f32(*shape):
     return jax.ShapeDtypeStruct(shape, jnp.float32)
 
 
-def call(kernel, out_shape, specs, name, scratch=(), cost=None):
+def call(kernel, out_shape, specs, name, scratch=(), cost=None, out_specs=None):
     return pl.pallas_call(
         kernel,
         out_shape=out_shape,
         in_specs=specs,
-        out_specs=tuple(VMEM for _ in out_shape),
+        out_specs=out_specs or tuple(VMEM for _ in out_shape),
         scratch_shapes=scratch,
         compiler_params=PARAMS,
         cost_estimate=cost,
@@ -268,7 +314,6 @@
     heads = queries.shape[2]
     width = queries.shape[3]
     gate_width = w_key_gate.shape[1]
-    per_half = tok_rows // 2 // POOL
     blocks = tok_rows // POOL
     ctx_count = lax.axis_size("ctx")
     seq_count = lax.axis_size("seq")
@@ -277,16 +322,6 @@
     scale = width ** (-0.5) * math.log2(math.e)
     columns = heads * tok_rows
 
-    place = lax.axis_index("ctx")
-    own_seq = lax.axis_index("seq")
-    along = lax.rem(place, near)
-    base = place - along
-    index = jnp.arange(8, dtype=jnp.int32)
-    own = jnp.zeros((8,), jnp.int32)
-    for j, value in enumerate((place, along, base, near, near - base, lax.rem(own_seq, 2), own_seq)):
-        own = jnp.where(index == j, value, own)
-    kb_pos = (order.reshape(-1, 1) * per_half + jnp.arange(per_half, dtype=jnp.int32)[None]).reshape(1, total)
-
     def get(x, offset):
         return lax.ppermute(x, "ctx", [(j, j // near * near + (j - offset) % near) for j in range(ctx_count)])
 
@@ -295,9 +330,18 @@
 
     own_keys = keys[0]
     step = {offset: get(own_keys, offset % near) for offset in (1, -1, near // 2)}
-    ahead = get(jnp.concatenate([own_keys, step[1]], axis=0), 2)
-    behind = get(jnp.concatenate([own_keys, step[-1]], axis=0), near - 2)
-    mid = jnp.concatenate([own_keys, step[1], step[-1], step[near // 2]], axis=0)
+    (own_copy,) = call(
+        copy_kernel,
+        (jax.ShapeDtypeStruct(own_keys.shape, keys.dtype),),
+        [VMEM],
+        "copy",
+        cost=pl.CostEstimate(flops=10**9, bytes_accessed=10**6, transcendentals=10**6),
+    )(own_keys)
+    two_parts = jax.ShapeDtypeStruct((2 * tok_rows, width), keys.dtype)
+    ahead, behind = call(pair_kernel, (two_parts, two_parts), [VMEM] * 3, "pair")(own_copy, step[1], step[-1])
+    ahead = get(ahead, 2)
+    behind = get(behind, near - 2)
+    mid = jnp.concatenate([own_copy, step[1], step[-1], step[near // 2]], axis=0)
     mid_far = across(mid)
     mid_from = (0, 1, near - 1, near // 2)
     ahead_from = (2, 3)
@@ -305,41 +349,44 @@
 
     q = jnp.transpose(queries[0], (1, 0, 2))
     state = (f32(1, columns), f32(SUB, columns))
-    diag, top, tot, pooled, gate_q, q2 = call(
-        functools.partial(local_kernel, scale),
+    diag, top, tot, pooled, gate_q, q2, seen, visible = call(
+        functools.partial(local_kernel, scale, near),
         (f32(SUB, columns),)
         + state
         + (
             f32(heads * SUB, width),
             f32(heads * SUB, gate_width),
             jax.ShapeDtypeStruct((heads, tok_rows, 2 * width), jnp.bfloat16),
+            f32(total, tok_rows),
+            f32(heads * SUB, total),
         ),
-        [VMEM] * 3 + [ANY] * 2,
+        [VMEM] * 4 + [ANY] * 2,
         "local",
         cost=pl.CostEstimate(flops=4 * 10**8, bytes_accessed=10**6, transcendentals=10**5),
-    )(q, own_keys, w_query_gate, step[1], step[-1])
+    )(q, own_copy, w_query_gate, order, step[1], step[-1])
 
     def attend_to(layout, top, tot, *keys):
         count = sum(len(offsets) for _, offsets in layout)
         return call(
             functools.partial(attend_kernel, layout),
             state + (f32(count * blocks, columns), f32(count * blocks, 3 * width)),
-            [SMEM, SMEM] + [VMEM] * (3 + len(keys)),
+            [VMEM] * (4 + len(keys)),
             "attend",
             cost=pl.CostEstimate(flops=1200000000, bytes_accessed=10**6, transcendentals=1300000),
-        )(order, own, q2, top, tot, *keys)
+        )(q2, seen, top, tot, *keys)
 
     layouts = (
         ((0, mid_from),),
         ((0, ahead_from), (0, behind_from)),
         ((1, mid_from),),
-        ((1, ahead_from), (1, behind_from)),
+        ((1, ahead_from),),
+        ((1, behind_from),),
     )
     places = [[(other, offset) for other, offsets in layout for offset in offsets] for layout in layouts]
     ahead_far = across(ahead)
     behind_far = across(behind)
     earlier = []
-    for layout, key_parts in zip(layouts[:-1], ((mid,), (ahead, behind), (mid_far,))):
+    for layout, key_parts in zip(layouts[:-1], ((mid,), (ahead, behind), (mid_far,), (ahead_far,))):
         top, tot, *found = attend_to(layout, top, tot, *key_parts)
         earlier += found
 
@@ -349,7 +396,7 @@
     target, keep, give = call(
         functools.partial(finish_kernel, layouts[-1], places),
         (f32(heads, blocks, total), f32(part, gate_width), f32(part + SUB, gate_width)),
-        [SMEM, SMEM] + [VMEM] * (10 + len(earlier)),
+        [VMEM] * (10 + len(earlier)),
         "finish",
         scratch=[
             pltpu.VMEM(shape, jnp.float32)
@@ -365,7 +412,7 @@
                 (grad_rows, gate_width),
             )
         ],
-    )(order, own, q2, top, tot, diag, pooled, gate_q, w_key_gate, kb_pos, ahead_far, behind_far, *earlier)
+    )(q2, seen, top, tot, diag, pooled, gate_q, w_key_gate, visible, behind_far, *earlier)
 
     every = ("seq", "ctx")
     half_seq = seq_count // 2
@@ -400,13 +447,16 @@
     )(parts)
     mine = lax.all_to_all(spread, every, 0, 0, axis_index_groups=planes, tiled=True).reshape(part, gate_width)
     other = lax.ppermute(mine, every, cores)
+    tiled = (part // width, width, gate_width)
     grad_q, grad_k, loss = call(
         last_kernel,
-        (f32(heads, width, gate_width), f32(3 * width, gate_width), f32(1, 1)),
-        [SMEM, VMEM, VMEM, VMEM],
+        (f32(heads, width, gate_width), f32(3, width, gate_width), f32(1, 1)),
+        [VMEM] * 3,
         "last",
-    )(own, mine, other, losses)
-    return (target[None, None], grad_q, grad_k, loss.reshape(1))
+        scratch=[pltpu.SemaphoreType.DMA((3,))],
+        out_specs=(ANY, ANY, VMEM),
+    )(mine.reshape(tiled), other.reshape(tiled), losses)
+    return (target[None, None], grad_q, grad_k.reshape(3 * width, gate_width), loss.reshape(1))
 
 
 def solution(mesh):

time: 81.6 us -> 80.4 us (0.985)
  Pallas kernels: 12 us -> 9.84 us
  waiting for transfers between devices: 4.42 us -> 6 us
    ppermute x3, waiting for transfers between devices: 0.57 us -> 2.01 us  [across(): lax.ppermute(x, 'ctx', [(j, (j + near) % ctx_count) for j in range(ctx_co...]
    pallas_call x1, Pallas kernels: 3.57 us -> 2.19 us  [on_device(): call(functools.partial(finish_kernel, layouts[-1], places), (f32(heads, b...]
    pallas_call x3 -> x4, Pallas kernels: 6.29 us -> 5.44 us  [attend_to(): call(functools.partial(attend_kernel, layout), state + (f32(count * block...]
    pallas_call x2 -> x4, Pallas kernels: 2.06 us -> 2.13 us  [the longest x1 1.4 us: on_device(): call(last_kernel, (f32(heads, width, gate_width), f32(3, width, gate_widt...]
  transfers between devices with their start and end apart: 10 -> 10, of which waited for: 4 -> 6; matrix products, arithmetic and copies ran while one was open for 1% -> 0% of each run, Pallas kernels for 9% -> 8%
where the time goes in v4:
time: 80.4 us; the launch traced here: 80.1 us
  blocking collectives  37.2 us (46%)
  starting transfers between devices  25.2 us (31%)
  Pallas kernels  9.84 us (12%)
  waiting for transfers between devices  6 us (7%)
  between operations  0.9 us (1%)
  local copies, waits for them, and re-layouts  0.89 us (1%)
    all_to_all x1, blocking collectives, on_device(): lax.all_to_all(parts, every, 0, 0, axis_index_groups=planes, tiled=True)  14.5 us
    all_to_all x1, blocking collectives, on_device(): lax.all_to_all(spread, 'ctx', 0, 0, axis_index_groups=[list(range(near)),...  12.5 us
    ppermute x5, starting transfers between devices, get(): lax.ppermute(x, 'ctx', [(j, j // near * near + (j - offset) % near) for j...  11.7 us
    all_to_all x1, blocking collectives, on_device(): lax.all_to_all(spread, every, 0, 0, axis_index_groups=planes, tiled=True)  10.3 us
    ppermute x3, starting transfers between devices, across(): lax.ppermute(x, 'ctx', [(j, (j + near) % ctx_count) for j in range(ctx_co...  5.8 us
    pallas_call x4, Pallas kernels, attend_to(): call(functools.partial(attend_kernel, layout), state + (f32(count * block...  5.44 us
    ppermute x1, starting transfers between devices, on_device(): other = lax.ppermute(mine, every, cores)  4.56 us
    ppermute x1, starting transfers between devices, on_device(): got = lax.ppermute(give, every, cores)  3.15 us
  transfers between devices with their start and end apart: 10, of which 6 were waited for; matrix products, arithmetic and copies ran while one was open for 0% of the time, Pallas kernels for 8%

profile of v4, /device:TPU:1, one launch (start us, length us, event | category | flops | bytes accessed | tf_op | source)
XLA Modules:
  0.0 80.1 jit_solution(4788047666891439127)
XLA Ops:
  0.6 6.5 %collective-permute-start = (bf16[256,128]{1,0:T(8,128)(2,1)}, bf16[256,128]{1,0:T(8,128)(2,1)S(1)}, u32[]{:S(2)}, u32[]{:S(2)}) collective-permute-start(bf16[256,128]{1,0:T(8,128)(2,1)} %bitcast.14), channel_id=1, source_target_pairs={{0,7},{1,0},{2,1},{3,2},{4,3},{5,4},{6,5},{7,6},{8,15},{9,8},{10,9... | collective-permute-start | bytes 196616 | tf_op jit(solution)/shard_map/ppermute | solution.py:326
  7.1 0.0 collective-permute-start.1
  7.1 2.8 %collective-permute-start.2 = (bf16[256,128]{1,0:T(8,128)(2,1)}, bf16[256,128]{1,0:T(8,128)(2,1)S(1)}, u32[]{:S(2)}, u32[]{:S(2)}) collective-permute-start(bf16[256,128]{1,0:T(8,128)(2,1)} %bitcast.16), channel_id=1, source_target_pairs={{0,4},{1,5},{2,6},{3,7},{4,0},{5,1},{6,2},{7,3},{8,12},{9,13},{10,... | collective-permute-start | bytes 196616 | tf_op jit(solution)/shard_map/ppermute | solution.py:326
  9.9 0.0 copy-start.3
  9.9 0.9 %copy-done.3 = bf16[1,256,128]{2,1,0:T(8,128)(2,1)S(1)} copy-done((bf16[1,256,128]{2,1,0:T(8,128)(2,1)S(1)}, bf16[1,256,128]{2,1,0:T(8,128)(2,1)}, u32[]{:S(2)}) %copy-start.3) | copy-done | bytes 65560
  10.8 0.0 copy-start.1
  10.8 0.0 copy-start.2
  10.8 0.0 collective-permute-done.refs_0_.a_ref
  10.8 1.5 %collective-permute-done.1.refs_1_.b_ref = bf16[256,128]{1,0:T(8,128)(2,1)S(1)} collective-permute-done((bf16[256,128]{1,0:T(8,128)(2,1)}, bf16[256,128]{1,0:T(8,128)(2,1)S(1)}, u32[]{:S(2)}, u32[]{:S(2)}) %collective-permute-start.1) | collective-permute-done | bytes 65568 | tf_op jit(solution)/shard_map/ppermute | solution.py:326
  12.3 0.1 collective-permute-start.3
  12.4 2.4 %collective-permute-start.4 = (bf16[512,128]{1,0:T(8,128)(2,1)S(1)}, bf16[512,128]{1,0:T(8,128)(2,1)S(1)}, u32[]{:S(2)}, u32[]{:S(2)}) collective-permute-start(bf16[512,128]{1,0:T(8,128)(2,1)S(1)} %get-tuple-element.45), channel_id=1, source_target_pairs={{0,2},{1,3},{2,4},{3,5},{4,6},{5,7},{6,0},{7,1},{8,10},{9,11},{10,... | collective-permute-start | bytes 393224 | tf_op jit(solution)/shard_map/ppermute | solution.py:326
  14.8 0.0 collective-permute-done.2
  14.8 0.0 copy-start.4
  14.8 2.8 %collective-permute-start.5 = (bf16[1024,128]{1,0:T(8,128)(2,1)S(1)}, bf16[1024,128]{1,0:T(8,128)(2,1)S(1)}, u32[]{:S(2)}, u32[]{:S(2)}) collective-permute-start(bf16[1024,128]{1,0:T(8,128)(2,1)S(1)} %pad_maximum_fusion.refs_4_), channel_id=1, source_target_pairs={{0,8},{1,9},{2,10},{3,11},{4,12},{5,13},{6,14},{7,15},{8,0},{9,1},... | collective-permute-start | bytes 786440 | tf_op jit(solution)/shard_map/ppermute | solution.py:329
  17.6 0.0 copy-done.1
  17.6 0.0 copy-done.2
  17.6 0.0 copy-done.4
  17.6 0.7 local.1
  18.3 1.5 %attend.4 = (f32[1,1280]{1,0:T(1,128)S(1)}, f32[8,1280]{1,0:T(8,128)S(1)}, f32[16,1280]{1,0:T(8,128)S(1)}, f32[16,384]{1,0:T(8,128)S(1)}) custom-call(bf16[5,256,256]{2,1,0:T(8,128)(2,1)S(1)} %get-tuple-element.38.refs_0_, f32[64,256]{1,0:T(8,128)S(1)} %get-tuple-element.39.refs_1_, f32[1,1280]{1,0:T(1,128)S(1)} %get-tuple-element.40.refs_2_, ...), custom_call_target="tpu_custom_call" | custom-call | flops 1200000000 | bytes 1000000 | tf_op jit(solution)/shard_map/attend/pallas_call | solution.py:370
  19.9 0.2 collective-permute-done.3.refs_4_
  20.1 2.7 %collective-permute-start.6 = (bf16[512,128]{1,0:T(8,128)(2,1)S(1)}, bf16[512,128]{1,0:T(8,128)(2,1)S(1)}, u32[]{:S(2)}, u32[]{:S(2)}) collective-permute-start(bf16[512,128]{1,0:T(8,128)(2,1)S(1)} %collective-permute-done.3.refs_4_), channel_id=1, source_target_pairs={{0,8},{1,9},{2,10},{3,11},{4,12},{5,13},{6,14},{7,15},{8,0},{9,1},... | collective-permute-start | bytes 393224 | tf_op jit(solution)/shard_map/ppermute | solution.py:329
  22.8 0.0 collective-permute-done.4.refs_5_
  22.8 0.2 collective-permute-start.7
  23.0 1.5 %attend.5 = (f32[1,1280]{1,0:T(1,128)S(1)}, f32[8,1280]{1,0:T(8,128)S(1)}, f32[16,1280]{1,0:T(8,128)S(1)}, f32[16,384]{1,0:T(8,128)S(1)}) custom-call(bf16[5,256,256]{2,1,0:T(8,128)(2,1)S(1)} %get-tuple-element.38.refs_0_, f32[64,256]{1,0:T(8,128)S(1)} %get-tuple-element.39.refs_1_, f32[1,1280]{1,0:T(1,128)S(1)} %get-tuple-element.42.refs_2_, ...), custom_call_target="tpu_custom_call" | custom-call | flops 1200000000 | bytes 1000000 | tf_op jit(solution)/shard_map/attend/pallas_call | solution.py:370
  24.6 0.0 collective-permute-done.5.refs_4_
  24.6 1.5 %attend.6 = (f32[1,1280]{1,0:T(1,128)S(1)}, f32[8,1280]{1,0:T(8,128)S(1)}, f32[16,1280]{1,0:T(8,128)S(1)}, f32[16,384]{1,0:T(8,128)S(1)}) custom-call(bf16[5,256,256]{2,1,0:T(8,128)(2,1)S(1)} %get-tuple-element.38.refs_0_, f32[64,256]{1,0:T(8,128)S(1)} %get-tuple-element.39.refs_1_, f32[1,1280]{1,0:T(1,128)S(1)} %get-tuple-element.46.refs_2_, ...), custom_call_target="tpu_custom_call" | custom-call | flops 1200000000 | bytes 1000000 | tf_op jit(solution)/shard_map/attend/pallas_call | solution.py:370
  26.1 1.0 %collective-permute-done.6.refs_4_ = bf16[512,128]{1,0:T(8,128)(2,1)S(1)} collective-permute-done((bf16[512,128]{1,0:T(8,128)(2,1)S(1)}, bf16[512,128]{1,0:T(8,128)(2,1)S(1)}, u32[]{:S(2)}, u32[]{:S(2)}) %collective-permute-start.6) | collective-permute-done | bytes 131104 | tf_op jit(solution)/shard_map/ppermute | solution.py:329
  27.1 0.0 copy-start
  27.1 0.9 %attend.7 = (f32[1,1280]{1,0:T(1,128)S(1)}, f32[8,1280]{1,0:T(8,128)S(1)}, f32[8,1280]{1,0:T(8,128)S(1)}, f32[8,384]{1,0:T(8,128)S(1)}) custom-call(bf16[5,256,256]{2,1,0:T(8,128)(2,1)S(1)} %get-tuple-element.38.refs_0_, f32[64,256]{1,0:T(8,128)S(1)} %get-tuple-element.39.refs_1_, f32[1,1280]{1,0:T(1,128)S(1)} %get-tuple-element.48.refs_2_, ...), custom_call_target="tpu_custom_call" | custom-call | flops 1200000000 | bytes 1000000 | tf_op jit(solution)/shard_map/attend/pallas_call | solution.py:370
  28.0 1.0 %collective-permute-done.7.refs_9_ = bf16[512,128]{1,0:T(8,128)(2,1)S(1)} collective-permute-done((bf16[512,128]{1,0:T(8,128)(2,1)S(1)}, bf16[512,128]{1,0:T(8,128)(2,1)S(1)}, u32[]{:S(2)}, u32[]{:S(2)}) %collective-permute-start.7) | collective-permute-done | bytes 131104 | tf_op jit(solution)/shard_map/ppermute | solution.py:329
  29.0 0.0 copy-done
  29.0 2.2 %finish.1 = (f32[5,4,64]{2,1,0:T(4,128)}, f32[512,128]{1,0:T(8,128)S(1)}, f32[520,128]{1,0:T(8,128)S(1)}) custom-call(bf16[5,256,256]{2,1,0:T(8,128)(2,1)S(1)} %get-tuple-element.38.refs_0_, f32[64,256]{1,0:T(8,128)S(1)} %get-tuple-element.39.refs_1_, f32[1,1280]{1,0:T(1,128)S(1)} %get-tuple-element.50.refs_2_, f32[8,1280]{1,0:T(8,128)S(1)} %get-tuple-element.51.refs_3_, ...), custom_call_target="tpu_custom_call" | custom-call | tf_op jit(solution)/shard_map/finish/pallas_call | solution.py:396
  31.2 3.2 %collective-permute-start.8 = (f32[520,128]{1,0:T(8,128)S(1)}, f32[520,128]{1,0:T(8,128)S(1)}, u32[]{:S(2)}, u32[]{:S(2)}) collective-permute-start(f32[520,128]{1,0:T(8,128)S(1)} %get-tuple-element.66.give_ref), channel_id=1, source_target_pairs={{0,16},{1,17},{2,18},{3,19},{4,20},{5,21},{6,22},{7,23},{8,24},{9,... | collective-permute-start | bytes 798728 | tf_op jit(solution)/shard_map/ppermute | solution.py:431
  34.3 1.2 %collective-permute-done.8.got_ref = f32[520,128]{1,0:T(8,128)S(1)} collective-permute-done((f32[520,128]{1,0:T(8,128)S(1)}, f32[520,128]{1,0:T(8,128)S(1)}, u32[]{:S(2)}, u32[]{:S(2)}) %collective-permute-start.8) | collective-permute-done | bytes 266272 | tf_op jit(solution)/shard_map/ppermute | solution.py:431
  35.5 14.5 %all_to_all.15.parts_ref = f32[16,40,128]{2,1,0:T(8,128)S(1)} all-to-all(f32[16,40,128]{2,1,0:T(8,128)S(1)} %fold.1), channel_id=1, replica_groups={{0,32,64,96,8,40,72,104,128,160,192,224,136,168,200,232},{1,33,65,97,9,..., dimensions={0} | all-to-all | bytes 655360 | tf_op jit(solution)/shard_map/all_to_all | solution.py:435
  50.0 12.5 %all_to_all.16.parts_ref = f32[8,40,128]{2,1,0:T(8,128)S(1)} all-to-all(f32[8,40,128]{2,1,0:T(8,128)S(1)} %sum.1), channel_id=1, replica_groups={{0,1,2,3,4,5,6,7},{8,9,10,11,12,13,14,15},{16,17,18,19,20,21,22,23},{24..., dimensions={0} | all-to-all | bytes 327680 | tf_op jit(solution)/shard_map/all_to_all | solution.py:437
  62.6 10.3 %all_to_all.17 = f32[16,32,128]{2,1,0:T(8,128)S(1)} all-to-all(f32[16,32,128]{2,1,0:T(8,128)S(1)} %get-tuple-element.67), channel_id=1, replica_groups={{0,32,64,96,8,40,72,104,128,160,192,224,136,168,200,232},{1,33,65,97,9,..., dimensions={0} | all-to-all | bytes 524288 | tf_op jit(solution)/shard_map/all_to_all | solution.py:448
  72.9 4.6 %collective-permute-start.9 = (f32[512,128]{1,0:T(8,128)S(1)}, f32[512,128]{1,0:T(8,128)S(1)}, u32[]{:S(2)}, u32[]{:S(2)}) collective-permute-start(f32[512,128]{1,0:T(8,128)S(1)} %bitcast.10), channel_id=1, source_target_pairs={{0,16},{1,17},{2,18},{3,19},{4,20},{5,21},{6,22},{7,23},{8,24},{9,... | collective-permute-start | bytes 786440 | tf_op jit(solution)/shard_map/ppermute | solution.py:449
  77.4 1.2 %collective-permute-done.9 = f32[512,128]{1,0:T(8,128)S(1)} collective-permute-done((f32[512,128]{1,0:T(8,128)S(1)}, f32[512,128]{1,0:T(8,128)S(1)}, u32[]{:S(2)}, u32[]{:S(2)}) %collective-permute-start.9) | collective-permute-done | bytes 262176 | tf_op jit(solution)/shard_map/ppermute | solution.py:449
  78.6 1.4 %last.1 = (f32[5,128,128]{2,1,0:T(8,128)}, f32[3,128,128]{2,1,0:T(8,128)}, f32[1,1]{1,0:T(1,128)}) custom-call(f32[4,128,128]{2,1,0:T(8,128)S(1)} %bitcast.11, f32[4,128,128]{2,1,0:T(8,128)S(1)} %bitcast.12, f32[8,128]{1,0:T(8,128)S(1)} %get-tuple-element.68.losses_ref), custom_call_target="tpu_custom_call" | custom-call | tf_op jit(solution)/shard_map/last/pallas_call | solution.py:451
  (6 shorter events, 0.1 us)
Async XLA Ops:
  0.6 10.2 %collective-permute-start = (bf16[256,128]{1,0:T(8,128)(2,1)}, bf16[256,128]{1,0:T(8,128)(2,1)S(1)}, u32[]{:S(2)}, u32[]{:S(2)}) collective-permute-start(bf16[256,128]{1,0:T(8,128)(2,1)} %bitcast.14), channel_id=1, source_target_pairs={{0,7},{1,0},{2,1},{3,2},{4,3},{5,4},{6,5},{7,6},{8,15},{9,8},{10,9... | collective-permute-start | bytes 196616 | tf_op jit(solution)/shard_map/ppermute | solution.py:326
  7.1 5.2 %collective-permute-start.1 = (bf16[256,128]{1,0:T(8,128)(2,1)}, bf16[256,128]{1,0:T(8,128)(2,1)S(1)}, u32[]{:S(2)}, u32[]{:S(2)}) collective-permute-start(bf16[256,128]{1,0:T(8,128)(2,1)} %bitcast.15), channel_id=1, source_target_pairs={{0,1},{1,2},{2,3},{3,4},{4,5},{5,6},{6,7},{7,0},{8,9},{9,10},{10,1... | collective-permute-start | bytes 196616 | tf_op jit(solution)/shard_map/ppermute | solution.py:326
  7.1 7.7 %collective-permute-start.2 = (bf16[256,128]{1,0:T(8,128)(2,1)}, bf16[256,128]{1,0:T(8,128)(2,1)S(1)}, u32[]{:S(2)}, u32[]{:S(2)}) collective-permute-start(bf16[256,128]{1,0:T(8,128)(2,1)} %bitcast.16), channel_id=1, source_target_pairs={{0,4},{1,5},{2,6},{3,7},{4,0},{5,1},{6,2},{7,3},{8,12},{9,13},{10,... | collective-permute-start | bytes 196616 | tf_op jit(solution)/shard_map/ppermute | solution.py:326
  9.9 0.9 %copy-start.3 = (bf16[1,256,128]{2,1,0:T(8,128)(2,1)S(1)}, bf16[1,256,128]{2,1,0:T(8,128)(2,1)}, u32[]{:S(2)}) copy-start(bf16[1,256,128]{2,1,0:T(8,128)(2,1)} %param.7) | copy-start | bytes 196612
  10.8 6.8 %copy-start.1 = (bf16[1,256,5,128]{3,1,2,0:T(8,128)(2,1)S(1)}, bf16[1,256,5,128]{3,1,2,0:T(8,128)(2,1)}, u32[]{:S(2)}) copy-start(bf16[1,256,5,128]{3,1,2,0:T(8,128)(2,1)} %param.6) | copy-start | bytes 983044
  10.8 6.8 %copy-start.2 = (f32[5,128,128]{2,1,0:T(8,128)S(1)}, f32[5,128,128]{2,1,0:T(8,128)}, u32[]{:S(2)}) copy-start(f32[5,128,128]{2,1,0:T(8,128)} %wq_ref.1) | copy-start | bytes 983044
  12.3 7.7 %collective-permute-start.3 = (bf16[512,128]{1,0:T(8,128)(2,1)S(1)}, bf16[512,128]{1,0:T(8,128)(2,1)S(1)}, u32[]{:S(2)}, u32[]{:S(2)}) collective-permute-start(bf16[512,128]{1,0:T(8,128)(2,1)S(1)} %get-tuple-element.44), channel_id=1, source_target_pairs={{0,6},{1,7},{2,0},{3,1},{4,2},{5,3},{6,4},{7,5},{8,14},{9,15},{10,... | collective-permute-start | bytes 393224 | tf_op jit(solution)/shard_map/ppermute | solution.py:326
  12.4 10.4 %collective-permute-start.4 = (bf16[512,128]{1,0:T(8,128)(2,1)S(1)}, bf16[512,128]{1,0:T(8,128)(2,1)S(1)}, u32[]{:S(2)}, u32[]{:S(2)}) collective-permute-start(bf16[512,128]{1,0:T(8,128)(2,1)S(1)} %get-tuple-element.45), channel_id=1, source_target_pairs={{0,2},{1,3},{2,4},{3,5},{4,6},{5,7},{6,0},{7,1},{8,10},{9,11},{10,... | collective-permute-start | bytes 393224 | tf_op jit(solution)/shard_map/ppermute | solution.py:326
  14.8 2.9 %copy-start.4 = (s32[1,32]{1,0:T(1,128)S(1)}, s32[1,32]{1,0:T(1,128)}, u32[]{:S(2)}) copy-start(s32[1,32]{1,0:T(1,128)} %order_ref.1) | copy-start | bytes 388
  14.8 9.8 %collective-permute-start.5 = (bf16[1024,128]{1,0:T(8,128)(2,1)S(1)}, bf16[1024,128]{1,0:T(8,128)(2,1)S(1)}, u32[]{:S(2)}, u32[]{:S(2)}) collective-permute-start(bf16[1024,128]{1,0:T(8,128)(2,1)S(1)} %pad_maximum_fusion.refs_4_), channel_id=1, source_target_pairs={{0,8},{1,9},{2,10},{3,11},{4,12},{5,13},{6,14},{7,15},{8,0},{9,1},... | collective-permute-start | bytes 786440 | tf_op jit(solution)/shard_map/ppermute | solution.py:329
  20.1 7.1 %collective-permute-start.6 = (bf16[512,128]{1,0:T(8,128)(2,1)S(1)}, bf16[512,128]{1,0:T(8,128)(2,1)S(1)}, u32[]{:S(2)}, u32[]{:S(2)}) collective-permute-start(bf16[512,128]{1,0:T(8,128)(2,1)S(1)} %collective-permute-done.3.refs_4_), channel_id=1, source_target_pairs={{0,8},{1,9},{2,10},{3,11},{4,12},{5,13},{6,14},{7,15},{8,0},{9,1},... | collective-permute-start | bytes 393224 | tf_op jit(solution)/shard_map/ppermute | solution.py:329
  22.8 6.2 %collective-permute-start.7 = (bf16[512,128]{1,0:T(8,128)(2,1)S(1)}, bf16[512,128]{1,0:T(8,128)(2,1)S(1)}, u32[]{:S(2)}, u32[]{:S(2)}) collective-permute-start(bf16[512,128]{1,0:T(8,128)(2,1)S(1)} %collective-permute-done.4.refs_5_), channel_id=1, source_target_pairs={{0,8},{1,9},{2,10},{3,11},{4,12},{5,13},{6,14},{7,15},{8,0},{9,1},... | collective-permute-start | bytes 393224 | tf_op jit(solution)/shard_map/ppermute | solution.py:329
  27.1 1.9 %copy-start = (f32[384,128]{1,0:T(8,128)S(1)}, f32[384,128]{1,0:T(8,128)}, u32[]{:S(2)}) copy-start(f32[384,128]{1,0:T(8,128)} %refs_7_.1) | copy-start | bytes 589828
  31.2 4.3 %collective-permute-start.8 = (f32[520,128]{1,0:T(8,128)S(1)}, f32[520,128]{1,0:T(8,128)S(1)}, u32[]{:S(2)}, u32[]{:S(2)}) collective-permute-start(f32[520,128]{1,0:T(8,128)S(1)} %get-tuple-element.66.give_ref), channel_id=1, source_target_pairs={{0,16},{1,17},{2,18},{3,19},{4,20},{5,21},{6,22},{7,23},{8,24},{9,... | collective-permute-start | bytes 798728 | tf_op jit(solution)/shard_map/ppermute | solution.py:431
  72.9 5.7 %collective-permute-start.9 = (f32[512,128]{1,0:T(8,128)S(1)}, f32[512,128]{1,0:T(8,128)S(1)}, u32[]{:S(2)}, u32[]{:S(2)}) collective-permute-start(f32[512,128]{1,0:T(8,128)S(1)} %bitcast.10), channel_id=1, source_target_pairs={{0,16},{1,17},{2,18},{3,19},{4,20},{5,21},{6,22},{7,23},{8,24},{9,... | collective-permute-start | bytes 786440 | tf_op jit(solution)/shard_map/ppermute | solution.py:449

commit v5 on v4

--- a/solution.py
+++ b/solution.py
@@ -257,39 +257,43 @@
     loss_ref[...] = total[rows:]
 
 
-def last_kernel(mine_ref, other_ref, losses_ref, grad_q_ref, grad_k_ref, loss_ref, sems):
+def last_kernel(
+    mine_ref, other_ref, losses_ref, target_in, grad_q_ref, grad_k_ref, loss_ref, target_ref, loss_row, sems
+):
     tiles = mine_ref.shape[0]
     left = grad_q_ref.shape[0] - tiles
     own_seq = lax.axis_index("seq")
     core = lax.rem(own_seq, 2)
 
-    def write(low_ref, high_ref):
-        copies = [
-            pltpu.make_async_copy(source, target, sems.at[j])
-            for j, (source, target) in enumerate(
-                (
-                    (low_ref, grad_q_ref.at[pl.ds(0, tiles)]),
-                    (high_ref.at[pl.ds(0, left)], grad_q_ref.at[pl.ds(tiles, left)]),
-                    (high_ref.at[pl.ds(left, tiles - left)], grad_k_ref),
-                )
-            )
-        ]
-        for copy in copies:
-            copy.start()
-        for copy in copies:
-            copy.wait()
+    def grads(low_ref, high_ref):
+        pairs = (
+            (low_ref, grad_q_ref.at[pl.ds(0, tiles)]),
+            (high_ref.at[pl.ds(0, left)], grad_q_ref.at[pl.ds(tiles, left)]),
+            (high_ref.at[pl.ds(left, tiles - left)], grad_k_ref),
+        )
+        return [pltpu.make_async_copy(source, target, sems.at[j]) for j, (source, target) in enumerate(pairs)]
 
     @pl.when(core == 0)
     def _():
-        write(mine_ref, other_ref)
+        for copy in grads(mine_ref, other_ref):
+            copy.start()
 
     @pl.when(core != 0)
     def _():
-        write(other_ref, mine_ref)
+        for copy in grads(other_ref, mine_ref):
+            copy.start()
 
     losses = losses_ref[0:1, :]
     lane = lax.broadcasted_iota(jnp.int32, losses.shape, 1)
-    loss_ref[...] = jnp.sum(jnp.where(lane == own_seq, losses, 0.0), axis=1, keepdims=True)
+    loss_row[...] = jnp.sum(jnp.where(lane == own_seq, losses, 0.0), axis=1, keepdims=True)
+    rest = [
+        pltpu.make_async_copy(loss_row, loss_ref, sems.at[3]),
+        pltpu.make_async_copy(target_in, target_ref, sems.at[4]),
+    ]
+    for copy in rest:
+        copy.start()
+    for copy in grads(mine_ref, other_ref) + rest:
+        copy.wait()
 
 
 def f32(*shape):
@@ -341,9 +345,10 @@
     ahead, behind = call(pair_kernel, (two_parts, two_parts), [VMEM] * 3, "pair")(own_copy, step[1], step[-1])
     ahead = get(ahead, 2)
     behind = get(behind, near - 2)
-    mid = jnp.concatenate([own_copy, step[1], step[-1], step[near // 2]], axis=0)
+    mid = jnp.concatenate([own_copy, step[1], step[-1]], axis=0)
     mid_far = across(mid)
-    mid_from = (0, 1, near - 1, near // 2)
+    mid_from = (0, 1, near - 1)
+    quad_from = (near // 2,)
     ahead_from = (2, 3)
     behind_from = (near - 2, near - 3)
 
@@ -377,16 +382,18 @@
 
     layouts = (
         ((0, mid_from),),
-        ((0, ahead_from), (0, behind_from)),
-        ((1, mid_from),),
+        ((0, ahead_from), (0, behind_from), (0, quad_from)),
+        ((1, mid_from), (1, quad_from)),
         ((1, ahead_from),),
         ((1, behind_from),),
     )
     places = [[(other, offset) for other, offsets in layout for offset in offsets] for layout in layouts]
+    quad = step[near // 2]
+    quad_far = across(quad)
     ahead_far = across(ahead)
     behind_far = across(behind)
     earlier = []
-    for layout, key_parts in zip(layouts[:-1], ((mid,), (ahead, behind), (mid_far,), (ahead_far,))):
+    for layout, key_parts in zip(layouts[:-1], ((mid,), (ahead, behind, quad), (mid_far, quad_far), (ahead_far,))):
         top, tot, *found = attend_to(layout, top, tot, *key_parts)
         earlier += found
 
@@ -448,14 +455,14 @@
     mine = lax.all_to_all(spread, every, 0, 0, axis_index_groups=planes, tiled=True).reshape(part, gate_width)
     other = lax.ppermute(mine, every, cores)
     tiled = (part // width, width, gate_width)
-    grad_q, grad_k, loss = call(
+    grad_q, grad_k, loss, target = call(
         last_kernel,
-        (f32(heads, width, gate_width), f32(3, width, gate_width), f32(1, 1)),
-        [VMEM] * 3,
+        (f32(heads, width, gate_width), f32(3, width, gate_width), f32(1, 1), f32(*target.shape)),
+        [VMEM] * 4,
         "last",
-        scratch=[pltpu.SemaphoreType.DMA((3,))],
-        out_specs=(ANY, ANY, VMEM),
-    )(mine.reshape(tiled), other.reshape(tiled), losses)
+        scratch=[pltpu.VMEM((1, 1), jnp.float32), pltpu.SemaphoreType.DMA((5,))],
+        out_specs=(ANY,) * 4,
+    )(mine.reshape(tiled), other.reshape(tiled), losses, target)
     return (target[None, None], grad_q, grad_k.reshape(3 * width, gate_width), loss.reshape(1))
 
 

time: 80.4 us -> 79.8 us (level)
  starting transfers between devices: 25.2 us -> 27.5 us
  blocking collectives: 37.2 us -> 36 us
  waiting for transfers between devices: 6 us -> 4.84 us
    ppermute x1, starting transfers between devices: 3.15 us -> 5.2 us  [on_device(): got = lax.ppermute(give, every, cores)]
    ppermute x3 -> x4, waiting for transfers between devices: 2.01 us -> 0.8 us  [across(): lax.ppermute(x, 'ctx', [(j, (j + near) % ctx_count) for j in range(ctx_co...]
    all_to_all x1, blocking collectives: 14.5 us -> 13.3 us  [on_device(): lax.all_to_all(parts, every, 0, 0, axis_index_groups=planes, tiled=True)]
    ppermute x3 -> x4, starting transfers between devices: 5.8 us -> 6.03 us  [across(): lax.ppermute(x, 'ctx', [(j, (j + near) % ctx_count) for j in range(ctx_co...]
  transfers between devices with their start and end apart: 10 -> 11, of which waited for: 6 -> 6; matrix products, arithmetic and copies ran while one was open for 0% -> 0% of each run, Pallas kernels for 8% -> 8%
where the time goes in v5:
time: 79.8 us; the launch traced here: 79.6 us
  blocking collectives  36 us (45%)
  starting transfers between devices  27.5 us (34%)
  Pallas kernels  9.46 us (12%)
  waiting for transfers between devices  4.84 us (6%)
  between operations  0.91 us (1%)
  local copies, waits for them, and re-layouts  0.89 us (1%)
    all_to_all x1, blocking collectives, on_device(): lax.all_to_all(parts, every, 0, 0, axis_index_groups=planes, tiled=True)  13.3 us
    all_to_all x1, blocking collectives, on_device(): lax.all_to_all(spread, 'ctx', 0, 0, axis_index_groups=[list(range(near)),...  12.4 us
    ppermute x5, starting transfers between devices, get(): lax.ppermute(x, 'ctx', [(j, j // near * near + (j - offset) % near) for j...  11.7 us
    all_to_all x1, blocking collectives, on_device(): lax.all_to_all(spread, every, 0, 0, axis_index_groups=planes, tiled=True)  10.3 us
    ppermute x4, starting transfers between devices, across(): lax.ppermute(x, 'ctx', [(j, (j + near) % ctx_count) for j in range(ctx_co...  6.03 us
    pallas_call x4, Pallas kernels, attend_to(): call(functools.partial(attend_kernel, layout), state + (f32(count * block...  5.62 us
    ppermute x1, starting transfers between devices, on_device(): got = lax.ppermute(give, every, cores)  5.2 us
    ppermute x1, starting transfers between devices, on_device(): other = lax.ppermute(mine, every, cores)  4.56 us
  transfers between devices with their start and end apart: 11, of which 6 were waited for; matrix products, arithmetic and copies ran while one was open for 0% of the time, Pallas kernels for 8%

profile of v5, /device:TPU:1, one launch (start us, length us, event | category | flops | bytes accessed | tf_op | source)
XLA Modules:
  0.0 79.6 jit_solution(11174182299440761965)
XLA Ops:
  0.6 6.5 %collective-permute-start = (bf16[256,128]{1,0:T(8,128)(2,1)}, bf16[256,128]{1,0:T(8,128)(2,1)S(1)}, u32[]{:S(2)}, u32[]{:S(2)}) collective-permute-start(bf16[256,128]{1,0:T(8,128)(2,1)} %bitcast.14), channel_id=1, source_target_pairs={{0,7},{1,0},{2,1},{3,2},{4,3},{5,4},{6,5},{7,6},{8,15},{9,8},{10,9... | collective-permute-start | bytes 196616 | tf_op jit(solution)/shard_map/ppermute | solution.py:330
  7.1 0.0 collective-permute-start.1
  7.1 2.8 %collective-permute-start.4 = (bf16[256,128]{1,0:T(8,128)(2,1)}, bf16[256,128]{1,0:T(8,128)(2,1)S(1)}, u32[]{:S(2)}, u32[]{:S(2)}) collective-permute-start(bf16[256,128]{1,0:T(8,128)(2,1)} %bitcast.16), channel_id=1, source_target_pairs={{0,4},{1,5},{2,6},{3,7},{4,0},{5,1},{6,2},{7,3},{8,12},{9,13},{10,... | collective-permute-start | bytes 196616 | tf_op jit(solution)/shard_map/ppermute | solution.py:330
  9.9 0.0 copy-start.3
  9.9 0.9 %copy-done.3 = bf16[1,256,128]{2,1,0:T(8,128)(2,1)S(1)} copy-done((bf16[1,256,128]{2,1,0:T(8,128)(2,1)S(1)}, bf16[1,256,128]{2,1,0:T(8,128)(2,1)}, u32[]{:S(2)}) %copy-start.3) | copy-done | bytes 65560
  10.8 0.0 copy-start.2
  10.8 0.0 copy-start.1
  10.8 0.0 collective-permute-done.refs_0_.a_ref
  10.8 1.5 %collective-permute-done.1.refs_1_.b_ref = bf16[256,128]{1,0:T(8,128)(2,1)S(1)} collective-permute-done((bf16[256,128]{1,0:T(8,128)(2,1)}, bf16[256,128]{1,0:T(8,128)(2,1)S(1)}, u32[]{:S(2)}, u32[]{:S(2)}) %collective-permute-start.1) | collective-permute-done | bytes 65568 | tf_op jit(solution)/shard_map/ppermute | solution.py:330
  12.3 0.1 collective-permute-start.2
  12.4 2.4 %collective-permute-start.3 = (bf16[512,128]{1,0:T(8,128)(2,1)S(1)}, bf16[512,128]{1,0:T(8,128)(2,1)S(1)}, u32[]{:S(2)}, u32[]{:S(2)}) collective-permute-start(bf16[512,128]{1,0:T(8,128)(2,1)S(1)} %get-tuple-element.46), channel_id=1, source_target_pairs={{0,2},{1,3},{2,4},{3,5},{4,6},{5,7},{6,0},{7,1},{8,10},{9,11},{10,... | collective-permute-start | bytes 393224 | tf_op jit(solution)/shard_map/ppermute | solution.py:330
  14.8 0.0 copy-start.4
  14.8 2.8 %collective-permute-start.5 = (bf16[768,128]{1,0:T(8,128)(2,1)S(1)}, bf16[768,128]{1,0:T(8,128)(2,1)S(1)}, u32[]{:S(2)}, u32[]{:S(2)}) collective-permute-start(bf16[768,128]{1,0:T(8,128)(2,1)S(1)} %pad_maximum_fusion.refs_4_), channel_id=1, source_target_pairs={{0,8},{1,9},{2,10},{3,11},{4,12},{5,13},{6,14},{7,15},{8,0},{9,1},... | collective-permute-start | bytes 589832 | tf_op jit(solution)/shard_map/ppermute | solution.py:333
  17.6 0.0 collective-permute-done.4.refs_6_
  17.6 0.2 collective-permute-start.6
  17.9 0.0 copy-done.2
  17.9 0.0 copy-done.1
  17.9 0.0 copy-done.4
  17.9 0.7 local.1
  18.6 1.3 %attend.4 = (f32[1,1280]{1,0:T(1,128)S(1)}, f32[8,1280]{1,0:T(8,128)S(1)}, f32[12,1280]{1,0:T(8,128)S(1)}, f32[12,384]{1,0:T(8,128)S(1)}) custom-call(bf16[5,256,256]{2,1,0:T(8,128)(2,1)S(1)} %get-tuple-element.39.refs_0_, f32[64,256]{1,0:T(8,128)S(1)} %get-tuple-element.40.refs_1_, f32[1,1280]{1,0:T(1,128)S(1)} %get-tuple-element.41.refs_2_, ...), custom_call_target="tpu_custom_call" | custom-call | flops 1200000000 | bytes 1000000 | tf_op jit(solution)/shard_map/attend/pallas_call | solution.py:375
  19.8 0.2 collective-permute-done.2.refs_4_
  20.1 2.7 %collective-permute-start.7 = (bf16[512,128]{1,0:T(8,128)(2,1)S(1)}, bf16[512,128]{1,0:T(8,128)(2,1)S(1)}, u32[]{:S(2)}, u32[]{:S(2)}) collective-permute-start(bf16[512,128]{1,0:T(8,128)(2,1)S(1)} %collective-permute-done.2.refs_4_), channel_id=1, source_target_pairs={{0,8},{1,9},{2,10},{3,11},{4,12},{5,13},{6,14},{7,15},{8,0},{9,1},... | collective-permute-start | bytes 393224 | tf_op jit(solution)/shard_map/ppermute | solution.py:333
  22.8 0.0 collective-permute-done.3.refs_5_
  22.8 0.2 collective-permute-start.8
  23.0 2.0 %attend.5 = (f32[1,1280]{1,0:T(1,128)S(1)}, f32[8,1280]{1,0:T(8,128)S(1)}, f32[20,1280]{1,0:T(8,128)S(1)}, f32[20,384]{1,0:T(8,128)S(1)}) custom-call(bf16[5,256,256]{2,1,0:T(8,128)(2,1)S(1)} %get-tuple-element.39.refs_0_, f32[64,256]{1,0:T(8,128)S(1)} %get-tuple-element.40.refs_1_, f32[1,1280]{1,0:T(1,128)S(1)} %get-tuple-element.43.refs_2_, ...), custom_call_target="tpu_custom_call" | custom-call | flops 1200000000 | bytes 1000000 | tf_op jit(solution)/shard_map/attend/pallas_call | solution.py:375
  25.0 0.0 collective-permute-done.6.refs_5_
  25.0 0.0 collective-permute-done.5.refs_4_
  25.0 1.5 %attend.6 = (f32[1,1280]{1,0:T(1,128)S(1)}, f32[8,1280]{1,0:T(8,128)S(1)}, f32[16,1280]{1,0:T(8,128)S(1)}, f32[16,384]{1,0:T(8,128)S(1)}) custom-call(bf16[5,256,256]{2,1,0:T(8,128)(2,1)S(1)} %get-tuple-element.39.refs_0_, f32[64,256]{1,0:T(8,128)S(1)} %get-tuple-element.40.refs_1_, f32[1,1280]{1,0:T(1,128)S(1)} %get-tuple-element.47.refs_2_, ...), custom_call_target="tpu_custom_call" | custom-call | flops 1200000000 | bytes 1000000 | tf_op jit(solution)/shard_map/attend/pallas_call | solution.py:375
  26.6 0.3 collective-permute-done.7.refs_4_
  26.8 0.0 copy-start
  26.8 0.9 %attend.7 = (f32[1,1280]{1,0:T(1,128)S(1)}, f32[8,1280]{1,0:T(8,128)S(1)}, f32[8,1280]{1,0:T(8,128)S(1)}, f32[8,384]{1,0:T(8,128)S(1)}) custom-call(bf16[5,256,256]{2,1,0:T(8,128)(2,1)S(1)} %get-tuple-element.39.refs_0_, f32[64,256]{1,0:T(8,128)S(1)} %get-tuple-element.40.refs_1_, f32[1,1280]{1,0:T(1,128)S(1)} %get-tuple-element.49.refs_2_, ...), custom_call_target="tpu_custom_call" | custom-call | flops 1200000000 | bytes 1000000 | tf_op jit(solution)/shard_map/attend/pallas_call | solution.py:375
  27.7 0.5 collective-permute-done.8.refs_9_
  28.2 0.0 copy-done
  28.2 2.2 %finish.1 = (f32[5,4,64]{2,1,0:T(4,128)S(1)}, f32[512,128]{1,0:T(8,128)S(1)}, f32[520,128]{1,0:T(8,128)S(1)}) custom-call(bf16[5,256,256]{2,1,0:T(8,128)(2,1)S(1)} %get-tuple-element.39.refs_0_, f32[64,256]{1,0:T(8,128)S(1)} %get-tuple-element.40.refs_1_, f32[1,1280]{1,0:T(1,128)S(1)} %get-tuple-element.51.refs_2_, f32[8,1280]{1,0:T(8,128)S(1)} %get-tuple-element.52.refs_3_, ...), custom_call_target="tpu_custom_call" | custom-call | tf_op jit(solution)/shard_map/finish/pallas_call | solution.py:403
  30.4 5.2 %collective-permute-start.9 = (f32[520,128]{1,0:T(8,128)S(1)}, f32[520,128]{1,0:T(8,128)S(1)}, u32[]{:S(2)}, u32[]{:S(2)}) collective-permute-start(f32[520,128]{1,0:T(8,128)S(1)} %get-tuple-element.66.give_ref), channel_id=1, source_target_pairs={{0,16},{1,17},{2,18},{3,19},{4,20},{5,21},{6,22},{7,23},{8,24},{9,... | collective-permute-start | bytes 798728 | tf_op jit(solution)/shard_map/ppermute | solution.py:438
  35.6 1.2 %collective-permute-done.9.got_ref = f32[520,128]{1,0:T(8,128)S(1)} collective-permute-done((f32[520,128]{1,0:T(8,128)S(1)}, f32[520,128]{1,0:T(8,128)S(1)}, u32[]{:S(2)}, u32[]{:S(2)}) %collective-permute-start.9) | collective-permute-done | bytes 266272 | tf_op jit(solution)/shard_map/ppermute | solution.py:438
  36.8 13.3 %all_to_all.15.parts_ref = f32[16,40,128]{2,1,0:T(8,128)S(1)} all-to-all(f32[16,40,128]{2,1,0:T(8,128)S(1)} %fold.1), channel_id=1, replica_groups={{0,32,64,96,8,40,72,104,128,160,192,224,136,168,200,232},{1,33,65,97,9,..., dimensions={0} | all-to-all | bytes 655360 | tf_op jit(solution)/shard_map/all_to_all | solution.py:442
  50.2 12.4 %all_to_all.16.parts_ref = f32[8,40,128]{2,1,0:T(8,128)S(1)} all-to-all(f32[8,40,128]{2,1,0:T(8,128)S(1)} %sum.1), channel_id=1, replica_groups={{0,1,2,3,4,5,6,7},{8,9,10,11,12,13,14,15},{16,17,18,19,20,21,22,23},{24..., dimensions={0} | all-to-all | bytes 327680 | tf_op jit(solution)/shard_map/all_to_all | solution.py:444
  62.6 10.3 %all_to_all.17 = f32[16,32,128]{2,1,0:T(8,128)S(1)} all-to-all(f32[16,32,128]{2,1,0:T(8,128)S(1)} %get-tuple-element.67), channel_id=1, replica_groups={{0,32,64,96,8,40,72,104,128,160,192,224,136,168,200,232},{1,33,65,97,9,..., dimensions={0} | all-to-all | bytes 524288 | tf_op jit(solution)/shard_map/all_to_all | solution.py:455
  72.9 4.6 %collective-permute-start.10 = (f32[512,128]{1,0:T(8,128)S(1)}, f32[512,128]{1,0:T(8,128)S(1)}, u32[]{:S(2)}, u32[]{:S(2)}) collective-permute-start(f32[512,128]{1,0:T(8,128)S(1)} %bitcast.10), channel_id=1, source_target_pairs={{0,16},{1,17},{2,18},{3,19},{4,20},{5,21},{6,22},{7,23},{8,24},{9,... | collective-permute-start | bytes 786440 | tf_op jit(solution)/shard_map/ppermute | solution.py:456
  77.4 1.2 %collective-permute-done.10 = f32[512,128]{1,0:T(8,128)S(1)} collective-permute-done((f32[512,128]{1,0:T(8,128)S(1)}, f32[512,128]{1,0:T(8,128)S(1)}, u32[]{:S(2)}, u32[]{:S(2)}) %collective-permute-start.10) | collective-permute-done | bytes 262176 | tf_op jit(solution)/shard_map/ppermute | solution.py:456
  78.6 0.8 %last.1 = (f32[5,128,128]{2,1,0:T(8,128)}, f32[3,128,128]{2,1,0:T(8,128)}, f32[1,1]{1,0:T(1,128)}, f32[5,4,64]{2,1,0:T(4,128)}) custom-call(f32[4,128,128]{2,1,0:T(8,128)S(1)} %bitcast.11, f32[4,128,128]{2,1,0:T(8,128)S(1)} %bitcast.12, f32[8,128]{1,0:T(8,128)S(1)} %get-tuple-element.68.losses_ref, f32[5,4,64]{2,1,0:T(4,128)S(1)} %get-tuple-element.69.target_in), custom_call_target="tpu_custom_call" | custom-call | tf_op jit(solution)/shard_map/last/pallas_call | solution.py:458
  (6 shorter events, 0.1 us)
Async XLA Ops:
  0.6 10.2 %collective-permute-start = (bf16[256,128]{1,0:T(8,128)(2,1)}, bf16[256,128]{1,0:T(8,128)(2,1)S(1)}, u32[]{:S(2)}, u32[]{:S(2)}) collective-permute-start(bf16[256,128]{1,0:T(8,128)(2,1)} %bitcast.14), channel_id=1, source_target_pairs={{0,7},{1,0},{2,1},{3,2},{4,3},{5,4},{6,5},{7,6},{8,15},{9,8},{10,9... | collective-permute-start | bytes 196616 | tf_op jit(solution)/shard_map/ppermute | solution.py:330
  7.1 5.2 %collective-permute-start.1 = (bf16[256,128]{1,0:T(8,128)(2,1)}, bf16[256,128]{1,0:T(8,128)(2,1)S(1)}, u32[]{:S(2)}, u32[]{:S(2)}) collective-permute-start(bf16[256,128]{1,0:T(8,128)(2,1)} %bitcast.15), channel_id=1, source_target_pairs={{0,1},{1,2},{2,3},{3,4},{4,5},{5,6},{6,7},{7,0},{8,9},{9,10},{10,1... | collective-permute-start | bytes 196616 | tf_op jit(solution)/shard_map/ppermute | solution.py:330
  7.1 10.5 %collective-permute-start.4 = (bf16[256,128]{1,0:T(8,128)(2,1)}, bf16[256,128]{1,0:T(8,128)(2,1)S(1)}, u32[]{:S(2)}, u32[]{:S(2)}) collective-permute-start(bf16[256,128]{1,0:T(8,128)(2,1)} %bitcast.16), channel_id=1, source_target_pairs={{0,4},{1,5},{2,6},{3,7},{4,0},{5,1},{6,2},{7,3},{8,12},{9,13},{10,... | collective-permute-start | bytes 196616 | tf_op jit(solution)/shard_map/ppermute | solution.py:330
  9.9 0.9 %copy-start.3 = (bf16[1,256,128]{2,1,0:T(8,128)(2,1)S(1)}, bf16[1,256,128]{2,1,0:T(8,128)(2,1)}, u32[]{:S(2)}) copy-start(bf16[1,256,128]{2,1,0:T(8,128)(2,1)} %param.7) | copy-start | bytes 196612
  10.8 7.1 %copy-start.2 = (f32[5,128,128]{2,1,0:T(8,128)S(1)}, f32[5,128,128]{2,1,0:T(8,128)}, u32[]{:S(2)}) copy-start(f32[5,128,128]{2,1,0:T(8,128)} %wq_ref.1) | copy-start | bytes 983044
  10.8 7.1 %copy-start.1 = (bf16[1,256,5,128]{3,1,2,0:T(8,128)(2,1)S(1)}, bf16[1,256,5,128]{3,1,2,0:T(8,128)(2,1)}, u32[]{:S(2)}) copy-start(bf16[1,256,5,128]{3,1,2,0:T(8,128)(2,1)} %param.6) | copy-start | bytes 983044
  12.3 7.7 %collective-permute-start.2 = (bf16[512,128]{1,0:T(8,128)(2,1)S(1)}, bf16[512,128]{1,0:T(8,128)(2,1)S(1)}, u32[]{:S(2)}, u32[]{:S(2)}) collective-permute-start(bf16[512,128]{1,0:T(8,128)(2,1)S(1)} %get-tuple-element.45), channel_id=1, source_target_pairs={{0,6},{1,7},{2,0},{3,1},{4,2},{5,3},{6,4},{7,5},{8,14},{9,15},{10,... | collective-permute-start | bytes 393224 | tf_op jit(solution)/shard_map/ppermute | solution.py:330
  12.4 10.4 %collective-permute-start.3 = (bf16[512,128]{1,0:T(8,128)(2,1)S(1)}, bf16[512,128]{1,0:T(8,128)(2,1)S(1)}, u32[]{:S(2)}, u32[]{:S(2)}) collective-permute-start(bf16[512,128]{1,0:T(8,128)(2,1)S(1)} %get-tuple-element.46), channel_id=1, source_target_pairs={{0,2},{1,3},{2,4},{3,5},{4,6},{5,7},{6,0},{7,1},{8,10},{9,11},{10,... | collective-permute-start | bytes 393224 | tf_op jit(solution)/shard_map/ppermute | solution.py:330
  14.8 3.1 %copy-start.4 = (s32[1,32]{1,0:T(1,128)S(1)}, s32[1,32]{1,0:T(1,128)}, u32[]{:S(2)}) copy-start(s32[1,32]{1,0:T(1,128)} %order_ref.1) | copy-start | bytes 388
  14.8 10.2 %collective-permute-start.5 = (bf16[768,128]{1,0:T(8,128)(2,1)S(1)}, bf16[768,128]{1,0:T(8,128)(2,1)S(1)}, u32[]{:S(2)}, u32[]{:S(2)}) collective-permute-start(bf16[768,128]{1,0:T(8,128)(2,1)S(1)} %pad_maximum_fusion.refs_4_), channel_id=1, source_target_pairs={{0,8},{1,9},{2,10},{3,11},{4,12},{5,13},{6,14},{7,15},{8,0},{9,1},... | collective-permute-start | bytes 589832 | tf_op jit(solution)/shard_map/ppermute | solution.py:333
  17.6 7.4 %collective-permute-start.6 = (bf16[256,128]{1,0:T(8,128)(2,1)S(1)}, bf16[256,128]{1,0:T(8,128)(2,1)S(1)}, u32[]{:S(2)}, u32[]{:S(2)}) collective-permute-start(bf16[256,128]{1,0:T(8,128)(2,1)S(1)} %collective-permute-done.4.refs_6_), channel_id=1, source_target_pairs={{0,8},{1,9},{2,10},{3,11},{4,12},{5,13},{6,14},{7,15},{8,0},{9,1},... | collective-permute-start | bytes 196616 | tf_op jit(solution)/shard_map/ppermute | solution.py:333
  20.1 6.8 %collective-permute-start.7 = (bf16[512,128]{1,0:T(8,128)(2,1)S(1)}, bf16[512,128]{1,0:T(8,128)(2,1)S(1)}, u32[]{:S(2)}, u32[]{:S(2)}) collective-permute-start(bf16[512,128]{1,0:T(8,128)(2,1)S(1)} %collective-permute-done.2.refs_4_), channel_id=1, source_target_pairs={{0,8},{1,9},{2,10},{3,11},{4,12},{5,13},{6,14},{7,15},{8,0},{9,1},... | collective-permute-start | bytes 393224 | tf_op jit(solution)/shard_map/ppermute | solution.py:333
  22.8 5.4 %collective-permute-start.8 = (bf16[512,128]{1,0:T(8,128)(2,1)S(1)}, bf16[512,128]{1,0:T(8,128)(2,1)S(1)}, u32[]{:S(2)}, u32[]{:S(2)}) collective-permute-start(bf16[512,128]{1,0:T(8,128)(2,1)S(1)} %collective-permute-done.3.refs_5_), channel_id=1, source_target_pairs={{0,8},{1,9},{2,10},{3,11},{4,12},{5,13},{6,14},{7,15},{8,0},{9,1},... | collective-permute-start | bytes 393224 | tf_op jit(solution)/shard_map/ppermute | solution.py:333
  26.8 1.4 %copy-start = (f32[384,128]{1,0:T(8,128)S(1)}, f32[384,128]{1,0:T(8,128)}, u32[]{:S(2)}) copy-start(f32[384,128]{1,0:T(8,128)} %refs_7_.1) | copy-start | bytes 589828
  30.4 6.4 %collective-permute-start.9 = (f32[520,128]{1,0:T(8,128)S(1)}, f32[520,128]{1,0:T(8,128)S(1)}, u32[]{:S(2)}, u32[]{:S(2)}) collective-permute-start(f32[520,128]{1,0:T(8,128)S(1)} %get-tuple-element.66.give_ref), channel_id=1, source_target_pairs={{0,16},{1,17},{2,18},{3,19},{4,20},{5,21},{6,22},{7,23},{8,24},{9,... | collective-permute-start | bytes 798728 | tf_op jit(solution)/shard_map/ppermute | solution.py:438
  72.9 5.7 %collective-permute-start.10 = (f32[512,128]{1,0:T(8,128)S(1)}, f32[512,128]{1,0:T(8,128)S(1)}, u32[]{:S(2)}, u32[]{:S(2)}) collective-permute-start(f32[512,128]{1,0:T(8,128)S(1)} %bitcast.10), channel_id=1, source_target_pairs={{0,16},{1,17},{2,18},{3,19},{4,20},{5,21},{6,22},{7,23},{8,24},{9,... | collective-permute-start | bytes 786440 | tf_op jit(solution)/shard_map/ppermute | solution.py:456

commit v6 on v5

--- a/solution.py
+++ b/solution.py
@@ -81,7 +81,7 @@
     lane = lax.broadcasted_iota(jnp.int32, (2 * group, rows), 1)
     halves = [pick(order, jnp.full((1, 1), 2 * place + part, jnp.int32)) for part in range(2)]
     seen = jnp.where(key_half < jnp.where(lane < half, halves[0], halves[1]), 1.0, 0.0)
-    shift = (near - along) * blocks
+    shift = lax.rem(near - along, near) * blocks
     low, high = [pltpu.roll(seen[j * group : (j + 1) * group], shift, 0) for j in range(2)]
     seen_ref[0:group, :] = jnp.where(base == 0, low, high)
     seen_ref[group:, :] = jnp.where(base == 0, high, low)
@@ -91,6 +91,11 @@
     row = lax.broadcasted_iota(jnp.int32, (heads * SUB, 1), 0) % SUB
     query_pos = jnp.where(row < per, halves[0], halves[1]) * per + (row % per).astype(jnp.float32)
     visible_ref[...] = jnp.where((key_pos <= query_pos) & (row < blocks), 1.0, 0.0)
+
+
+def pool_of(keys):
+    x = keys.astype(jnp.float32).reshape(keys.shape[0] // POOL, POOL, keys.shape[1])
+    return jnp.concatenate([jnp.max(x, axis=1), jnp.min(x, axis=1), jnp.sum(x, axis=1) * (1.0 / POOL)], axis=1)
 
 
 def attend(q2_ref, seen_ref, chunks, top_in, tot_in, top_ref, tot_ref, map_ref, pool_ref):
@@ -103,10 +108,7 @@
         group = chunks[first : first + 2]
         keys = jnp.concatenate([read() for read, _ in group], axis=0)
         count = len(group) * blocks
-        x = keys.astype(jnp.float32).reshape(count, POOL, keys.shape[1])
-        pool_ref[row : row + count, :] = jnp.concatenate(
-            [jnp.max(x, axis=1), jnp.min(x, axis=1), jnp.sum(x, axis=1) * (1.0 / POOL)], axis=1
-        )
+        pool_ref[row : row + count, :] = pool_of(keys)
         seen = jnp.concatenate([seen_ref[at : at + blocks, :] for _, at in group], axis=0)
         seen_rows = jnp.broadcast_to(seen[:, None, :], (count, SUB, rows)) > 0.5
         seen = seen > 0.5
@@ -154,12 +156,24 @@
         out_ref[rows:, :] = other_ref[...]
 
 
+def gradient_half(low, pooled_ref, gate_q_grad_ref, pool_ref, gate_k_grad_ref, out_ref):
+    heads = pooled_ref.shape[0] // SUB
+    width = pooled_ref.shape[1]
+    whole = (heads + pool_ref.shape[1] // width) // 2
+    chosen = range(whole) if low else range(whole, heads)
+    for j, h in enumerate(chosen):
+        here = slice(h * SUB, (h + 1) * SUB)
+        out_ref[j * width : (j + 1) * width, :] = dot_split(pooled_ref[here, :], gate_q_grad_ref[here, :], TN)
+    if not low:
+        out_ref[len(chosen) * width : whole * width, :] = dot_split(pool_ref[...], gate_k_grad_ref[...], TN)
+
+
 def finish_kernel(layout, places, *refs):
     q2_ref, seen_ref, top_in, tot_in, diag_ref, pooled_ref, gate_q_ref, wk_ref, visible_ref = refs[:9]
     key_refs = refs[9 : 9 + len(layout)]
     earlier = refs[9 + len(layout) : -12]
-    target_ref, keep_ref, give_ref = refs[-12:-9]
-    top_ref, tot_ref, last_map, last_pool, map_ref, rel_pool, pool_ref, block_ref, grad_ref = refs[-9:]
+    target_ref, give_ref, gate_q_grad_ref, gate_k_grad_ref, pool_ref = refs[-12:-7]
+    top_ref, tot_ref, last_map, last_pool, map_ref, rel_pool, block_ref = refs[-7:]
     heads, rows, _ = q2_ref.shape
     half = rows // 2
     per = half // POOL
@@ -220,18 +234,21 @@
     count = heads * total
     loss = -jnp.sum(jnp.where(visible, target * log_gate, 0.0)) / count
     d_logits = jnp.where(visible, weights / norm_sum - target, 0.0) / count * gate_width ** (-0.5)
-    gate_q_grad = dot_split(d_logits, gate_k, NN)
-    for h in range(heads):
-        here = slice(h * SUB, (h + 1) * SUB)
-        grad_ref[h * width : (h + 1) * width, :] = dot_split(pooled_ref[here, :], gate_q_grad[here], TN)
-    grad_ref[heads * width :, :] = dot_split(pool_ref[...], dot_split(d_logits, gate_q, TN), TN)
-    part = keep_ref.shape[0]
+    gate_q_grad_ref[...] = dot_split(d_logits, gate_k, NN)
+    gate_k_grad_ref[...] = dot_split(d_logits, gate_q, TN)
     own_seq = lax.axis_index("seq")
-    core = lax.rem(own_seq, 2)
-    keep_ref[...] = grad_ref[pl.ds(pl.multiple_of(core * part, part), part), :]
-    give_ref[0:part, :] = grad_ref[pl.ds(pl.multiple_of((1 - core) * part, part), part), :]
+    terms = (pooled_ref, gate_q_grad_ref, pool_ref, gate_k_grad_ref)
+    pl.when(lax.rem(own_seq, 2) == 0)(lambda: gradient_half(False, *terms, give_ref))
+    pl.when(lax.rem(own_seq, 2) != 0)(lambda: gradient_half(True, *terms, give_ref))
     lane = lax.broadcasted_iota(jnp.int32, (SUB, gate_width), 1)
-    give_ref[part:, :] = jnp.where(lane == own_seq, loss, 0.0)
+    give_ref[give_ref.shape[0] - SUB :, :] = jnp.where(lane == own_seq, loss, 0.0)
+
+
+def keep_kernel(pooled_ref, gate_q_grad_ref, pool_ref, gate_k_grad_ref, keep_ref):
+    terms = (pooled_ref, gate_q_grad_ref, pool_ref, gate_k_grad_ref)
+    core = lax.rem(lax.axis_index("seq"), 2)
+    pl.when(core == 0)(lambda: gradient_half(True, *terms, keep_ref))
+    pl.when(core != 0)(lambda: gradient_half(False, *terms, keep_ref))
 
 
 def fold_kernel(keep_ref, give_ref, got_ref, out_ref):
@@ -400,9 +417,15 @@
     grad_rows = heads * width + 3 * width
     part = grad_rows // 2
     last_blocks = len(places[-1]) * blocks
-    target, keep, give = call(
+    target, give, *terms = call(
         functools.partial(finish_kernel, layouts[-1], places),
-        (f32(heads, blocks, total), f32(part, gate_width), f32(part + SUB, gate_width)),
+        (
+            f32(heads, blocks, total),
+            f32(part + SUB, gate_width),
+            f32(heads * SUB, gate_width),
+            f32(total, gate_width),
+            f32(total, 3 * width),
+        ),
         [VMEM] * (10 + len(earlier)),
         "finish",
         scratch=[
@@ -414,9 +437,7 @@
                 (last_blocks, 3 * width),
                 (total, columns),
                 (total, 3 * width),
-                (total, 3 * width),
                 (heads * SUB, total),
-                (grad_rows, gate_width),
             )
         ],
     )(q2, seen, top, tot, diag, pooled, gate_q, w_key_gate, visible, behind_far, *earlier)
@@ -436,6 +457,9 @@
     planes = [[flat(a, y, b, c, z) for a in pair for c in pair for y in ys] for b in pair for z in zs]
     tiles = len(planes[0])
     got = lax.ppermute(give, every, cores)
+    (keep,) = call(keep_kernel, (f32(part, gate_width),), [VMEM] * 4, "keep")(
+        pooled, terms[0], terms[2], terms[1]
+    )
     (parts,) = call(
         fold_kernel, (f32(tiles, part // tiles + SUB, gate_width),), [VMEM] * 3, "fold"
     )(keep, give, got)

time: 79.8 us -> 79.6 us (level)
  no operation moved by 1% of the time
where the time goes in v6:
time: 79.6 us; the launch traced here: 79.3 us
  blocking collectives  35.9 us (45%)
  starting transfers between devices  27.5 us (35%)
  Pallas kernels  9.55 us (12%)
  waiting for transfers between devices  4.5 us (6%)
  between operations  0.92 us (1%)
  local copies, waits for them, and re-layouts  0.89 us (1%)
    all_to_all x1, blocking collectives, on_device(): lax.all_to_all(parts, every, 0, 0, axis_index_groups=planes, tiled=True)  13.3 us
    all_to_all x1, blocking collectives, on_device(): lax.all_to_all(spread, 'ctx', 0, 0, axis_index_groups=[list(range(near)),...  12.4 us
    ppermute x5, starting transfers between devices, get(): lax.ppermute(x, 'ctx', [(j, j // near * near + (j - offset) % near) for j...  11.7 us
    all_to_all x1, blocking collectives, on_device(): lax.all_to_all(spread, every, 0, 0, axis_index_groups=planes, tiled=True)  10.3 us
    ppermute x4, starting transfers between devices, across(): lax.ppermute(x, 'ctx', [(j, (j + near) % ctx_count) for j in range(ctx_co...  6.03 us
    pallas_call x4, Pallas kernels, attend_to(): call(functools.partial(attend_kernel, layout), state + (f32(count * block...  5.65 us
    ppermute x1, starting transfers between devices, on_device(): got = lax.ppermute(give, every, cores)  5.19 us
    ppermute x1, starting transfers between devices, on_device(): other = lax.ppermute(mine, every, cores)  4.56 us
  transfers between devices with their start and end apart: 11, of which 6 were waited for; matrix products, arithmetic and copies ran while one was open for 0% of the time, Pallas kernels for 8%

profile of v6, /device:TPU:1, one launch (start us, length us, event | category | flops | bytes accessed | tf_op | source)
XLA Modules:
  0.0 79.3 jit_solution(13420313535347787840)
XLA Ops:
  0.6 6.5 %collective-permute-start = (bf16[256,128]{1,0:T(8,128)(2,1)}, bf16[256,128]{1,0:T(8,128)(2,1)S(1)}, u32[]{:S(2)}, u32[]{:S(2)}) collective-permute-start(bf16[256,128]{1,0:T(8,128)(2,1)} %bitcast.14), channel_id=1, source_target_pairs={{0,7},{1,0},{2,1},{3,2},{4,3},{5,4},{6,5},{7,6},{8,15},{9,8},{10,9... | collective-permute-start | bytes 196616 | tf_op jit(solution)/shard_map/ppermute | solution.py:347
  7.1 0.0 collective-permute-start.1
  7.1 2.8 %collective-permute-start.4 = (bf16[256,128]{1,0:T(8,128)(2,1)}, bf16[256,128]{1,0:T(8,128)(2,1)S(1)}, u32[]{:S(2)}, u32[]{:S(2)}) collective-permute-start(bf16[256,128]{1,0:T(8,128)(2,1)} %bitcast.16), channel_id=1, source_target_pairs={{0,4},{1,5},{2,6},{3,7},{4,0},{5,1},{6,2},{7,3},{8,12},{9,13},{10,... | collective-permute-start | bytes 196616 | tf_op jit(solution)/shard_map/ppermute | solution.py:347
  9.9 0.0 copy-start.3
  9.9 0.9 %copy-done.3 = bf16[1,256,128]{2,1,0:T(8,128)(2,1)S(1)} copy-done((bf16[1,256,128]{2,1,0:T(8,128)(2,1)S(1)}, bf16[1,256,128]{2,1,0:T(8,128)(2,1)}, u32[]{:S(2)}) %copy-start.3) | copy-done | bytes 65560
  10.8 0.0 copy-start.2
  10.8 0.0 copy-start.1
  10.8 0.0 collective-permute-done.refs_0_.a_ref
  10.8 1.5 %collective-permute-done.1.refs_1_.b_ref = bf16[256,128]{1,0:T(8,128)(2,1)S(1)} collective-permute-done((bf16[256,128]{1,0:T(8,128)(2,1)}, bf16[256,128]{1,0:T(8,128)(2,1)S(1)}, u32[]{:S(2)}, u32[]{:S(2)}) %collective-permute-start.1) | collective-permute-done | bytes 65568 | tf_op jit(solution)/shard_map/ppermute | solution.py:347
  12.3 0.1 collective-permute-start.2
  12.4 2.4 %collective-permute-start.3 = (bf16[512,128]{1,0:T(8,128)(2,1)S(1)}, bf16[512,128]{1,0:T(8,128)(2,1)S(1)}, u32[]{:S(2)}, u32[]{:S(2)}) collective-permute-start(bf16[512,128]{1,0:T(8,128)(2,1)S(1)} %get-tuple-element.49), channel_id=1, source_target_pairs={{0,2},{1,3},{2,4},{3,5},{4,6},{5,7},{6,0},{7,1},{8,10},{9,11},{10,... | collective-permute-start | bytes 393224 | tf_op jit(solution)/shard_map/ppermute | solution.py:347
  14.8 0.0 copy-start.4
  14.8 2.8 %collective-permute-start.5 = (bf16[768,128]{1,0:T(8,128)(2,1)S(1)}, bf16[768,128]{1,0:T(8,128)(2,1)S(1)}, u32[]{:S(2)}, u32[]{:S(2)}) collective-permute-start(bf16[768,128]{1,0:T(8,128)(2,1)S(1)} %pad_maximum_fusion.refs_4_), channel_id=1, source_target_pairs={{0,8},{1,9},{2,10},{3,11},{4,12},{5,13},{6,14},{7,15},{8,0},{9,1},... | collective-permute-start | bytes 589832 | tf_op jit(solution)/shard_map/ppermute | solution.py:350
  17.6 0.0 collective-permute-done.4.refs_6_
  17.6 0.2 collective-permute-start.6
  17.9 0.0 copy-done.2
  17.9 0.0 copy-done.1
  17.9 0.0 copy-done.4
  17.9 0.7 local.1
  18.6 1.3 %attend.4 = (f32[1,1280]{1,0:T(1,128)S(1)}, f32[8,1280]{1,0:T(8,128)S(1)}, f32[12,1280]{1,0:T(8,128)S(1)}, f32[12,384]{1,0:T(8,128)S(1)}) custom-call(bf16[5,256,256]{2,1,0:T(8,128)(2,1)S(1)} %get-tuple-element.42.refs_0_, f32[64,256]{1,0:T(8,128)S(1)} %get-tuple-element.43.refs_1_, f32[1,1280]{1,0:T(1,128)S(1)} %get-tuple-element.44.refs_2_, ...), custom_call_target="tpu_custom_call" | custom-call | flops 1200000000 | bytes 1000000 | tf_op jit(solution)/shard_map/attend/pallas_call | solution.py:392
  19.8 0.2 collective-permute-done.2.refs_4_
  20.1 2.7 %collective-permute-start.7 = (bf16[512,128]{1,0:T(8,128)(2,1)S(1)}, bf16[512,128]{1,0:T(8,128)(2,1)S(1)}, u32[]{:S(2)}, u32[]{:S(2)}) collective-permute-start(bf16[512,128]{1,0:T(8,128)(2,1)S(1)} %collective-permute-done.2.refs_4_), channel_id=1, source_target_pairs={{0,8},{1,9},{2,10},{3,11},{4,12},{5,13},{6,14},{7,15},{8,0},{9,1},... | collective-permute-start | bytes 393224 | tf_op jit(solution)/shard_map/ppermute | solution.py:350
  22.8 0.0 collective-permute-done.3.refs_5_
  22.8 0.2 collective-permute-start.8
  23.0 2.0 %attend.5 = (f32[1,1280]{1,0:T(1,128)S(1)}, f32[8,1280]{1,0:T(8,128)S(1)}, f32[20,1280]{1,0:T(8,128)S(1)}, f32[20,384]{1,0:T(8,128)S(1)}) custom-call(bf16[5,256,256]{2,1,0:T(8,128)(2,1)S(1)} %get-tuple-element.42.refs_0_, f32[64,256]{1,0:T(8,128)S(1)} %get-tuple-element.43.refs_1_, f32[1,1280]{1,0:T(1,128)S(1)} %get-tuple-element.46.refs_2_, ...), custom_call_target="tpu_custom_call" | custom-call | flops 1200000000 | bytes 1000000 | tf_op jit(solution)/shard_map/attend/pallas_call | solution.py:392
  25.0 0.0 collective-permute-done.6.refs_5_
  25.0 0.0 collective-permute-done.5.refs_4_
  25.1 1.5 %attend.6 = (f32[1,1280]{1,0:T(1,128)S(1)}, f32[8,1280]{1,0:T(8,128)S(1)}, f32[16,1280]{1,0:T(8,128)S(1)}, f32[16,384]{1,0:T(8,128)S(1)}) custom-call(bf16[5,256,256]{2,1,0:T(8,128)(2,1)S(1)} %get-tuple-element.42.refs_0_, f32[64,256]{1,0:T(8,128)S(1)} %get-tuple-element.43.refs_1_, f32[1,1280]{1,0:T(1,128)S(1)} %get-tuple-element.50.refs_2_, ...), custom_call_target="tpu_custom_call" | custom-call | flops 1200000000 | bytes 1000000 | tf_op jit(solution)/shard_map/attend/pallas_call | solution.py:392
  26.6 0.2 collective-permute-done.7.refs_4_
  26.8 0.0 copy-start
  26.8 0.9 %attend.7 = (f32[1,1280]{1,0:T(1,128)S(1)}, f32[8,1280]{1,0:T(8,128)S(1)}, f32[8,1280]{1,0:T(8,128)S(1)}, f32[8,384]{1,0:T(8,128)S(1)}) custom-call(bf16[5,256,256]{2,1,0:T(8,128)(2,1)S(1)} %get-tuple-element.42.refs_0_, f32[64,256]{1,0:T(8,128)S(1)} %get-tuple-element.43.refs_1_, f32[1,1280]{1,0:T(1,128)S(1)} %get-tuple-element.52.refs_2_, ...), custom_call_target="tpu_custom_call" | custom-call | flops 1200000000 | bytes 1000000 | tf_op jit(solution)/shard_map/attend/pallas_call | solution.py:392
  27.7 0.5 collective-permute-done.8.refs_9_
  28.2 0.0 copy-done
  28.2 1.9 %finish.1 = (f32[5,4,64]{2,1,0:T(4,128)S(1)}, f32[520,128]{1,0:T(8,128)S(1)}, f32[40,128]{1,0:T(8,128)S(1)}, f32[64,128]{1,0:T(8,128)S(1)}, f32[64,384]{1,0:T(8,128)S(1)}) custom-call(bf16[5,256,256]{2,1,0:T(8,128)(2,1)S(1)} %get-tuple-element.42.refs_0_, f32[64,256]{1,0:T(8,128)S(1)} %get-tuple-element.43.refs_1_, f32[1,1280]{1,0:T(1,128)S(1)} %get-tuple-element.54.refs_2_, ...), custom_call_target="tpu_custom_call" | custom-call | tf_op jit(solution)/shard_map/finish/pallas_call | solution.py:420
  30.2 5.2 %collective-permute-start.9 = (f32[520,128]{1,0:T(8,128)S(1)}, f32[520,128]{1,0:T(8,128)S(1)}, u32[]{:S(2)}, u32[]{:S(2)}) collective-permute-start(f32[520,128]{1,0:T(8,128)S(1)} %get-tuple-element.70.give_ref), channel_id=1, source_target_pairs={{0,16},{1,17},{2,18},{3,19},{4,20},{5,21},{6,22},{7,23},{8,24},{9,... | collective-permute-start | bytes 798728 | tf_op jit(solution)/shard_map/ppermute | solution.py:459
  35.4 0.3 keep.1.keep_ref
  35.7 0.8 %collective-permute-done.9.got_ref = f32[520,128]{1,0:T(8,128)S(1)} collective-permute-done((f32[520,128]{1,0:T(8,128)S(1)}, f32[520,128]{1,0:T(8,128)S(1)}, u32[]{:S(2)}, u32[]{:S(2)}) %collective-permute-start.9) | collective-permute-done | bytes 266272 | tf_op jit(solution)/shard_map/ppermute | solution.py:459
  36.6 13.3 %all_to_all.15.parts_ref = f32[16,40,128]{2,1,0:T(8,128)S(1)} all-to-all(f32[16,40,128]{2,1,0:T(8,128)S(1)} %fold.1), channel_id=1, replica_groups={{0,32,64,96,8,40,72,104,128,160,192,224,136,168,200,232},{1,33,65,97,9,..., dimensions={0} | all-to-all | bytes 655360 | tf_op jit(solution)/shard_map/all_to_all | solution.py:466
  49.9 12.4 %all_to_all.16.parts_ref = f32[8,40,128]{2,1,0:T(8,128)S(1)} all-to-all(f32[8,40,128]{2,1,0:T(8,128)S(1)} %sum.1), channel_id=1, replica_groups={{0,1,2,3,4,5,6,7},{8,9,10,11,12,13,14,15},{16,17,18,19,20,21,22,23},{24..., dimensions={0} | all-to-all | bytes 327680 | tf_op jit(solution)/shard_map/all_to_all | solution.py:468
  62.3 10.3 %all_to_all.17 = f32[16,32,128]{2,1,0:T(8,128)S(1)} all-to-all(f32[16,32,128]{2,1,0:T(8,128)S(1)} %get-tuple-element.71), channel_id=1, replica_groups={{0,32,64,96,8,40,72,104,128,160,192,224,136,168,200,232},{1,33,65,97,9,..., dimensions={0} | all-to-all | bytes 524288 | tf_op jit(solution)/shard_map/all_to_all | solution.py:479
  72.6 4.6 %collective-permute-start.10 = (f32[512,128]{1,0:T(8,128)S(1)}, f32[512,128]{1,0:T(8,128)S(1)}, u32[]{:S(2)}, u32[]{:S(2)}) collective-permute-start(f32[512,128]{1,0:T(8,128)S(1)} %bitcast.10), channel_id=1, source_target_pairs={{0,16},{1,17},{2,18},{3,19},{4,20},{5,21},{6,22},{7,23},{8,24},{9,... | collective-permute-start | bytes 786440 | tf_op jit(solution)/shard_map/ppermute | solution.py:480
  77.2 1.2 %collective-permute-done.10 = f32[512,128]{1,0:T(8,128)S(1)} collective-permute-done((f32[512,128]{1,0:T(8,128)S(1)}, f32[512,128]{1,0:T(8,128)S(1)}, u32[]{:S(2)}, u32[]{:S(2)}) %collective-permute-start.10) | collective-permute-done | bytes 262176 | tf_op jit(solution)/shard_map/ppermute | solution.py:480
  78.3 0.8 %last.1 = (f32[5,128,128]{2,1,0:T(8,128)}, f32[3,128,128]{2,1,0:T(8,128)}, f32[1,1]{1,0:T(1,128)}, f32[5,4,64]{2,1,0:T(4,128)}) custom-call(f32[4,128,128]{2,1,0:T(8,128)S(1)} %bitcast.11, f32[4,128,128]{2,1,0:T(8,128)S(1)} %bitcast.12, f32[8,128]{1,0:T(8,128)S(1)} %get-tuple-element.72.losses_ref, f32[5,4,64]{2,1,0:T(4,128)S(1)} %get-tuple-element.73.target_in), custom_call_target="tpu_custom_call" | custom-call | tf_op jit(solution)/shard_map/last/pallas_call | solution.py:482
  (6 shorter events, 0.1 us)
Async XLA Ops:
  0.6 10.2 %collective-permute-start = (bf16[256,128]{1,0:T(8,128)(2,1)}, bf16[256,128]{1,0:T(8,128)(2,1)S(1)}, u32[]{:S(2)}, u32[]{:S(2)}) collective-permute-start(bf16[256,128]{1,0:T(8,128)(2,1)} %bitcast.14), channel_id=1, source_target_pairs={{0,7},{1,0},{2,1},{3,2},{4,3},{5,4},{6,5},{7,6},{8,15},{9,8},{10,9... | collective-permute-start | bytes 196616 | tf_op jit(solution)/shard_map/ppermute | solution.py:347
  7.1 5.2 %collective-permute-start.1 = (bf16[256,128]{1,0:T(8,128)(2,1)}, bf16[256,128]{1,0:T(8,128)(2,1)S(1)}, u32[]{:S(2)}, u32[]{:S(2)}) collective-permute-start(bf16[256,128]{1,0:T(8,128)(2,1)} %bitcast.15), channel_id=1, source_target_pairs={{0,1},{1,2},{2,3},{3,4},{4,5},{5,6},{6,7},{7,0},{8,9},{9,10},{10,1... | collective-permute-start | bytes 196616 | tf_op jit(solution)/shard_map/ppermute | solution.py:347
  7.1 10.5 %collective-permute-start.4 = (bf16[256,128]{1,0:T(8,128)(2,1)}, bf16[256,128]{1,0:T(8,128)(2,1)S(1)}, u32[]{:S(2)}, u32[]{:S(2)}) collective-permute-start(bf16[256,128]{1,0:T(8,128)(2,1)} %bitcast.16), channel_id=1, source_target_pairs={{0,4},{1,5},{2,6},{3,7},{4,0},{5,1},{6,2},{7,3},{8,12},{9,13},{10,... | collective-permute-start | bytes 196616 | tf_op jit(solution)/shard_map/ppermute | solution.py:347
  9.9 0.9 %copy-start.3 = (bf16[1,256,128]{2,1,0:T(8,128)(2,1)S(1)}, bf16[1,256,128]{2,1,0:T(8,128)(2,1)}, u32[]{:S(2)}) copy-start(bf16[1,256,128]{2,1,0:T(8,128)(2,1)} %param.7) | copy-start | bytes 196612
  10.8 7.1 %copy-start.2 = (f32[5,128,128]{2,1,0:T(8,128)S(1)}, f32[5,128,128]{2,1,0:T(8,128)}, u32[]{:S(2)}) copy-start(f32[5,128,128]{2,1,0:T(8,128)} %wq_ref.1) | copy-start | bytes 983044
  10.8 7.1 %copy-start.1 = (bf16[1,256,5,128]{3,1,2,0:T(8,128)(2,1)S(1)}, bf16[1,256,5,128]{3,1,2,0:T(8,128)(2,1)}, u32[]{:S(2)}) copy-start(bf16[1,256,5,128]{3,1,2,0:T(8,128)(2,1)} %param.6) | copy-start | bytes 983044
  12.3 7.7 %collective-permute-start.2 = (bf16[512,128]{1,0:T(8,128)(2,1)S(1)}, bf16[512,128]{1,0:T(8,128)(2,1)S(1)}, u32[]{:S(2)}, u32[]{:S(2)}) collective-permute-start(bf16[512,128]{1,0:T(8,128)(2,1)S(1)} %get-tuple-element.48), channel_id=1, source_target_pairs={{0,6},{1,7},{2,0},{3,1},{4,2},{5,3},{6,4},{7,5},{8,14},{9,15},{10,... | collective-permute-start | bytes 393224 | tf_op jit(solution)/shard_map/ppermute | solution.py:347
  12.4 10.4 %collective-permute-start.3 = (bf16[512,128]{1,0:T(8,128)(2,1)S(1)}, bf16[512,128]{1,0:T(8,128)(2,1)S(1)}, u32[]{:S(2)}, u32[]{:S(2)}) collective-permute-start(bf16[512,128]{1,0:T(8,128)(2,1)S(1)} %get-tuple-element.49), channel_id=1, source_target_pairs={{0,2},{1,3},{2,4},{3,5},{4,6},{5,7},{6,0},{7,1},{8,10},{9,11},{10,... | collective-permute-start | bytes 393224 | tf_op jit(solution)/shard_map/ppermute | solution.py:347
  14.8 3.1 %copy-start.4 = (s32[1,32]{1,0:T(1,128)S(1)}, s32[1,32]{1,0:T(1,128)}, u32[]{:S(2)}) copy-start(s32[1,32]{1,0:T(1,128)} %order_ref.1) | copy-start | bytes 388
  14.8 10.2 %collective-permute-start.5 = (bf16[768,128]{1,0:T(8,128)(2,1)S(1)}, bf16[768,128]{1,0:T(8,128)(2,1)S(1)}, u32[]{:S(2)}, u32[]{:S(2)}) collective-permute-start(bf16[768,128]{1,0:T(8,128)(2,1)S(1)} %pad_maximum_fusion.refs_4_), channel_id=1, source_target_pairs={{0,8},{1,9},{2,10},{3,11},{4,12},{5,13},{6,14},{7,15},{8,0},{9,1},... | collective-permute-start | bytes 589832 | tf_op jit(solution)/shard_map/ppermute | solution.py:350
  17.6 7.4 %collective-permute-start.6 = (bf16[256,128]{1,0:T(8,128)(2,1)S(1)}, bf16[256,128]{1,0:T(8,128)(2,1)S(1)}, u32[]{:S(2)}, u32[]{:S(2)}) collective-permute-start(bf16[256,128]{1,0:T(8,128)(2,1)S(1)} %collective-permute-done.4.refs_6_), channel_id=1, source_target_pairs={{0,8},{1,9},{2,10},{3,11},{4,12},{5,13},{6,14},{7,15},{8,0},{9,1},... | collective-permute-start | bytes 196616 | tf_op jit(solution)/shard_map/ppermute | solution.py:350
  20.1 6.8 %collective-permute-start.7 = (bf16[512,128]{1,0:T(8,128)(2,1)S(1)}, bf16[512,128]{1,0:T(8,128)(2,1)S(1)}, u32[]{:S(2)}, u32[]{:S(2)}) collective-permute-start(bf16[512,128]{1,0:T(8,128)(2,1)S(1)} %collective-permute-done.2.refs_4_), channel_id=1, source_target_pairs={{0,8},{1,9},{2,10},{3,11},{4,12},{5,13},{6,14},{7,15},{8,0},{9,1},... | collective-permute-start | bytes 393224 | tf_op jit(solution)/shard_map/ppermute | solution.py:350
  22.8 5.4 %collective-permute-start.8 = (bf16[512,128]{1,0:T(8,128)(2,1)S(1)}, bf16[512,128]{1,0:T(8,128)(2,1)S(1)}, u32[]{:S(2)}, u32[]{:S(2)}) collective-permute-start(bf16[512,128]{1,0:T(8,128)(2,1)S(1)} %collective-permute-done.3.refs_5_), channel_id=1, source_target_pairs={{0,8},{1,9},{2,10},{3,11},{4,12},{5,13},{6,14},{7,15},{8,0},{9,1},... | collective-permute-start | bytes 393224 | tf_op jit(solution)/shard_map/ppermute | solution.py:350
  26.8 1.4 %copy-start = (f32[384,128]{1,0:T(8,128)S(1)}, f32[384,128]{1,0:T(8,128)}, u32[]{:S(2)}) copy-start(f32[384,128]{1,0:T(8,128)} %refs_7_.1) | copy-start | bytes 589828
  30.2 6.4 %collective-permute-start.9 = (f32[520,128]{1,0:T(8,128)S(1)}, f32[520,128]{1,0:T(8,128)S(1)}, u32[]{:S(2)}, u32[]{:S(2)}) collective-permute-start(f32[520,128]{1,0:T(8,128)S(1)} %get-tuple-element.70.give_ref), channel_id=1, source_target_pairs={{0,16},{1,17},{2,18},{3,19},{4,20},{5,21},{6,22},{7,23},{8,24},{9,... | collective-permute-start | bytes 798728 | tf_op jit(solution)/shard_map/ppermute | solution.py:459
  72.6 5.7 %collective-permute-start.10 = (f32[512,128]{1,0:T(8,128)S(1)}, f32[512,128]{1,0:T(8,128)S(1)}, u32[]{:S(2)}, u32[]{:S(2)}) collective-permute-start(f32[512,128]{1,0:T(8,128)S(1)} %bitcast.10), channel_id=1, source_target_pairs={{0,16},{1,17},{2,18},{3,19},{4,20},{5,21},{6,22},{7,23},{8,24},{9,... | collective-permute-start | bytes 786440 | tf_op jit(solution)/shard_map/ppermute | solution.py:480

commit v7 on v6

--- a/solution.py
+++ b/solution.py
@@ -274,50 +274,48 @@
     loss_ref[...] = total[rows:]
 
 
-def last_kernel(
-    mine_ref, other_ref, losses_ref, target_in, grad_q_ref, grad_k_ref, loss_ref, target_ref, loss_row, sems
+def write_half(low, source_ref, grad_q_ref, grad_k_ref, sems, others=()):
+    tiles = source_ref.shape[0]
+    left = grad_q_ref.shape[0] - tiles
+    if low:
+        pairs = [(source_ref, grad_q_ref.at[pl.ds(0, tiles)])]
+    else:
+        pairs = [
+            (source_ref.at[pl.ds(0, left)], grad_q_ref.at[pl.ds(tiles, left)]),
+            (source_ref.at[pl.ds(left, tiles - left)], grad_k_ref),
+        ]
+    pairs += others
+    copies = [pltpu.make_async_copy(source, target, sems.at[j]) for j, (source, target) in enumerate(pairs)]
+    for copy in copies:
+        copy.start()
+    for copy in copies:
+        copy.wait()
+
+
+def mine_kernel(
+    mine_ref, losses_ref, target_in, grad_q_ref, grad_k_ref, loss_ref, target_ref, loss_row, sems
 ):
-    tiles = mine_ref.shape[0]
-    left = grad_q_ref.shape[0] - tiles
     own_seq = lax.axis_index("seq")
     core = lax.rem(own_seq, 2)
-
-    def grads(low_ref, high_ref):
-        pairs = (
-            (low_ref, grad_q_ref.at[pl.ds(0, tiles)]),
-            (high_ref.at[pl.ds(0, left)], grad_q_ref.at[pl.ds(tiles, left)]),
-            (high_ref.at[pl.ds(left, tiles - left)], grad_k_ref),
-        )
-        return [pltpu.make_async_copy(source, target, sems.at[j]) for j, (source, target) in enumerate(pairs)]
-
-    @pl.when(core == 0)
-    def _():
-        for copy in grads(mine_ref, other_ref):
-            copy.start()
-
-    @pl.when(core != 0)
-    def _():
-        for copy in grads(other_ref, mine_ref):
-            copy.start()
-
     losses = losses_ref[0:1, :]
     lane = lax.broadcasted_iota(jnp.int32, losses.shape, 1)
     loss_row[...] = jnp.sum(jnp.where(lane == own_seq, losses, 0.0), axis=1, keepdims=True)
-    rest = [
-        pltpu.make_async_copy(loss_row, loss_ref, sems.at[3]),
-        pltpu.make_async_copy(target_in, target_ref, sems.at[4]),
-    ]
-    for copy in rest:
-        copy.start()
-    for copy in grads(mine_ref, other_ref) + rest:
-        copy.wait()
+    others = [(loss_row, loss_ref), (target_in, target_ref)]
+    pl.when(core == 0)(lambda: write_half(True, mine_ref, grad_q_ref, grad_k_ref, sems, others))
+    pl.when(core != 0)(lambda: write_half(False, mine_ref, grad_q_ref, grad_k_ref, sems, others))
+
+
+def other_kernel(other_ref, grad_q_in, grad_k_in, grad_q_ref, grad_k_ref, sems):
+    core = lax.rem(lax.axis_index("seq"), 2)
+    pl.when(core == 0)(lambda: write_half(False, other_ref, grad_q_ref, grad_k_ref, sems))
+    pl.when(core != 0)(lambda: write_half(True, other_ref, grad_q_ref, grad_k_ref, sems))
 
 
 def f32(*shape):
     return jax.ShapeDtypeStruct(shape, jnp.float32)
 
 
-def call(kernel, out_shape, specs, name, scratch=(), cost=None, out_specs=None):
+def call(kernel, out_shape, specs, name, scratch=(), cost=None, out_specs=None, aliases={}):
     return pl.pallas_call(
         kernel,
         out_shape=out_shape,
@@ -326,6 +324,7 @@
         scratch_shapes=scratch,
         compiler_params=PARAMS,
         cost_estimate=cost,
+        input_output_aliases=aliases,
         name=name,
     )
 
@@ -479,14 +478,24 @@
     mine = lax.all_to_all(spread, every, 0, 0, axis_index_groups=planes, tiled=True).reshape(part, gate_width)
     other = lax.ppermute(mine, every, cores)
     tiled = (part // width, width, gate_width)
+    grads = (f32(heads, width, gate_width), f32(3, width, gate_width))
     grad_q, grad_k, loss, target = call(
-        last_kernel,
-        (f32(heads, width, gate_width), f32(3, width, gate_width), f32(1, 1), f32(*target.shape)),
-        [VMEM] * 4,
-        "last",
-        scratch=[pltpu.VMEM((1, 1), jnp.float32), pltpu.SemaphoreType.DMA((5,))],
+        mine_kernel,
+        grads + (f32(1, 1), f32(*target.shape)),
+        [VMEM] * 3,
+        "mine",
+        scratch=[pltpu.VMEM((1, 1), jnp.float32), pltpu.SemaphoreType.DMA((4,))],
         out_specs=(ANY,) * 4,
-    )(mine.reshape(tiled), other.reshape(tiled), losses, target)
+    )(mine.reshape(tiled), losses, target)
+    grad_q, grad_k = call(
+        other_kernel,
+        grads,
+        [VMEM, ANY, ANY],
+        "other",
+        scratch=[pltpu.SemaphoreType.DMA((2,))],
+        out_specs=(ANY,) * 2,
+        aliases={1: 0, 2: 1},
+    )(other.reshape(tiled), grad_q, grad_k)
     return (target[None, None], grad_q, grad_k.reshape(3 * width, gate_width), loss.reshape(1))
 
 

time: 79.6 us -> 79.5 us (level)
  waiting for transfers between devices: 4.5 us -> 3.69 us
    ppermute x1, waiting for transfers between devices: 1.16 us -> 0.34 us  [on_device(): other = lax.ppermute(mine, every, cores)]
  transfers between devices with their start and end apart: 11 -> 11, of which waited for: 6 -> 6; matrix products, arithmetic and copies ran while one was open for 0% -> 0% of each run, Pallas kernels for 8% -> 9%
where the time goes in v7:
time: 79.5 us; the launch traced here: 79.2 us
  blocking collectives  35.9 us (45%)
  starting transfers between devices  27.5 us (35%)
  Pallas kernels  10.2 us (13%)
  waiting for transfers between devices  3.69 us (5%)
  between operations  0.93 us (1%)
  local copies, waits for them, and re-layouts  0.89 us (1%)
    all_to_all x1, blocking collectives, on_device(): lax.all_to_all(parts, every, 0, 0, axis_index_groups=planes, tiled=True)  13.3 us
    all_to_all x1, blocking collectives, on_device(): lax.all_to_all(spread, 'ctx', 0, 0, axis_index_groups=[list(range(near)),...  12.4 us
    ppermute x5, starting transfers between devices, get(): lax.ppermute(x, 'ctx', [(j, j // near * near + (j - offset) % near) for j...  11.7 us
    all_to_all x1, blocking collectives, on_device(): lax.all_to_all(spread, every, 0, 0, axis_index_groups=planes, tiled=True)  10.3 us
    ppermute x4, starting transfers between devices, across(): lax.ppermute(x, 'ctx', [(j, (j + near) % ctx_count) for j in range(ctx_co...  6.03 us
    pallas_call x4, Pallas kernels, attend_to(): call(functools.partial(attend_kernel, layout), state + (f32(count * block...  5.64 us
    ppermute x1, starting transfers between devices, on_device(): got = lax.ppermute(give, every, cores)  5.19 us
    ppermute x1, starting transfers between devices, on_device(): other = lax.ppermute(mine, every, cores)  4.56 us
  transfers between devices with their start and end apart: 11, of which 6 were waited for; matrix products, arithmetic and copies ran while one was open for 0% of the time, Pallas kernels for 9%

profile of v7, /device:TPU:1, one launch (start us, length us, event | category | flops | bytes accessed | tf_op | source)
XLA Modules:
  0.0 79.2 jit_solution(7403166142623545894)
XLA Ops:
  0.6 6.5 %collective-permute-start = (bf16[256,128]{1,0:T(8,128)(2,1)}, bf16[256,128]{1,0:T(8,128)(2,1)S(1)}, u32[]{:S(2)}, u32[]{:S(2)}) collective-permute-start(bf16[256,128]{1,0:T(8,128)(2,1)} %bitcast.14), channel_id=1, source_target_pairs={{0,7},{1,0},{2,1},{3,2},{4,3},{5,4},{6,5},{7,6},{8,15},{9,8},{10,9... | collective-permute-start | bytes 196616 | tf_op jit(solution)/shard_map/ppermute | solution.py:346
  7.1 0.0 collective-permute-start.1
  7.1 2.8 %collective-permute-start.4 = (bf16[256,128]{1,0:T(8,128)(2,1)}, bf16[256,128]{1,0:T(8,128)(2,1)S(1)}, u32[]{:S(2)}, u32[]{:S(2)}) collective-permute-start(bf16[256,128]{1,0:T(8,128)(2,1)} %bitcast.16), channel_id=1, source_target_pairs={{0,4},{1,5},{2,6},{3,7},{4,0},{5,1},{6,2},{7,3},{8,12},{9,13},{10,... | collective-permute-start | bytes 196616 | tf_op jit(solution)/shard_map/ppermute | solution.py:346
  9.9 0.0 copy-start.3
  9.9 0.9 %copy-done.3 = bf16[1,256,128]{2,1,0:T(8,128)(2,1)S(1)} copy-done((bf16[1,256,128]{2,1,0:T(8,128)(2,1)S(1)}, bf16[1,256,128]{2,1,0:T(8,128)(2,1)}, u32[]{:S(2)}) %copy-start.3) | copy-done | bytes 65560
  10.8 0.0 copy-start.2
  10.8 0.0 copy-start.1
  10.8 0.0 collective-permute-done.refs_0_.a_ref
  10.8 1.5 %collective-permute-done.1.refs_1_.b_ref = bf16[256,128]{1,0:T(8,128)(2,1)S(1)} collective-permute-done((bf16[256,128]{1,0:T(8,128)(2,1)}, bf16[256,128]{1,0:T(8,128)(2,1)S(1)}, u32[]{:S(2)}, u32[]{:S(2)}) %collective-permute-start.1) | collective-permute-done | bytes 65568 | tf_op jit(solution)/shard_map/ppermute | solution.py:346
  12.3 0.1 collective-permute-start.2
  12.4 2.4 %collective-permute-start.3 = (bf16[512,128]{1,0:T(8,128)(2,1)S(1)}, bf16[512,128]{1,0:T(8,128)(2,1)S(1)}, u32[]{:S(2)}, u32[]{:S(2)}) collective-permute-start(bf16[512,128]{1,0:T(8,128)(2,1)S(1)} %get-tuple-element.51), channel_id=1, source_target_pairs={{0,2},{1,3},{2,4},{3,5},{4,6},{5,7},{6,0},{7,1},{8,10},{9,11},{10,... | collective-permute-start | bytes 393224 | tf_op jit(solution)/shard_map/ppermute | solution.py:346
  14.8 0.0 copy-start.4
  14.8 2.8 %collective-permute-start.5 = (bf16[768,128]{1,0:T(8,128)(2,1)S(1)}, bf16[768,128]{1,0:T(8,128)(2,1)S(1)}, u32[]{:S(2)}, u32[]{:S(2)}) collective-permute-start(bf16[768,128]{1,0:T(8,128)(2,1)S(1)} %pad_maximum_fusion.refs_4_), channel_id=1, source_target_pairs={{0,8},{1,9},{2,10},{3,11},{4,12},{5,13},{6,14},{7,15},{8,0},{9,1},... | collective-permute-start | bytes 589832 | tf_op jit(solution)/shard_map/ppermute | solution.py:349
  17.6 0.0 collective-permute-done.4.refs_6_
  17.6 0.2 collective-permute-start.6
  17.9 0.0 copy-done.2
  17.9 0.0 copy-done.1
  17.9 0.0 copy-done.4
  17.9 0.7 local.1
  18.6 1.3 %attend.4 = (f32[1,1280]{1,0:T(1,128)S(1)}, f32[8,1280]{1,0:T(8,128)S(1)}, f32[12,1280]{1,0:T(8,128)S(1)}, f32[12,384]{1,0:T(8,128)S(1)}) custom-call(bf16[5,256,256]{2,1,0:T(8,128)(2,1)S(1)} %get-tuple-element.44.refs_0_, f32[64,256]{1,0:T(8,128)S(1)} %get-tuple-element.45.refs_1_, f32[1,1280]{1,0:T(1,128)S(1)} %get-tuple-element.46.refs_2_, ...), custom_call_target="tpu_custom_call" | custom-call | flops 1200000000 | bytes 1000000 | tf_op jit(solution)/shard_map/attend/pallas_call | solution.py:391
  19.8 0.2 collective-permute-done.2.refs_4_
  20.1 2.7 %collective-permute-start.7 = (bf16[512,128]{1,0:T(8,128)(2,1)S(1)}, bf16[512,128]{1,0:T(8,128)(2,1)S(1)}, u32[]{:S(2)}, u32[]{:S(2)}) collective-permute-start(bf16[512,128]{1,0:T(8,128)(2,1)S(1)} %collective-permute-done.2.refs_4_), channel_id=1, source_target_pairs={{0,8},{1,9},{2,10},{3,11},{4,12},{5,13},{6,14},{7,15},{8,0},{9,1},... | collective-permute-start | bytes 393224 | tf_op jit(solution)/shard_map/ppermute | solution.py:349
  22.8 0.0 collective-permute-done.3.refs_5_
  22.8 0.2 collective-permute-start.8
  23.0 2.0 %attend.5 = (f32[1,1280]{1,0:T(1,128)S(1)}, f32[8,1280]{1,0:T(8,128)S(1)}, f32[20,1280]{1,0:T(8,128)S(1)}, f32[20,384]{1,0:T(8,128)S(1)}) custom-call(bf16[5,256,256]{2,1,0:T(8,128)(2,1)S(1)} %get-tuple-element.44.refs_0_, f32[64,256]{1,0:T(8,128)S(1)} %get-tuple-element.45.refs_1_, f32[1,1280]{1,0:T(1,128)S(1)} %get-tuple-element.48.refs_2_, ...), custom_call_target="tpu_custom_call" | custom-call | flops 1200000000 | bytes 1000000 | tf_op jit(solution)/shard_map/attend/pallas_call | solution.py:391
  25.0 0.0 collective-permute-done.6.refs_5_
  25.0 0.0 collective-permute-done.5.refs_4_
  25.1 1.5 %attend.6 = (f32[1,1280]{1,0:T(1,128)S(1)}, f32[8,1280]{1,0:T(8,128)S(1)}, f32[16,1280]{1,0:T(8,128)S(1)}, f32[16,384]{1,0:T(8,128)S(1)}) custom-call(bf16[5,256,256]{2,1,0:T(8,128)(2,1)S(1)} %get-tuple-element.44.refs_0_, f32[64,256]{1,0:T(8,128)S(1)} %get-tuple-element.45.refs_1_, f32[1,1280]{1,0:T(1,128)S(1)} %get-tuple-element.52.refs_2_, ...), custom_call_target="tpu_custom_call" | custom-call | flops 1200000000 | bytes 1000000 | tf_op jit(solution)/shard_map/attend/pallas_call | solution.py:391
  26.6 0.2 collective-permute-done.7.refs_4_
  26.8 0.0 copy-start
  26.8 0.9 %attend.7 = (f32[1,1280]{1,0:T(1,128)S(1)}, f32[8,1280]{1,0:T(8,128)S(1)}, f32[8,1280]{1,0:T(8,128)S(1)}, f32[8,384]{1,0:T(8,128)S(1)}) custom-call(bf16[5,256,256]{2,1,0:T(8,128)(2,1)S(1)} %get-tuple-element.44.refs_0_, f32[64,256]{1,0:T(8,128)S(1)} %get-tuple-element.45.refs_1_, f32[1,1280]{1,0:T(1,128)S(1)} %get-tuple-element.54.refs_2_, ...), custom_call_target="tpu_custom_call" | custom-call | flops 1200000000 | bytes 1000000 | tf_op jit(solution)/shard_map/attend/pallas_call | solution.py:391
  27.7 0.5 collective-permute-done.8.refs_9_
  28.2 0.0 copy-done
  28.2 1.9 %finish.1 = (f32[5,4,64]{2,1,0:T(4,128)S(1)}, f32[520,128]{1,0:T(8,128)S(1)}, f32[40,128]{1,0:T(8,128)S(1)}, f32[64,128]{1,0:T(8,128)S(1)}, f32[64,384]{1,0:T(8,128)S(1)}) custom-call(bf16[5,256,256]{2,1,0:T(8,128)(2,1)S(1)} %get-tuple-element.44.refs_0_, f32[64,256]{1,0:T(8,128)S(1)} %get-tuple-element.45.refs_1_, f32[1,1280]{1,0:T(1,128)S(1)} %get-tuple-element.56.refs_2_, ...), custom_call_target="tpu_custom_call" | custom-call | tf_op jit(solution)/shard_map/finish/pallas_call | solution.py:419
  30.2 5.2 %collective-permute-start.9 = (f32[520,128]{1,0:T(8,128)S(1)}, f32[520,128]{1,0:T(8,128)S(1)}, u32[]{:S(2)}, u32[]{:S(2)}) collective-permute-start(f32[520,128]{1,0:T(8,128)S(1)} %get-tuple-element.72.give_ref), channel_id=1, source_target_pairs={{0,16},{1,17},{2,18},{3,19},{4,20},{5,21},{6,22},{7,23},{8,24},{9,... | collective-permute-start | bytes 798728 | tf_op jit(solution)/shard_map/ppermute | solution.py:458
  35.4 0.3 keep.1.keep_ref
  35.7 0.8 %collective-permute-done.9.got_ref = f32[520,128]{1,0:T(8,128)S(1)} collective-permute-done((f32[520,128]{1,0:T(8,128)S(1)}, f32[520,128]{1,0:T(8,128)S(1)}, u32[]{:S(2)}, u32[]{:S(2)}) %collective-permute-start.9) | collective-permute-done | bytes 266272 | tf_op jit(solution)/shard_map/ppermute | solution.py:458
  36.6 13.3 %all_to_all.15.parts_ref = f32[16,40,128]{2,1,0:T(8,128)S(1)} all-to-all(f32[16,40,128]{2,1,0:T(8,128)S(1)} %fold.1), channel_id=1, replica_groups={{0,32,64,96,8,40,72,104,128,160,192,224,136,168,200,232},{1,33,65,97,9,..., dimensions={0} | all-to-all | bytes 655360 | tf_op jit(solution)/shard_map/all_to_all | solution.py:465
  49.9 12.4 %all_to_all.16.parts_ref = f32[8,40,128]{2,1,0:T(8,128)S(1)} all-to-all(f32[8,40,128]{2,1,0:T(8,128)S(1)} %sum.1), channel_id=1, replica_groups={{0,1,2,3,4,5,6,7},{8,9,10,11,12,13,14,15},{16,17,18,19,20,21,22,23},{24..., dimensions={0} | all-to-all | bytes 327680 | tf_op jit(solution)/shard_map/all_to_all | solution.py:467
  62.3 10.3 %all_to_all.17 = f32[16,32,128]{2,1,0:T(8,128)S(1)} all-to-all(f32[16,32,128]{2,1,0:T(8,128)S(1)} %get-tuple-element.73), channel_id=1, replica_groups={{0,32,64,96,8,40,72,104,128,160,192,224,136,168,200,232},{1,33,65,97,9,..., dimensions={0} | all-to-all | bytes 524288 | tf_op jit(solution)/shard_map/all_to_all | solution.py:478
  72.6 4.6 %collective-permute-start.10 = (f32[512,128]{1,0:T(8,128)S(1)}, f32[512,128]{1,0:T(8,128)S(1)}, u32[]{:S(2)}, u32[]{:S(2)}) collective-permute-start(f32[512,128]{1,0:T(8,128)S(1)} %bitcast.10), channel_id=1, source_target_pairs={{0,16},{1,17},{2,18},{3,19},{4,20},{5,21},{6,22},{7,23},{8,24},{9,... | collective-permute-start | bytes 786440 | tf_op jit(solution)/shard_map/ppermute | solution.py:479
  77.2 0.8 %mine.1 = (f32[5,128,128]{2,1,0:T(8,128)}, f32[3,128,128]{2,1,0:T(8,128)}, f32[1,1]{1,0:T(1,128)}, f32[5,4,64]{2,1,0:T(4,128)}) custom-call(f32[4,128,128]{2,1,0:T(8,128)S(1)} %bitcast.11, f32[8,128]{1,0:T(8,128)S(1)} %get-tuple-element.74.losses_ref, f32[5,4,64]{2,1,0:T(4,128)S(1)} %get-tuple-element.75.target_in), custom_call_target="tpu_custom_call" | custom-call | tf_op jit(solution)/shard_map/mine/pallas_call | solution.py:482
  78.0 0.3 collective-permute-done.10
  78.3 0.7 other.1
  (6 shorter events, 0.1 us)
Async XLA Ops:
  0.6 10.2 %collective-permute-start = (bf16[256,128]{1,0:T(8,128)(2,1)}, bf16[256,128]{1,0:T(8,128)(2,1)S(1)}, u32[]{:S(2)}, u32[]{:S(2)}) collective-permute-start(bf16[256,128]{1,0:T(8,128)(2,1)} %bitcast.14), channel_id=1, source_target_pairs={{0,7},{1,0},{2,1},{3,2},{4,3},{5,4},{6,5},{7,6},{8,15},{9,8},{10,9... | collective-permute-start | bytes 196616 | tf_op jit(solution)/shard_map/ppermute | solution.py:346
  7.1 5.2 %collective-permute-start.1 = (bf16[256,128]{1,0:T(8,128)(2,1)}, bf16[256,128]{1,0:T(8,128)(2,1)S(1)}, u32[]{:S(2)}, u32[]{:S(2)}) collective-permute-start(bf16[256,128]{1,0:T(8,128)(2,1)} %bitcast.15), channel_id=1, source_target_pairs={{0,1},{1,2},{2,3},{3,4},{4,5},{5,6},{6,7},{7,0},{8,9},{9,10},{10,1... | collective-permute-start | bytes 196616 | tf_op jit(solution)/shard_map/ppermute | solution.py:346
  7.1 10.5 %collective-permute-start.4 = (bf16[256,128]{1,0:T(8,128)(2,1)}, bf16[256,128]{1,0:T(8,128)(2,1)S(1)}, u32[]{:S(2)}, u32[]{:S(2)}) collective-permute-start(bf16[256,128]{1,0:T(8,128)(2,1)} %bitcast.16), channel_id=1, source_target_pairs={{0,4},{1,5},{2,6},{3,7},{4,0},{5,1},{6,2},{7,3},{8,12},{9,13},{10,... | collective-permute-start | bytes 196616 | tf_op jit(solution)/shard_map/ppermute | solution.py:346
  9.9 0.9 %copy-start.3 = (bf16[1,256,128]{2,1,0:T(8,128)(2,1)S(1)}, bf16[1,256,128]{2,1,0:T(8,128)(2,1)}, u32[]{:S(2)}) copy-start(bf16[1,256,128]{2,1,0:T(8,128)(2,1)} %param.7) | copy-start | bytes 196612
  10.8 7.1 %copy-start.2 = (f32[5,128,128]{2,1,0:T(8,128)S(1)}, f32[5,128,128]{2,1,0:T(8,128)}, u32[]{:S(2)}) copy-start(f32[5,128,128]{2,1,0:T(8,128)} %wq_ref.1) | copy-start | bytes 983044
  10.8 7.1 %copy-start.1 = (bf16[1,256,5,128]{3,1,2,0:T(8,128)(2,1)S(1)}, bf16[1,256,5,128]{3,1,2,0:T(8,128)(2,1)}, u32[]{:S(2)}) copy-start(bf16[1,256,5,128]{3,1,2,0:T(8,128)(2,1)} %param.6) | copy-start | bytes 983044
  12.3 7.7 %collective-permute-start.2 = (bf16[512,128]{1,0:T(8,128)(2,1)S(1)}, bf16[512,128]{1,0:T(8,128)(2,1)S(1)}, u32[]{:S(2)}, u32[]{:S(2)}) collective-permute-start(bf16[512,128]{1,0:T(8,128)(2,1)S(1)} %get-tuple-element.50), channel_id=1, source_target_pairs={{0,6},{1,7},{2,0},{3,1},{4,2},{5,3},{6,4},{7,5},{8,14},{9,15},{10,... | collective-permute-start | bytes 393224 | tf_op jit(solution)/shard_map/ppermute | solution.py:346
  12.4 10.4 %collective-permute-start.3 = (bf16[512,128]{1,0:T(8,128)(2,1)S(1)}, bf16[512,128]{1,0:T(8,128)(2,1)S(1)}, u32[]{:S(2)}, u32[]{:S(2)}) collective-permute-start(bf16[512,128]{1,0:T(8,128)(2,1)S(1)} %get-tuple-element.51), channel_id=1, source_target_pairs={{0,2},{1,3},{2,4},{3,5},{4,6},{5,7},{6,0},{7,1},{8,10},{9,11},{10,... | collective-permute-start | bytes 393224 | tf_op jit(solution)/shard_map/ppermute | solution.py:346
  14.8 3.1 %copy-start.4 = (s32[1,32]{1,0:T(1,128)S(1)}, s32[1,32]{1,0:T(1,128)}, u32[]{:S(2)}) copy-start(s32[1,32]{1,0:T(1,128)} %order_ref.1) | copy-start | bytes 388
  14.8 10.2 %collective-permute-start.5 = (bf16[768,128]{1,0:T(8,128)(2,1)S(1)}, bf16[768,128]{1,0:T(8,128)(2,1)S(1)}, u32[]{:S(2)}, u32[]{:S(2)}) collective-permute-start(bf16[768,128]{1,0:T(8,128)(2,1)S(1)} %pad_maximum_fusion.refs_4_), channel_id=1, source_target_pairs={{0,8},{1,9},{2,10},{3,11},{4,12},{5,13},{6,14},{7,15},{8,0},{9,1},... | collective-permute-start | bytes 589832 | tf_op jit(solution)/shard_map/ppermute | solution.py:349
  17.6 7.4 %collective-permute-start.6 = (bf16[256,128]{1,0:T(8,128)(2,1)S(1)}, bf16[256,128]{1,0:T(8,128)(2,1)S(1)}, u32[]{:S(2)}, u32[]{:S(2)}) collective-permute-start(bf16[256,128]{1,0:T(8,128)(2,1)S(1)} %collective-permute-done.4.refs_6_), channel_id=1, source_target_pairs={{0,8},{1,9},{2,10},{3,11},{4,12},{5,13},{6,14},{7,15},{8,0},{9,1},... | collective-permute-start | bytes 196616 | tf_op jit(solution)/shard_map/ppermute | solution.py:349
  20.1 6.8 %collective-permute-start.7 = (bf16[512,128]{1,0:T(8,128)(2,1)S(1)}, bf16[512,128]{1,0:T(8,128)(2,1)S(1)}, u32[]{:S(2)}, u32[]{:S(2)}) collective-permute-start(bf16[512,128]{1,0:T(8,128)(2,1)S(1)} %collective-permute-done.2.refs_4_), channel_id=1, source_target_pairs={{0,8},{1,9},{2,10},{3,11},{4,12},{5,13},{6,14},{7,15},{8,0},{9,1},... | collective-permute-start | bytes 393224 | tf_op jit(solution)/shard_map/ppermute | solution.py:349
  22.8 5.4 %collective-permute-start.8 = (bf16[512,128]{1,0:T(8,128)(2,1)S(1)}, bf16[512,128]{1,0:T(8,128)(2,1)S(1)}, u32[]{:S(2)}, u32[]{:S(2)}) collective-permute-start(bf16[512,128]{1,0:T(8,128)(2,1)S(1)} %collective-permute-done.3.refs_5_), channel_id=1, source_target_pairs={{0,8},{1,9},{2,10},{3,11},{4,12},{5,13},{6,14},{7,15},{8,0},{9,1},... | collective-permute-start | bytes 393224 | tf_op jit(solution)/shard_map/ppermute | solution.py:349
  26.8 1.4 %copy-start = (f32[384,128]{1,0:T(8,128)S(1)}, f32[384,128]{1,0:T(8,128)}, u32[]{:S(2)}) copy-start(f32[384,128]{1,0:T(8,128)} %refs_7_.1) | copy-start | bytes 589828
  30.2 6.4 %collective-permute-start.9 = (f32[520,128]{1,0:T(8,128)S(1)}, f32[520,128]{1,0:T(8,128)S(1)}, u32[]{:S(2)}, u32[]{:S(2)}) collective-permute-start(f32[520,128]{1,0:T(8,128)S(1)} %get-tuple-element.72.give_ref), channel_id=1, source_target_pairs={{0,16},{1,17},{2,18},{3,19},{4,20},{5,21},{6,22},{7,23},{8,24},{9,... | collective-permute-start | bytes 798728 | tf_op jit(solution)/shard_map/ppermute | solution.py:458
  72.6 5.7 %collective-permute-start.10 = (f32[512,128]{1,0:T(8,128)S(1)}, f32[512,128]{1,0:T(8,128)S(1)}, u32[]{:S(2)}, u32[]{:S(2)}) collective-permute-start(f32[512,128]{1,0:T(8,128)S(1)} %bitcast.10), channel_id=1, source_target_pairs={{0,16},{1,17},{2,18},{3,19},{4,20},{5,21},{6,22},{7,23},{8,24},{9,... | collective-permute-start | bytes 786440 | tf_op jit(solution)/shard_map/ppermute | solution.py:479

commit v8 on v6

--- a/solution.py
+++ b/solution.py
@@ -149,11 +149,10 @@
     out_ref[...] = in_ref[...]
 
 
-def pair_kernel(own_ref, a_ref, b_ref, ahead_ref, behind_ref):
+def pair_kernel(own_ref, other_ref, out_ref):
     rows = own_ref.shape[0]
-    for out_ref, other_ref in ((ahead_ref, a_ref), (behind_ref, b_ref)):
-        out_ref[0:rows, :] = own_ref[...]
-        out_ref[rows:, :] = other_ref[...]
+    out_ref[0:rows, :] = own_ref[...]
+    out_ref[rows:, :] = other_ref[...]
 
 
 def gradient_half(low, pooled_ref, gate_q_grad_ref, pool_ref, gate_k_grad_ref, out_ref):
@@ -359,8 +358,9 @@
         cost=pl.CostEstimate(flops=10**9, bytes_accessed=10**6, transcendentals=10**6),
     )(own_keys)
     two_parts = jax.ShapeDtypeStruct((2 * tok_rows, width), keys.dtype)
-    ahead, behind = call(pair_kernel, (two_parts, two_parts), [VMEM] * 3, "pair")(own_copy, step[1], step[-1])
+    (ahead,) = call(pair_kernel, (two_parts,), [VMEM] * 2, "ahead")(own_copy, step[1])
     ahead = get(ahead, 2)
+    (behind,) = call(pair_kernel, (two_parts,), [VMEM] * 2, "behind")(own_copy, step[-1])
     behind = get(behind, near - 2)
     mid = jnp.concatenate([own_copy, step[1], step[-1]], axis=0)
     mid_far = across(mid)

time: 79.6 us -> 78.3 us (0.984)
  starting transfers between devices: 27.5 us -> 24.6 us
  waiting for transfers between devices: 4.5 us -> 6.53 us
    ppermute x1, starting transfers between devices: 5.19 us -> 2.77 us  [on_device(): got = lax.ppermute(give, every, cores)]
    ppermute x5, waiting for transfers between devices: 1.72 us -> 3.3 us  [get(): lax.ppermute(x, 'ctx', [(j, j // near * near + (j - offset) % near) for j...]
    ppermute x5, starting transfers between devices: 11.7 us -> 10.5 us  [get(): lax.ppermute(x, 'ctx', [(j, j // near * near + (j - offset) % near) for j...]
    all_to_all x1, blocking collectives: 12.4 us -> 11.5 us  [on_device(): lax.all_to_all(spread, 'ctx', 0, 0, axis_index_groups=[list(range(near)),...]
  transfers between devices with their start and end apart: 11 -> 11, of which waited for: 6 -> 5; matrix products, arithmetic and copies ran while one was open for 0% -> 0% of each run, Pallas kernels for 8% -> 9%
where the time goes in v8:
time: 78.3 us; the launch traced here: 78 us
  blocking collectives  35.5 us (45%)
  starting transfers between devices  24.6 us (31%)
  Pallas kernels  9.55 us (12%)
  waiting for transfers between devices  6.53 us (8%)
  between operations  0.94 us (1%)
  local copies, waits for them, and re-layouts  0.9 us (1%)
    all_to_all x1, blocking collectives, on_device(): lax.all_to_all(parts, every, 0, 0, axis_index_groups=planes, tiled=True)  13.7 us
    all_to_all x1, blocking collectives, on_device(): lax.all_to_all(spread, 'ctx', 0, 0, axis_index_groups=[list(range(near)),...  11.5 us
    ppermute x5, starting transfers between devices, get(): lax.ppermute(x, 'ctx', [(j, j // near * near + (j - offset) % near) for j...  10.5 us
    all_to_all x1, blocking collectives, on_device(): lax.all_to_all(spread, every, 0, 0, axis_index_groups=planes, tiled=True)  10.3 us
    ppermute x4, starting transfers between devices, across(): lax.ppermute(x, 'ctx', [(j, (j + near) % ctx_count) for j in range(ctx_co...  6.71 us
    pallas_call x4, Pallas kernels, attend_to(): call(functools.partial(attend_kernel, layout), state + (f32(count * block...  5.66 us
    ppermute x1, starting transfers between devices, on_device(): other = lax.ppermute(mine, every, cores)  4.56 us
    ppermute x5, waiting for transfers between devices, get(): lax.ppermute(x, 'ctx', [(j, j // near * near + (j - offset) % near) for j...  3.3 us
  transfers between devices with their start and end apart: 11, of which 5 were waited for; matrix products, arithmetic and copies ran while one was open for 0% of the time, Pallas kernels for 9%

profile of v8, /device:TPU:1, one launch (start us, length us, event | category | flops | bytes accessed | tf_op | source)
XLA Modules:
  0.0 78.0 jit_solution(16083194429123270303)
XLA Ops:
  0.6 6.5 %collective-permute-start = (bf16[256,128]{1,0:T(8,128)(2,1)}, bf16[256,128]{1,0:T(8,128)(2,1)S(1)}, u32[]{:S(2)}, u32[]{:S(2)}) collective-permute-start(bf16[256,128]{1,0:T(8,128)(2,1)} %bitcast.14), channel_id=1, source_target_pairs={{0,7},{1,0},{2,1},{3,2},{4,3},{5,4},{6,5},{7,6},{8,15},{9,8},{10,9... | collective-permute-start | bytes 196616 | tf_op jit(solution)/shard_map/ppermute | solution.py:346
  7.1 0.0 collective-permute-start.1
  7.1 2.8 %collective-permute-start.4 = (bf16[256,128]{1,0:T(8,128)(2,1)}, bf16[256,128]{1,0:T(8,128)(2,1)S(1)}, u32[]{:S(2)}, u32[]{:S(2)}) collective-permute-start(bf16[256,128]{1,0:T(8,128)(2,1)} %bitcast.16), channel_id=1, source_target_pairs={{0,4},{1,5},{2,6},{3,7},{4,0},{5,1},{6,2},{7,3},{8,12},{9,13},{10,... | collective-permute-start | bytes 196616 | tf_op jit(solution)/shard_map/ppermute | solution.py:346
  9.9 0.0 copy-start.3
  9.9 0.9 %copy-done.3 = bf16[1,256,128]{2,1,0:T(8,128)(2,1)S(1)} copy-done((bf16[1,256,128]{2,1,0:T(8,128)(2,1)S(1)}, bf16[1,256,128]{2,1,0:T(8,128)(2,1)}, u32[]{:S(2)}) %copy-start.3) | copy-done | bytes 65560
  10.8 0.0 collective-permute-done.refs_0_.other_ref
  10.8 0.0 copy-start.1
  10.8 0.0 copy-start.2
  10.8 0.2 collective-permute-start.2
  11.0 1.3 %collective-permute-done.1.refs_1_.other_ref = bf16[256,128]{1,0:T(8,128)(2,1)S(1)} collective-permute-done((bf16[256,128]{1,0:T(8,128)(2,1)}, bf16[256,128]{1,0:T(8,128)(2,1)S(1)}, u32[]{:S(2)}, u32[]{:S(2)}) %collective-permute-start.1) | collective-permute-done | bytes 65568 | tf_op jit(solution)/shard_map/ppermute | solution.py:346
  12.3 1.1 %collective-permute-start.3 = (bf16[512,128]{1,0:T(8,128)(2,1)S(1)}, bf16[512,128]{1,0:T(8,128)(2,1)S(1)}, u32[]{:S(2)}, u32[]{:S(2)}) collective-permute-start(bf16[512,128]{1,0:T(8,128)(2,1)S(1)} %behind.1), channel_id=1, source_target_pairs={{0,2},{1,3},{2,4},{3,5},{4,6},{5,7},{6,0},{7,1},{8,10},{9,11},{10,... | collective-permute-start | bytes 393224 | tf_op jit(solution)/shard_map/ppermute | solution.py:346
  13.4 0.0 copy-start.4
  13.4 2.8 %collective-permute-start.5 = (bf16[768,128]{1,0:T(8,128)(2,1)S(1)}, bf16[768,128]{1,0:T(8,128)(2,1)S(1)}, u32[]{:S(2)}, u32[]{:S(2)}) collective-permute-start(bf16[768,128]{1,0:T(8,128)(2,1)S(1)} %pad_maximum_fusion.refs_4_), channel_id=1, source_target_pairs={{0,8},{1,9},{2,10},{3,11},{4,12},{5,13},{6,14},{7,15},{8,0},{9,1},... | collective-permute-start | bytes 589832 | tf_op jit(solution)/shard_map/ppermute | solution.py:349
  16.2 0.0 collective-permute-done.4.refs_6_
  16.2 0.9 %collective-permute-start.6 = (bf16[256,128]{1,0:T(8,128)(2,1)S(1)}, bf16[256,128]{1,0:T(8,128)(2,1)S(1)}, u32[]{:S(2)}, u32[]{:S(2)}) collective-permute-start(bf16[256,128]{1,0:T(8,128)(2,1)S(1)} %collective-permute-done.4.refs_6_), channel_id=1, source_target_pairs={{0,8},{1,9},{2,10},{3,11},{4,12},{5,13},{6,14},{7,15},{8,0},{9,1},... | collective-permute-start | bytes 196616 | tf_op jit(solution)/shard_map/ppermute | solution.py:349
  17.2 0.0 copy-done.1
  17.2 0.0 copy-done.2
  17.2 0.0 copy-done.4
  17.2 0.7 local.1
  17.9 1.3 %attend.4 = (f32[1,1280]{1,0:T(1,128)S(1)}, f32[8,1280]{1,0:T(8,128)S(1)}, f32[12,1280]{1,0:T(8,128)S(1)}, f32[12,384]{1,0:T(8,128)S(1)}) custom-call(bf16[5,256,256]{2,1,0:T(8,128)(2,1)S(1)} %get-tuple-element.40.refs_0_, f32[64,256]{1,0:T(8,128)S(1)} %get-tuple-element.41.refs_1_, f32[1,1280]{1,0:T(1,128)S(1)} %get-tuple-element.42.refs_2_, ...), custom_call_target="tpu_custom_call" | custom-call | flops 1200000000 | bytes 1000000 | tf_op jit(solution)/shard_map/attend/pallas_call | solution.py:392
  19.1 2.0 %collective-permute-done.2.refs_4_ = bf16[512,128]{1,0:T(8,128)(2,1)S(1)} collective-permute-done((bf16[512,128]{1,0:T(8,128)(2,1)S(1)}, bf16[512,128]{1,0:T(8,128)(2,1)S(1)}, u32[]{:S(2)}, u32[]{:S(2)}) %collective-permute-start.2) | collective-permute-done | bytes 131104 | tf_op jit(solution)/shard_map/ppermute | solution.py:346
  21.1 2.7 %collective-permute-start.7 = (bf16[512,128]{1,0:T(8,128)(2,1)S(1)}, bf16[512,128]{1,0:T(8,128)(2,1)S(1)}, u32[]{:S(2)}, u32[]{:S(2)}) collective-permute-start(bf16[512,128]{1,0:T(8,128)(2,1)S(1)} %collective-permute-done.2.refs_4_), channel_id=1, source_target_pairs={{0,8},{1,9},{2,10},{3,11},{4,12},{5,13},{6,14},{7,15},{8,0},{9,1},... | collective-permute-start | bytes 393224 | tf_op jit(solution)/shard_map/ppermute | solution.py:349
  23.9 0.0 collective-permute-done.3.refs_5_
  23.9 0.2 collective-permute-start.8
  24.1 2.0 %attend.5 = (f32[1,1280]{1,0:T(1,128)S(1)}, f32[8,1280]{1,0:T(8,128)S(1)}, f32[20,1280]{1,0:T(8,128)S(1)}, f32[20,384]{1,0:T(8,128)S(1)}) custom-call(bf16[5,256,256]{2,1,0:T(8,128)(2,1)S(1)} %get-tuple-element.40.refs_0_, f32[64,256]{1,0:T(8,128)S(1)} %get-tuple-element.41.refs_1_, f32[1,1280]{1,0:T(1,128)S(1)} %get-tuple-element.44.refs_2_, ...), custom_call_target="tpu_custom_call" | custom-call | flops 1200000000 | bytes 1000000 | tf_op jit(solution)/shard_map/attend/pallas_call | solution.py:392
  26.1 0.0 collective-permute-done.6.refs_5_
  26.1 0.0 collective-permute-done.5.refs_4_
  26.1 1.5 %attend.6 = (f32[1,1280]{1,0:T(1,128)S(1)}, f32[8,1280]{1,0:T(8,128)S(1)}, f32[16,1280]{1,0:T(8,128)S(1)}, f32[16,384]{1,0:T(8,128)S(1)}) custom-call(bf16[5,256,256]{2,1,0:T(8,128)(2,1)S(1)} %get-tuple-element.40.refs_0_, f32[64,256]{1,0:T(8,128)S(1)} %get-tuple-element.41.refs_1_, f32[1,1280]{1,0:T(1,128)S(1)} %get-tuple-element.46.refs_2_, ...), custom_call_target="tpu_custom_call" | custom-call | flops 1200000000 | bytes 1000000 | tf_op jit(solution)/shard_map/attend/pallas_call | solution.py:392
  27.7 0.0 collective-permute-done.7.refs_4_
  27.7 0.0 copy-start
  27.7 0.9 %attend.7 = (f32[1,1280]{1,0:T(1,128)S(1)}, f32[8,1280]{1,0:T(8,128)S(1)}, f32[8,1280]{1,0:T(8,128)S(1)}, f32[8,384]{1,0:T(8,128)S(1)}) custom-call(bf16[5,256,256]{2,1,0:T(8,128)(2,1)S(1)} %get-tuple-element.40.refs_0_, f32[64,256]{1,0:T(8,128)S(1)} %get-tuple-element.41.refs_1_, f32[1,1280]{1,0:T(1,128)S(1)} %get-tuple-element.48.refs_2_, ...), custom_call_target="tpu_custom_call" | custom-call | flops 1200000000 | bytes 1000000 | tf_op jit(solution)/shard_map/attend/pallas_call | solution.py:392
  28.6 1.2 %collective-permute-done.8.refs_9_ = bf16[512,128]{1,0:T(8,128)(2,1)S(1)} collective-permute-done((bf16[512,128]{1,0:T(8,128)(2,1)S(1)}, bf16[512,128]{1,0:T(8,128)(2,1)S(1)}, u32[]{:S(2)}, u32[]{:S(2)}) %collective-permute-start.8) | collective-permute-done | bytes 131104 | tf_op jit(solution)/shard_map/ppermute | solution.py:349
  29.8 0.0 copy-done
  29.8 1.9 %finish.1 = (f32[5,4,64]{2,1,0:T(4,128)S(1)}, f32[520,128]{1,0:T(8,128)S(1)}, f32[40,128]{1,0:T(8,128)S(1)}, f32[64,128]{1,0:T(8,128)S(1)}, f32[64,384]{1,0:T(8,128)S(1)}) custom-call(bf16[5,256,256]{2,1,0:T(8,128)(2,1)S(1)} %get-tuple-element.40.refs_0_, f32[64,256]{1,0:T(8,128)S(1)} %get-tuple-element.41.refs_1_, f32[1,1280]{1,0:T(1,128)S(1)} %get-tuple-element.50.refs_2_, ...), custom_call_target="tpu_custom_call" | custom-call | tf_op jit(solution)/shard_map/finish/pallas_call | solution.py:420
  31.7 2.8 %collective-permute-start.9 = (f32[520,128]{1,0:T(8,128)S(1)}, f32[520,128]{1,0:T(8,128)S(1)}, u32[]{:S(2)}, u32[]{:S(2)}) collective-permute-start(f32[520,128]{1,0:T(8,128)S(1)} %get-tuple-element.66.give_ref), channel_id=1, source_target_pairs={{0,16},{1,17},{2,18},{3,19},{4,20},{5,21},{6,22},{7,23},{8,24},{9,... | collective-permute-start | bytes 798728 | tf_op jit(solution)/shard_map/ppermute | solution.py:459
  34.5 0.3 keep.1.keep_ref
  34.8 0.9 %collective-permute-done.9.got_ref = f32[520,128]{1,0:T(8,128)S(1)} collective-permute-done((f32[520,128]{1,0:T(8,128)S(1)}, f32[520,128]{1,0:T(8,128)S(1)}, u32[]{:S(2)}, u32[]{:S(2)}) %collective-permute-start.9) | collective-permute-done | bytes 266272 | tf_op jit(solution)/shard_map/ppermute | solution.py:459
  35.7 13.7 %all_to_all.15.parts_ref = f32[16,40,128]{2,1,0:T(8,128)S(1)} all-to-all(f32[16,40,128]{2,1,0:T(8,128)S(1)} %fold.1), channel_id=1, replica_groups={{0,32,64,96,8,40,72,104,128,160,192,224,136,168,200,232},{1,33,65,97,9,..., dimensions={0} | all-to-all | bytes 655360 | tf_op jit(solution)/shard_map/all_to_all | solution.py:466
  49.5 11.5 %all_to_all.16.parts_ref = f32[8,40,128]{2,1,0:T(8,128)S(1)} all-to-all(f32[8,40,128]{2,1,0:T(8,128)S(1)} %sum.1), channel_id=1, replica_groups={{0,1,2,3,4,5,6,7},{8,9,10,11,12,13,14,15},{16,17,18,19,20,21,22,23},{24..., dimensions={0} | all-to-all | bytes 327680 | tf_op jit(solution)/shard_map/all_to_all | solution.py:468
  61.0 10.3 %all_to_all.17 = f32[16,32,128]{2,1,0:T(8,128)S(1)} all-to-all(f32[16,32,128]{2,1,0:T(8,128)S(1)} %get-tuple-element.67), channel_id=1, replica_groups={{0,32,64,96,8,40,72,104,128,160,192,224,136,168,200,232},{1,33,65,97,9,..., dimensions={0} | all-to-all | bytes 524288 | tf_op jit(solution)/shard_map/all_to_all | solution.py:479
  71.3 4.6 %collective-permute-start.10 = (f32[512,128]{1,0:T(8,128)S(1)}, f32[512,128]{1,0:T(8,128)S(1)}, u32[]{:S(2)}, u32[]{:S(2)}) collective-permute-start(f32[512,128]{1,0:T(8,128)S(1)} %bitcast.10), channel_id=1, source_target_pairs={{0,16},{1,17},{2,18},{3,19},{4,20},{5,21},{6,22},{7,23},{8,24},{9,... | collective-permute-start | bytes 786440 | tf_op jit(solution)/shard_map/ppermute | solution.py:480
  75.9 1.2 %collective-permute-done.10 = f32[512,128]{1,0:T(8,128)S(1)} collective-permute-done((f32[512,128]{1,0:T(8,128)S(1)}, f32[512,128]{1,0:T(8,128)S(1)}, u32[]{:S(2)}, u32[]{:S(2)}) %collective-permute-start.10) | collective-permute-done | bytes 262176 | tf_op jit(solution)/shard_map/ppermute | solution.py:480
  77.0 0.8 %last.1 = (f32[5,128,128]{2,1,0:T(8,128)}, f32[3,128,128]{2,1,0:T(8,128)}, f32[1,1]{1,0:T(1,128)}, f32[5,4,64]{2,1,0:T(4,128)}) custom-call(f32[4,128,128]{2,1,0:T(8,128)S(1)} %bitcast.11, f32[4,128,128]{2,1,0:T(8,128)S(1)} %bitcast.12, f32[8,128]{1,0:T(8,128)S(1)} %get-tuple-element.68.losses_ref, f32[5,4,64]{2,1,0:T(4,128)S(1)} %get-tuple-element.69.target_in), custom_call_target="tpu_custom_call" | custom-call | tf_op jit(solution)/shard_map/last/pallas_call | solution.py:482
  (7 shorter events, 0.1 us)
Async XLA Ops:
  0.6 10.2 %collective-permute-start = (bf16[256,128]{1,0:T(8,128)(2,1)}, bf16[256,128]{1,0:T(8,128)(2,1)S(1)}, u32[]{:S(2)}, u32[]{:S(2)}) collective-permute-start(bf16[256,128]{1,0:T(8,128)(2,1)} %bitcast.14), channel_id=1, source_target_pairs={{0,7},{1,0},{2,1},{3,2},{4,3},{5,4},{6,5},{7,6},{8,15},{9,8},{10,9... | collective-permute-start | bytes 196616 | tf_op jit(solution)/shard_map/ppermute | solution.py:346
  7.1 5.2 %collective-permute-start.1 = (bf16[256,128]{1,0:T(8,128)(2,1)}, bf16[256,128]{1,0:T(8,128)(2,1)S(1)}, u32[]{:S(2)}, u32[]{:S(2)}) collective-permute-start(bf16[256,128]{1,0:T(8,128)(2,1)} %bitcast.15), channel_id=1, source_target_pairs={{0,1},{1,2},{2,3},{3,4},{4,5},{5,6},{6,7},{7,0},{8,9},{9,10},{10,1... | collective-permute-start | bytes 196616 | tf_op jit(solution)/shard_map/ppermute | solution.py:346
  7.1 9.1 %collective-permute-start.4 = (bf16[256,128]{1,0:T(8,128)(2,1)}, bf16[256,128]{1,0:T(8,128)(2,1)S(1)}, u32[]{:S(2)}, u32[]{:S(2)}) collective-permute-start(bf16[256,128]{1,0:T(8,128)(2,1)} %bitcast.16), channel_id=1, source_target_pairs={{0,4},{1,5},{2,6},{3,7},{4,0},{5,1},{6,2},{7,3},{8,12},{9,13},{10,... | collective-permute-start | bytes 196616 | tf_op jit(solution)/shard_map/ppermute | solution.py:346
  9.9 0.9 %copy-start.3 = (bf16[1,256,128]{2,1,0:T(8,128)(2,1)S(1)}, bf16[1,256,128]{2,1,0:T(8,128)(2,1)}, u32[]{:S(2)}) copy-start(bf16[1,256,128]{2,1,0:T(8,128)(2,1)} %param.7) | copy-start | bytes 196612
  10.8 6.3 %copy-start.1 = (bf16[1,256,5,128]{3,1,2,0:T(8,128)(2,1)S(1)}, bf16[1,256,5,128]{3,1,2,0:T(8,128)(2,1)}, u32[]{:S(2)}) copy-start(bf16[1,256,5,128]{3,1,2,0:T(8,128)(2,1)} %param.6) | copy-start | bytes 983044
  10.8 6.3 %copy-start.2 = (f32[5,128,128]{2,1,0:T(8,128)S(1)}, f32[5,128,128]{2,1,0:T(8,128)}, u32[]{:S(2)}) copy-start(f32[5,128,128]{2,1,0:T(8,128)} %wq_ref.1) | copy-start | bytes 983044
  10.8 10.3 %collective-permute-start.2 = (bf16[512,128]{1,0:T(8,128)(2,1)S(1)}, bf16[512,128]{1,0:T(8,128)(2,1)S(1)}, u32[]{:S(2)}, u32[]{:S(2)}) collective-permute-start(bf16[512,128]{1,0:T(8,128)(2,1)S(1)} %ahead.1), channel_id=1, source_target_pairs={{0,6},{1,7},{2,0},{3,1},{4,2},{5,3},{6,4},{7,5},{8,14},{9,15},{10,... | collective-permute-start | bytes 393224 | tf_op jit(solution)/shard_map/ppermute | solution.py:346
  12.3 11.6 %collective-permute-start.3 = (bf16[512,128]{1,0:T(8,128)(2,1)S(1)}, bf16[512,128]{1,0:T(8,128)(2,1)S(1)}, u32[]{:S(2)}, u32[]{:S(2)}) collective-permute-start(bf16[512,128]{1,0:T(8,128)(2,1)S(1)} %behind.1), channel_id=1, source_target_pairs={{0,2},{1,3},{2,4},{3,5},{4,6},{5,7},{6,0},{7,1},{8,10},{9,11},{10,... | collective-permute-start | bytes 393224 | tf_op jit(solution)/shard_map/ppermute | solution.py:346
  13.4 3.8 %copy-start.4 = (s32[1,32]{1,0:T(1,128)S(1)}, s32[1,32]{1,0:T(1,128)}, u32[]{:S(2)}) copy-start(s32[1,32]{1,0:T(1,128)} %order_ref.1) | copy-start | bytes 388
  13.4 12.7 %collective-permute-start.5 = (bf16[768,128]{1,0:T(8,128)(2,1)S(1)}, bf16[768,128]{1,0:T(8,128)(2,1)S(1)}, u32[]{:S(2)}, u32[]{:S(2)}) collective-permute-start(bf16[768,128]{1,0:T(8,128)(2,1)S(1)} %pad_maximum_fusion.refs_4_), channel_id=1, source_target_pairs={{0,8},{1,9},{2,10},{3,11},{4,12},{5,13},{6,14},{7,15},{8,0},{9,1},... | collective-permute-start | bytes 589832 | tf_op jit(solution)/shard_map/ppermute | solution.py:349
  16.2 9.9 %collective-permute-start.6 = (bf16[256,128]{1,0:T(8,128)(2,1)S(1)}, bf16[256,128]{1,0:T(8,128)(2,1)S(1)}, u32[]{:S(2)}, u32[]{:S(2)}) collective-permute-start(bf16[256,128]{1,0:T(8,128)(2,1)S(1)} %collective-permute-done.4.refs_6_), channel_id=1, source_target_pairs={{0,8},{1,9},{2,10},{3,11},{4,12},{5,13},{6,14},{7,15},{8,0},{9,1},... | collective-permute-start | bytes 196616 | tf_op jit(solution)/shard_map/ppermute | solution.py:349
  21.1 6.5 %collective-permute-start.7 = (bf16[512,128]{1,0:T(8,128)(2,1)S(1)}, bf16[512,128]{1,0:T(8,128)(2,1)S(1)}, u32[]{:S(2)}, u32[]{:S(2)}) collective-permute-start(bf16[512,128]{1,0:T(8,128)(2,1)S(1)} %collective-permute-done.2.refs_4_), channel_id=1, source_target_pairs={{0,8},{1,9},{2,10},{3,11},{4,12},{5,13},{6,14},{7,15},{8,0},{9,1},... | collective-permute-start | bytes 393224 | tf_op jit(solution)/shard_map/ppermute | solution.py:349
  23.9 5.9 %collective-permute-start.8 = (bf16[512,128]{1,0:T(8,128)(2,1)S(1)}, bf16[512,128]{1,0:T(8,128)(2,1)S(1)}, u32[]{:S(2)}, u32[]{:S(2)}) collective-permute-start(bf16[512,128]{1,0:T(8,128)(2,1)S(1)} %collective-permute-done.3.refs_5_), channel_id=1, source_target_pairs={{0,8},{1,9},{2,10},{3,11},{4,12},{5,13},{6,14},{7,15},{8,0},{9,1},... | collective-permute-start | bytes 393224 | tf_op jit(solution)/shard_map/ppermute | solution.py:349
  27.7 2.1 %copy-start = (f32[384,128]{1,0:T(8,128)S(1)}, f32[384,128]{1,0:T(8,128)}, u32[]{:S(2)}) copy-start(f32[384,128]{1,0:T(8,128)} %refs_7_.1) | copy-start | bytes 589828
  31.7 3.9 %collective-permute-start.9 = (f32[520,128]{1,0:T(8,128)S(1)}, f32[520,128]{1,0:T(8,128)S(1)}, u32[]{:S(2)}, u32[]{:S(2)}) collective-permute-start(f32[520,128]{1,0:T(8,128)S(1)} %get-tuple-element.66.give_ref), channel_id=1, source_target_pairs={{0,16},{1,17},{2,18},{3,19},{4,20},{5,21},{6,22},{7,23},{8,24},{9,... | collective-permute-start | bytes 798728 | tf_op jit(solution)/shard_map/ppermute | solution.py:459
  71.3 5.7 %collective-permute-start.10 = (f32[512,128]{1,0:T(8,128)S(1)}, f32[512,128]{1,0:T(8,128)S(1)}, u32[]{:S(2)}, u32[]{:S(2)}) collective-permute-start(f32[512,128]{1,0:T(8,128)S(1)} %bitcast.10), channel_id=1, source_target_pairs={{0,16},{1,17},{2,18},{3,19},{4,20},{5,21},{6,22},{7,23},{8,24},{9,... | collective-permute-start | bytes 786440 | tf_op jit(solution)/shard_map/ppermute | solution.py:480

commit v9 on v7

--- a/solution.py
+++ b/solution.py
@@ -149,11 +149,10 @@
     out_ref[...] = in_ref[...]
 
 
-def pair_kernel(own_ref, a_ref, b_ref, ahead_ref, behind_ref):
+def pair_kernel(own_ref, other_ref, out_ref):
     rows = own_ref.shape[0]
-    for out_ref, other_ref in ((ahead_ref, a_ref), (behind_ref, b_ref)):
-        out_ref[0:rows, :] = own_ref[...]
-        out_ref[rows:, :] = other_ref[...]
+    out_ref[0:rows, :] = own_ref[...]
+    out_ref[rows:, :] = other_ref[...]
 
 
 def gradient_half(low, pooled_ref, gate_q_grad_ref, pool_ref, gate_k_grad_ref, out_ref):
@@ -358,8 +357,9 @@
         cost=pl.CostEstimate(flops=10**9, bytes_accessed=10**6, transcendentals=10**6),
     )(own_keys)
     two_parts = jax.ShapeDtypeStruct((2 * tok_rows, width), keys.dtype)
-    ahead, behind = call(pair_kernel, (two_parts, two_parts), [VMEM] * 3, "pair")(own_copy, step[1], step[-1])
+    (ahead,) = call(pair_kernel, (two_parts,), [VMEM] * 2, "ahead")(own_copy, step[1])
     ahead = get(ahead, 2)
+    (behind,) = call(pair_kernel, (two_parts,), [VMEM] * 2, "behind")(own_copy, step[-1])
     behind = get(behind, near - 2)
     mid = jnp.concatenate([own_copy, step[1], step[-1]], axis=0)
     mid_far = across(mid)

time: 79.5 us -> 78.2 us (0.984)
  starting transfers between devices: 27.5 us -> 24.6 us
  waiting for transfers between devices: 3.69 us -> 5.73 us
    ppermute x1, starting transfers between devices: 5.19 us -> 2.77 us  [on_device(): got = lax.ppermute(give, every, cores)]
    ppermute x5, waiting for transfers between devices: 1.72 us -> 3.3 us  [get(): lax.ppermute(x, 'ctx', [(j, j // near * near + (j - offset) % near) for j...]
    ppermute x5, starting transfers between devices: 11.7 us -> 10.5 us  [get(): lax.ppermute(x, 'ctx', [(j, j // near * near + (j - offset) % near) for j...]
    all_to_all x1, blocking collectives: 12.4 us -> 11.5 us  [on_device(): lax.all_to_all(spread, 'ctx', 0, 0, axis_index_groups=[list(range(near)),...]
  transfers between devices with their start and end apart: 11 -> 11, of which waited for: 6 -> 5; matrix products, arithmetic and copies ran while one was open for 0% -> 0% of each run, Pallas kernels for 9% -> 10%
where the time goes in v9:
time: 78.2 us; the launch traced here: 77.9 us
  blocking collectives  35.5 us (45%)
  starting transfers between devices  24.6 us (31%)
  Pallas kernels  10.2 us (13%)
  waiting for transfers between devices  5.73 us (7%)
  between operations  0.95 us (1%)
  local copies, waits for them, and re-layouts  0.9 us (1%)
    all_to_all x1, blocking collectives, on_device(): lax.all_to_all(parts, every, 0, 0, axis_index_groups=planes, tiled=True)  13.7 us
    all_to_all x1, blocking collectives, on_device(): lax.all_to_all(spread, 'ctx', 0, 0, axis_index_groups=[list(range(near)),...  11.5 us
    ppermute x5, starting transfers between devices, get(): lax.ppermute(x, 'ctx', [(j, j // near * near + (j - offset) % near) for j...  10.5 us
    all_to_all x1, blocking collectives, on_device(): lax.all_to_all(spread, every, 0, 0, axis_index_groups=planes, tiled=True)  10.3 us
    ppermute x4, starting transfers between devices, across(): lax.ppermute(x, 'ctx', [(j, (j + near) % ctx_count) for j in range(ctx_co...  6.71 us
    pallas_call x4, Pallas kernels, attend_to(): call(functools.partial(attend_kernel, layout), state + (f32(count * block...  5.64 us
    ppermute x1, starting transfers between devices, on_device(): other = lax.ppermute(mine, every, cores)  4.56 us
    ppermute x5, waiting for transfers between devices, get(): lax.ppermute(x, 'ctx', [(j, j // near * near + (j - offset) % near) for j...  3.3 us
  transfers between devices with their start and end apart: 11, of which 5 were waited for; matrix products, arithmetic and copies ran while one was open for 0% of the time, Pallas kernels for 10%

profile of v9, /device:TPU:1, one launch (start us, length us, event | category | flops | bytes accessed | tf_op | source)
XLA Modules:
  0.0 77.9 jit_solution(11358817776067824848)
XLA Ops:
  0.6 6.5 %collective-permute-start = (bf16[256,128]{1,0:T(8,128)(2,1)}, bf16[256,128]{1,0:T(8,128)(2,1)S(1)}, u32[]{:S(2)}, u32[]{:S(2)}) collective-permute-start(bf16[256,128]{1,0:T(8,128)(2,1)} %bitcast.14), channel_id=1, source_target_pairs={{0,7},{1,0},{2,1},{3,2},{4,3},{5,4},{6,5},{7,6},{8,15},{9,8},{10,9... | collective-permute-start | bytes 196616 | tf_op jit(solution)/shard_map/ppermute | solution.py:345
  7.1 0.0 collective-permute-start.1
  7.1 2.8 %collective-permute-start.4 = (bf16[256,128]{1,0:T(8,128)(2,1)}, bf16[256,128]{1,0:T(8,128)(2,1)S(1)}, u32[]{:S(2)}, u32[]{:S(2)}) collective-permute-start(bf16[256,128]{1,0:T(8,128)(2,1)} %bitcast.16), channel_id=1, source_target_pairs={{0,4},{1,5},{2,6},{3,7},{4,0},{5,1},{6,2},{7,3},{8,12},{9,13},{10,... | collective-permute-start | bytes 196616 | tf_op jit(solution)/shard_map/ppermute | solution.py:345
  9.9 0.0 copy-start.3
  9.9 0.9 %copy-done.3 = bf16[1,256,128]{2,1,0:T(8,128)(2,1)S(1)} copy-done((bf16[1,256,128]{2,1,0:T(8,128)(2,1)S(1)}, bf16[1,256,128]{2,1,0:T(8,128)(2,1)}, u32[]{:S(2)}) %copy-start.3) | copy-done | bytes 65560
  10.8 0.0 collective-permute-done.refs_0_.other_ref
  10.8 0.0 copy-start.1
  10.8 0.0 copy-start.2
  10.8 0.2 collective-permute-start.2
  11.0 1.3 %collective-permute-done.1.refs_1_.other_ref = bf16[256,128]{1,0:T(8,128)(2,1)S(1)} collective-permute-done((bf16[256,128]{1,0:T(8,128)(2,1)}, bf16[256,128]{1,0:T(8,128)(2,1)S(1)}, u32[]{:S(2)}, u32[]{:S(2)}) %collective-permute-start.1) | collective-permute-done | bytes 65568 | tf_op jit(solution)/shard_map/ppermute | solution.py:345
  12.3 1.1 %collective-permute-start.3 = (bf16[512,128]{1,0:T(8,128)(2,1)S(1)}, bf16[512,128]{1,0:T(8,128)(2,1)S(1)}, u32[]{:S(2)}, u32[]{:S(2)}) collective-permute-start(bf16[512,128]{1,0:T(8,128)(2,1)S(1)} %behind.1), channel_id=1, source_target_pairs={{0,2},{1,3},{2,4},{3,5},{4,6},{5,7},{6,0},{7,1},{8,10},{9,11},{10,... | collective-permute-start | bytes 393224 | tf_op jit(solution)/shard_map/ppermute | solution.py:345
  13.4 0.0 copy-start.4
  13.4 2.8 %collective-permute-start.5 = (bf16[768,128]{1,0:T(8,128)(2,1)S(1)}, bf16[768,128]{1,0:T(8,128)(2,1)S(1)}, u32[]{:S(2)}, u32[]{:S(2)}) collective-permute-start(bf16[768,128]{1,0:T(8,128)(2,1)S(1)} %pad_maximum_fusion.refs_4_), channel_id=1, source_target_pairs={{0,8},{1,9},{2,10},{3,11},{4,12},{5,13},{6,14},{7,15},{8,0},{9,1},... | collective-permute-start | bytes 589832 | tf_op jit(solution)/shard_map/ppermute | solution.py:348
  16.2 0.0 collective-permute-done.4.refs_6_
  16.2 0.9 %collective-permute-start.6 = (bf16[256,128]{1,0:T(8,128)(2,1)S(1)}, bf16[256,128]{1,0:T(8,128)(2,1)S(1)}, u32[]{:S(2)}, u32[]{:S(2)}) collective-permute-start(bf16[256,128]{1,0:T(8,128)(2,1)S(1)} %collective-permute-done.4.refs_6_), channel_id=1, source_target_pairs={{0,8},{1,9},{2,10},{3,11},{4,12},{5,13},{6,14},{7,15},{8,0},{9,1},... | collective-permute-start | bytes 196616 | tf_op jit(solution)/shard_map/ppermute | solution.py:348
  17.2 0.0 copy-done.1
  17.2 0.0 copy-done.2
  17.2 0.0 copy-done.4
  17.2 0.7 local.1
  17.9 1.3 %attend.4 = (f32[1,1280]{1,0:T(1,128)S(1)}, f32[8,1280]{1,0:T(8,128)S(1)}, f32[12,1280]{1,0:T(8,128)S(1)}, f32[12,384]{1,0:T(8,128)S(1)}) custom-call(bf16[5,256,256]{2,1,0:T(8,128)(2,1)S(1)} %get-tuple-element.42.refs_0_, f32[64,256]{1,0:T(8,128)S(1)} %get-tuple-element.43.refs_1_, f32[1,1280]{1,0:T(1,128)S(1)} %get-tuple-element.44.refs_2_, ...), custom_call_target="tpu_custom_call" | custom-call | flops 1200000000 | bytes 1000000 | tf_op jit(solution)/shard_map/attend/pallas_call | solution.py:391
  19.1 2.0 %collective-permute-done.2.refs_4_ = bf16[512,128]{1,0:T(8,128)(2,1)S(1)} collective-permute-done((bf16[512,128]{1,0:T(8,128)(2,1)S(1)}, bf16[512,128]{1,0:T(8,128)(2,1)S(1)}, u32[]{:S(2)}, u32[]{:S(2)}) %collective-permute-start.2) | collective-permute-done | bytes 131104 | tf_op jit(solution)/shard_map/ppermute | solution.py:345
  21.1 2.7 %collective-permute-start.7 = (bf16[512,128]{1,0:T(8,128)(2,1)S(1)}, bf16[512,128]{1,0:T(8,128)(2,1)S(1)}, u32[]{:S(2)}, u32[]{:S(2)}) collective-permute-start(bf16[512,128]{1,0:T(8,128)(2,1)S(1)} %collective-permute-done.2.refs_4_), channel_id=1, source_target_pairs={{0,8},{1,9},{2,10},{3,11},{4,12},{5,13},{6,14},{7,15},{8,0},{9,1},... | collective-permute-start | bytes 393224 | tf_op jit(solution)/shard_map/ppermute | solution.py:348
  23.9 0.0 collective-permute-done.3.refs_5_
  23.9 0.2 collective-permute-start.8
  24.1 2.0 %attend.5 = (f32[1,1280]{1,0:T(1,128)S(1)}, f32[8,1280]{1,0:T(8,128)S(1)}, f32[20,1280]{1,0:T(8,128)S(1)}, f32[20,384]{1,0:T(8,128)S(1)}) custom-call(bf16[5,256,256]{2,1,0:T(8,128)(2,1)S(1)} %get-tuple-element.42.refs_0_, f32[64,256]{1,0:T(8,128)S(1)} %get-tuple-element.43.refs_1_, f32[1,1280]{1,0:T(1,128)S(1)} %get-tuple-element.46.refs_2_, ...), custom_call_target="tpu_custom_call" | custom-call | flops 1200000000 | bytes 1000000 | tf_op jit(solution)/shard_map/attend/pallas_call | solution.py:391
  26.1 0.0 collective-permute-done.6.refs_5_
  26.1 0.0 collective-permute-done.5.refs_4_
  26.1 1.6 %attend.6 = (f32[1,1280]{1,0:T(1,128)S(1)}, f32[8,1280]{1,0:T(8,128)S(1)}, f32[16,1280]{1,0:T(8,128)S(1)}, f32[16,384]{1,0:T(8,128)S(1)}) custom-call(bf16[5,256,256]{2,1,0:T(8,128)(2,1)S(1)} %get-tuple-element.42.refs_0_, f32[64,256]{1,0:T(8,128)S(1)} %get-tuple-element.43.refs_1_, f32[1,1280]{1,0:T(1,128)S(1)} %get-tuple-element.48.refs_2_, ...), custom_call_target="tpu_custom_call" | custom-call | flops 1200000000 | bytes 1000000 | tf_op jit(solution)/shard_map/attend/pallas_call | solution.py:391
  27.7 0.0 collective-permute-done.7.refs_4_
  27.7 0.0 copy-start
  27.7 0.8 %attend.7 = (f32[1,1280]{1,0:T(1,128)S(1)}, f32[8,1280]{1,0:T(8,128)S(1)}, f32[8,1280]{1,0:T(8,128)S(1)}, f32[8,384]{1,0:T(8,128)S(1)}) custom-call(bf16[5,256,256]{2,1,0:T(8,128)(2,1)S(1)} %get-tuple-element.42.refs_0_, f32[64,256]{1,0:T(8,128)S(1)} %get-tuple-element.43.refs_1_, f32[1,1280]{1,0:T(1,128)S(1)} %get-tuple-element.50.refs_2_, ...), custom_call_target="tpu_custom_call" | custom-call | flops 1200000000 | bytes 1000000 | tf_op jit(solution)/shard_map/attend/pallas_call | solution.py:391
  28.6 1.2 %collective-permute-done.8.refs_9_ = bf16[512,128]{1,0:T(8,128)(2,1)S(1)} collective-permute-done((bf16[512,128]{1,0:T(8,128)(2,1)S(1)}, bf16[512,128]{1,0:T(8,128)(2,1)S(1)}, u32[]{:S(2)}, u32[]{:S(2)}) %collective-permute-start.8) | collective-permute-done | bytes 131104 | tf_op jit(solution)/shard_map/ppermute | solution.py:348
  29.8 0.0 copy-done
  29.8 1.9 %finish.1 = (f32[5,4,64]{2,1,0:T(4,128)S(1)}, f32[520,128]{1,0:T(8,128)S(1)}, f32[40,128]{1,0:T(8,128)S(1)}, f32[64,128]{1,0:T(8,128)S(1)}, f32[64,384]{1,0:T(8,128)S(1)}) custom-call(bf16[5,256,256]{2,1,0:T(8,128)(2,1)S(1)} %get-tuple-element.42.refs_0_, f32[64,256]{1,0:T(8,128)S(1)} %get-tuple-element.43.refs_1_, f32[1,1280]{1,0:T(1,128)S(1)} %get-tuple-element.52.refs_2_, ...), custom_call_target="tpu_custom_call" | custom-call | tf_op jit(solution)/shard_map/finish/pallas_call | solution.py:419
  31.7 2.8 %collective-permute-start.9 = (f32[520,128]{1,0:T(8,128)S(1)}, f32[520,128]{1,0:T(8,128)S(1)}, u32[]{:S(2)}, u32[]{:S(2)}) collective-permute-start(f32[520,128]{1,0:T(8,128)S(1)} %get-tuple-element.68.give_ref), channel_id=1, source_target_pairs={{0,16},{1,17},{2,18},{3,19},{4,20},{5,21},{6,22},{7,23},{8,24},{9,... | collective-permute-start | bytes 798728 | tf_op jit(solution)/shard_map/ppermute | solution.py:458
  34.5 0.3 keep.1.keep_ref
  34.8 0.9 %collective-permute-done.9.got_ref = f32[520,128]{1,0:T(8,128)S(1)} collective-permute-done((f32[520,128]{1,0:T(8,128)S(1)}, f32[520,128]{1,0:T(8,128)S(1)}, u32[]{:S(2)}, u32[]{:S(2)}) %collective-permute-start.9) | collective-permute-done | bytes 266272 | tf_op jit(solution)/shard_map/ppermute | solution.py:458
  35.7 13.7 %all_to_all.15.parts_ref = f32[16,40,128]{2,1,0:T(8,128)S(1)} all-to-all(f32[16,40,128]{2,1,0:T(8,128)S(1)} %fold.1), channel_id=1, replica_groups={{0,32,64,96,8,40,72,104,128,160,192,224,136,168,200,232},{1,33,65,97,9,..., dimensions={0} | all-to-all | bytes 655360 | tf_op jit(solution)/shard_map/all_to_all | solution.py:465
  49.5 11.5 %all_to_all.16.parts_ref = f32[8,40,128]{2,1,0:T(8,128)S(1)} all-to-all(f32[8,40,128]{2,1,0:T(8,128)S(1)} %sum.1), channel_id=1, replica_groups={{0,1,2,3,4,5,6,7},{8,9,10,11,12,13,14,15},{16,17,18,19,20,21,22,23},{24..., dimensions={0} | all-to-all | bytes 327680 | tf_op jit(solution)/shard_map/all_to_all | solution.py:467
  61.0 10.3 %all_to_all.17 = f32[16,32,128]{2,1,0:T(8,128)S(1)} all-to-all(f32[16,32,128]{2,1,0:T(8,128)S(1)} %get-tuple-element.69), channel_id=1, replica_groups={{0,32,64,96,8,40,72,104,128,160,192,224,136,168,200,232},{1,33,65,97,9,..., dimensions={0} | all-to-all | bytes 524288 | tf_op jit(solution)/shard_map/all_to_all | solution.py:478
  71.3 4.6 %collective-permute-start.10 = (f32[512,128]{1,0:T(8,128)S(1)}, f32[512,128]{1,0:T(8,128)S(1)}, u32[]{:S(2)}, u32[]{:S(2)}) collective-permute-start(f32[512,128]{1,0:T(8,128)S(1)} %bitcast.10), channel_id=1, source_target_pairs={{0,16},{1,17},{2,18},{3,19},{4,20},{5,21},{6,22},{7,23},{8,24},{9,... | collective-permute-start | bytes 786440 | tf_op jit(solution)/shard_map/ppermute | solution.py:479
  75.9 0.8 %mine.1 = (f32[5,128,128]{2,1,0:T(8,128)}, f32[3,128,128]{2,1,0:T(8,128)}, f32[1,1]{1,0:T(1,128)}, f32[5,4,64]{2,1,0:T(4,128)}) custom-call(f32[4,128,128]{2,1,0:T(8,128)S(1)} %bitcast.11, f32[8,128]{1,0:T(8,128)S(1)} %get-tuple-element.70.losses_ref, f32[5,4,64]{2,1,0:T(4,128)S(1)} %get-tuple-element.71.target_in), custom_call_target="tpu_custom_call" | custom-call | tf_op jit(solution)/shard_map/mine/pallas_call | solution.py:482
  76.7 0.3 collective-permute-done.10
  77.0 0.7 other.1
  (7 shorter events, 0.1 us)
Async XLA Ops:
  0.6 10.2 %collective-permute-start = (bf16[256,128]{1,0:T(8,128)(2,1)}, bf16[256,128]{1,0:T(8,128)(2,1)S(1)}, u32[]{:S(2)}, u32[]{:S(2)}) collective-permute-start(bf16[256,128]{1,0:T(8,128)(2,1)} %bitcast.14), channel_id=1, source_target_pairs={{0,7},{1,0},{2,1},{3,2},{4,3},{5,4},{6,5},{7,6},{8,15},{9,8},{10,9... | collective-permute-start | bytes 196616 | tf_op jit(solution)/shard_map/ppermute | solution.py:345
  7.1 5.2 %collective-permute-start.1 = (bf16[256,128]{1,0:T(8,128)(2,1)}, bf16[256,128]{1,0:T(8,128)(2,1)S(1)}, u32[]{:S(2)}, u32[]{:S(2)}) collective-permute-start(bf16[256,128]{1,0:T(8,128)(2,1)} %bitcast.15), channel_id=1, source_target_pairs={{0,1},{1,2},{2,3},{3,4},{4,5},{5,6},{6,7},{7,0},{8,9},{9,10},{10,1... | collective-permute-start | bytes 196616 | tf_op jit(solution)/shard_map/ppermute | solution.py:345
  7.1 9.1 %collective-permute-start.4 = (bf16[256,128]{1,0:T(8,128)(2,1)}, bf16[256,128]{1,0:T(8,128)(2,1)S(1)}, u32[]{:S(2)}, u32[]{:S(2)}) collective-permute-start(bf16[256,128]{1,0:T(8,128)(2,1)} %bitcast.16), channel_id=1, source_target_pairs={{0,4},{1,5},{2,6},{3,7},{4,0},{5,1},{6,2},{7,3},{8,12},{9,13},{10,... | collective-permute-start | bytes 196616 | tf_op jit(solution)/shard_map/ppermute | solution.py:345
  9.9 0.9 %copy-start.3 = (bf16[1,256,128]{2,1,0:T(8,128)(2,1)S(1)}, bf16[1,256,128]{2,1,0:T(8,128)(2,1)}, u32[]{:S(2)}) copy-start(bf16[1,256,128]{2,1,0:T(8,128)(2,1)} %param.7) | copy-start | bytes 196612
  10.8 6.3 %copy-start.1 = (bf16[1,256,5,128]{3,1,2,0:T(8,128)(2,1)S(1)}, bf16[1,256,5,128]{3,1,2,0:T(8,128)(2,1)}, u32[]{:S(2)}) copy-start(bf16[1,256,5,128]{3,1,2,0:T(8,128)(2,1)} %param.6) | copy-start | bytes 983044
  10.8 6.3 %copy-start.2 = (f32[5,128,128]{2,1,0:T(8,128)S(1)}, f32[5,128,128]{2,1,0:T(8,128)}, u32[]{:S(2)}) copy-start(f32[5,128,128]{2,1,0:T(8,128)} %wq_ref.1) | copy-start | bytes 983044
  10.8 10.3 %collective-permute-start.2 = (bf16[512,128]{1,0:T(8,128)(2,1)S(1)}, bf16[512,128]{1,0:T(8,128)(2,1)S(1)}, u32[]{:S(2)}, u32[]{:S(2)}) collective-permute-start(bf16[512,128]{1,0:T(8,128)(2,1)S(1)} %ahead.1), channel_id=1, source_target_pairs={{0,6},{1,7},{2,0},{3,1},{4,2},{5,3},{6,4},{7,5},{8,14},{9,15},{10,... | collective-permute-start | bytes 393224 | tf_op jit(solution)/shard_map/ppermute | solution.py:345
  12.3 11.6 %collective-permute-start.3 = (bf16[512,128]{1,0:T(8,128)(2,1)S(1)}, bf16[512,128]{1,0:T(8,128)(2,1)S(1)}, u32[]{:S(2)}, u32[]{:S(2)}) collective-permute-start(bf16[512,128]{1,0:T(8,128)(2,1)S(1)} %behind.1), channel_id=1, source_target_pairs={{0,2},{1,3},{2,4},{3,5},{4,6},{5,7},{6,0},{7,1},{8,10},{9,11},{10,... | collective-permute-start | bytes 393224 | tf_op jit(solution)/shard_map/ppermute | solution.py:345
  13.4 3.8 %copy-start.4 = (s32[1,32]{1,0:T(1,128)S(1)}, s32[1,32]{1,0:T(1,128)}, u32[]{:S(2)}) copy-start(s32[1,32]{1,0:T(1,128)} %order_ref.1) | copy-start | bytes 388
  13.4 12.7 %collective-permute-start.5 = (bf16[768,128]{1,0:T(8,128)(2,1)S(1)}, bf16[768,128]{1,0:T(8,128)(2,1)S(1)}, u32[]{:S(2)}, u32[]{:S(2)}) collective-permute-start(bf16[768,128]{1,0:T(8,128)(2,1)S(1)} %pad_maximum_fusion.refs_4_), channel_id=1, source_target_pairs={{0,8},{1,9},{2,10},{3,11},{4,12},{5,13},{6,14},{7,15},{8,0},{9,1},... | collective-permute-start | bytes 589832 | tf_op jit(solution)/shard_map/ppermute | solution.py:348
  16.2 9.9 %collective-permute-start.6 = (bf16[256,128]{1,0:T(8,128)(2,1)S(1)}, bf16[256,128]{1,0:T(8,128)(2,1)S(1)}, u32[]{:S(2)}, u32[]{:S(2)}) collective-permute-start(bf16[256,128]{1,0:T(8,128)(2,1)S(1)} %collective-permute-done.4.refs_6_), channel_id=1, source_target_pairs={{0,8},{1,9},{2,10},{3,11},{4,12},{5,13},{6,14},{7,15},{8,0},{9,1},... | collective-permute-start | bytes 196616 | tf_op jit(solution)/shard_map/ppermute | solution.py:348
  21.1 6.5 %collective-permute-start.7 = (bf16[512,128]{1,0:T(8,128)(2,1)S(1)}, bf16[512,128]{1,0:T(8,128)(2,1)S(1)}, u32[]{:S(2)}, u32[]{:S(2)}) collective-permute-start(bf16[512,128]{1,0:T(8,128)(2,1)S(1)} %collective-permute-done.2.refs_4_), channel_id=1, source_target_pairs={{0,8},{1,9},{2,10},{3,11},{4,12},{5,13},{6,14},{7,15},{8,0},{9,1},... | collective-permute-start | bytes 393224 | tf_op jit(solution)/shard_map/ppermute | solution.py:348
  23.9 5.9 %collective-permute-start.8 = (bf16[512,128]{1,0:T(8,128)(2,1)S(1)}, bf16[512,128]{1,0:T(8,128)(2,1)S(1)}, u32[]{:S(2)}, u32[]{:S(2)}) collective-permute-start(bf16[512,128]{1,0:T(8,128)(2,1)S(1)} %collective-permute-done.3.refs_5_), channel_id=1, source_target_pairs={{0,8},{1,9},{2,10},{3,11},{4,12},{5,13},{6,14},{7,15},{8,0},{9,1},... | collective-permute-start | bytes 393224 | tf_op jit(solution)/shard_map/ppermute | solution.py:348
  27.7 2.1 %copy-start = (f32[384,128]{1,0:T(8,128)S(1)}, f32[384,128]{1,0:T(8,128)}, u32[]{:S(2)}) copy-start(f32[384,128]{1,0:T(8,128)} %refs_7_.1) | copy-start | bytes 589828
  31.7 3.9 %collective-permute-start.9 = (f32[520,128]{1,0:T(8,128)S(1)}, f32[520,128]{1,0:T(8,128)S(1)}, u32[]{:S(2)}, u32[]{:S(2)}) collective-permute-start(f32[520,128]{1,0:T(8,128)S(1)} %get-tuple-element.68.give_ref), channel_id=1, source_target_pairs={{0,16},{1,17},{2,18},{3,19},{4,20},{5,21},{6,22},{7,23},{8,24},{9,... | collective-permute-start | bytes 798728 | tf_op jit(solution)/shard_map/ppermute | solution.py:458
  71.3 5.7 %collective-permute-start.10 = (f32[512,128]{1,0:T(8,128)S(1)}, f32[512,128]{1,0:T(8,128)S(1)}, u32[]{:S(2)}, u32[]{:S(2)}) collective-permute-start(f32[512,128]{1,0:T(8,128)S(1)} %bitcast.10), channel_id=1, source_target_pairs={{0,16},{1,17},{2,18},{3,19},{4,20},{5,21},{6,22},{7,23},{8,24},{9,... | collective-permute-start | bytes 786440 | tf_op jit(solution)/shard_map/ppermute | solution.py:479
